TPU v7x, 512 devices: a whole 4x8x8 slice. The times are simulated.
512 devices in a mesh: pipe: 32 (over y, x), expert: 16 (over z, core).
Axes of the slice: x: 4, y: 8, z: 8, core: 2. Of those that a mesh axis runs over, the one named last changes fastest.
Arguments:
- acts: bfloat16 [2048, 3072], P('expert'), may hold values from -6 to 6
- cotangent: bfloat16 [2048, 3072], P('expert'), may hold values from -6 to 6
- norm_gain: float32 [3072], replicated, may hold values from 0.5 to 1.5
- router: bfloat16 [3072, 16], replicated, may hold values from -0.109375 to 0.109375
- expert_ids: int32 [2048, 4], P('expert'), may hold values from 0 to 15, all different within a row; in each aligned block of 128 rows (0 to 127, 128 to 255, ...) at most 34 rows name the same one
- w_gate: bfloat16 [16, 3072, 5376], P('expert', None, 'pipe'), may hold values from -0.109375 to 0.109375
- w_up: bfloat16 [16, 3072, 5376], P('expert', None, 'pipe'), may hold values from -0.109375 to 0.109375
- w_down: bfloat16 [16, 5376, 3072], P('expert', 'pipe'), may hold values from -0.078125 to 0.078125
Outputs:
- grad_in: float32 [32, 64, 3072], P('pipe', 'expert')
Inputs may be any that keep to these rules, and one draw needn't show every extreme that they name: `expert_ids`: each row names 4 different experts. In each aligned block of 128 rows (the tokens of one index of the expert axis) no expert is named by more than 34 rows, a bound that some block reaches.
All inputs are finite; a program needn't handle non-finite values.
Results may differ from a plain program's by a relative error of at most 0.007.
Values may be sent and summed in bfloat16 or wider, within the bound.
No kernel may reach another device: no remote copies, remote signals or barrier semaphores. Data moves between devices by JAX's collectives and lax.ppermute only.
A program may use at most 128 MiB of HBM per device.

v0:
```python
import jax
import jax.numpy as jnp
from jax import lax
from jax.sharding import PartitionSpec as P

eps = 1e-05


def normed(rows, gain):
    wide = rows.astype(jnp.float32)
    return wide * lax.rsqrt(jnp.mean(wide * wide, axis=-1, keepdims=True) + eps) * gain


def slot_table(ids, cap, experts):
    flat = ids.reshape(-1)
    pairs = flat.shape[0]
    onehot = (flat[:, None] == jnp.arange(experts, dtype=jnp.int32)[None, :]).astype(jnp.int32)
    before = jnp.cumsum(onehot, axis=0) - onehot
    place = jnp.sum(onehot * before, axis=1)
    slot = flat * cap + place
    table = (
        jnp.full((experts * cap,), pairs, jnp.int32)
        .at[slot]
        .set(jnp.arange(pairs, dtype=jnp.int32))
    )
    return (slot, table)


def token_front(x, gain, router_w, ids, cap):
    tokens, top = ids.shape
    experts = router_w.shape[1]
    h = normed(x, gain).astype(jnp.bfloat16)
    logits = jnp.dot(h, router_w, preferred_element_type=jnp.float32)
    select = (ids[:, :, None] == jnp.arange(experts, dtype=jnp.int32)[None, None, :]).astype(
        jnp.float32
    )
    picked = jnp.einsum("tke,te->tk", select, logits)
    sig = jax.nn.sigmoid(picked)
    total = jnp.sum(sig, axis=1, keepdims=True)
    weight = sig / total
    slot, table = slot_table(ids, cap, experts)
    pairs = tokens * top
    valid = table < pairs
    source = jnp.minimum(table, pairs - 1)
    owner = source // top
    return (h, sig, total, weight, select, slot, valid, owner, source)


def pack_rows(rows, valid, owner, experts, cap):
    width = rows.shape[1]
    return jnp.where(valid[:, None], rows[owner], jnp.zeros((), rows.dtype)).reshape(
        experts, cap, width
    )


def weighted_rows(weight, grads, valid, owner, source, experts, cap):
    gate_rows = weight.reshape(-1)[source].astype(jnp.bfloat16).astype(jnp.float32)
    scaled = (gate_rows[:, None] * grads[owner].astype(jnp.float32)).astype(jnp.bfloat16)
    return jnp.where(valid[:, None], scaled, jnp.zeros((), jnp.bfloat16)).reshape(
        experts, cap, grads.shape[1]
    )


def expert_rows(rows, dy_rows, w_both, wd):
    contract = (((1,), (1,)), ((), ()))
    hidden = wd.shape[0]
    both = jnp.dot(rows, w_both, preferred_element_type=jnp.float32)
    a_part = both[:, :hidden]
    b_part = both[:, hidden:]
    sg = jax.nn.sigmoid(a_part)
    sa = a_part * sg
    act = (sa * b_part).astype(jnp.bfloat16)
    y_rows = jnp.dot(act, wd, preferred_element_type=jnp.float32)
    dact = lax.dot_general(dy_rows, wd, contract, preferred_element_type=jnp.float32)
    da_rows = (dact * b_part * sg * (1.0 + a_part * (1.0 - sg))).astype(jnp.bfloat16)
    db_rows = (dact * sa).astype(jnp.bfloat16)
    dboth = jnp.concatenate([da_rows, db_rows], axis=1)
    dh_rows = lax.dot_general(dboth, w_both, contract, preferred_element_type=jnp.float32)
    return (dh_rows, y_rows)


def sum_pairs(back_dh, slot, tokens, top):
    width = back_dh.shape[-1]
    return jnp.sum(back_dh.reshape(-1, width)[slot].reshape(tokens, top, width), axis=1)


def token_back(x, g, gain, router_w, dh_tok, dscore, sig, total, weight, select):
    dsig = (dscore - jnp.sum(weight * dscore, axis=1, keepdims=True)) / total
    dpick = dsig * sig * (1.0 - sig)
    dlogits = jnp.einsum("tk,tke->te", dpick, select)
    dh_total = dh_tok + lax.dot_general(
        dlogits, router_w.astype(jnp.float32), (((1,), (1,)), ((), ()))
    )
    wide = x.astype(jnp.float32)
    recip = lax.rsqrt(jnp.mean(wide * wide, axis=-1, keepdims=True) + eps)
    scaled = dh_total * gain
    pulled = recip * scaled - wide * (recip * recip * recip) * jnp.mean(
        wide * scaled, axis=-1, keepdims=True
    )
    return g.astype(jnp.float32) + pulled


def shards(acts, cotangent, norm_gain, router, expert_ids, w_gate, w_up, w_down):
    experts = lax.axis_size("expert")
    sections = lax.axis_size("pipe")
    tok_rows, width = acts.shape
    chosen = expert_ids.shape[1]
    cap = min(tok_rows, (17 * tok_rows * chosen + 16 * experts - 1) // (16 * experts))
    share = tok_rows // sections
    w_both = jnp.concatenate([w_gate[0], w_up[0]], axis=1)
    wd = w_down[0]
    h, sig, total, weight, select, slot, valid, owner, source = token_front(
        acts, norm_gain, router, expert_ids, cap
    )
    send_h = pack_rows(h, valid, owner, experts, cap)
    start = lax.axis_index("pipe") * share
    g_share = lax.dynamic_slice_in_dim(cotangent, start, share, 0)
    send_dy = weighted_rows(weight, cotangent, valid, owner, source, experts, cap)
    recv_h = lax.all_to_all(send_h, "expert", split_axis=0, concat_axis=0, tiled=True)
    recv_dy = lax.all_to_all(send_dy, "expert", split_axis=0, concat_axis=0, tiled=True)
    count = recv_h.shape[1]
    dh_rows, y_rows = expert_rows(recv_h.reshape(-1, width), recv_dy.reshape(-1, width), w_both, wd)
    back_dh = lax.all_to_all(
        dh_rows.reshape(experts, count, width), "expert", split_axis=0, concat_axis=0, tiled=True
    )
    back_y = lax.all_to_all(
        y_rows.reshape(experts, count, width), "expert", split_axis=0, concat_axis=0, tiled=True
    )
    dh_tok = sum_pairs(back_dh, slot, tok_rows, chosen)
    y_pairs = back_y.reshape(-1, width)[slot].reshape(tok_rows, chosen, width)
    dh_share, y_share = (
        lax.psum_scatter(dh_tok, "pipe", scatter_dimension=0, tiled=True),
        lax.psum_scatter(y_pairs, "pipe", scatter_dimension=0, tiled=True),
    )
    dscore = jnp.sum(y_share * g_share.astype(jnp.float32)[:, None, :], axis=-1)
    x_share = lax.dynamic_slice_in_dim(acts, start, share, 0)
    sig_share = lax.dynamic_slice_in_dim(sig, start, share, 0)
    total_share = lax.dynamic_slice_in_dim(total, start, share, 0)
    weight_share = lax.dynamic_slice_in_dim(weight, start, share, 0)
    select_share = lax.dynamic_slice_in_dim(select, start, share, 0)
    result = token_back(
        x_share,
        g_share,
        norm_gain,
        router,
        dh_share,
        dscore,
        sig_share,
        total_share,
        weight_share,
        select_share,
    )
    return result[None]


def solution(mesh):
    in_specs = (
        P("expert", None),
        P("expert", None),
        P(),
        P(),
        P("expert", None),
        P("expert", None, "pipe"),
        P("expert", None, "pipe"),
        P("expert", "pipe", None),
    )
    out_specs = P("pipe", "expert", None)
    return jax.shard_map(shards, mesh=mesh, in_specs=in_specs, out_specs=out_specs, check_vma=False)
```

profile of v0, /device:TPU:1, one launch (start us, length us, event | category | flops | bytes accessed | tf_op | source)
XLA Modules:
  0.0 875.1 jit_solution(15194530749361862013)
XLA Ops:
  26.0 4.9 gather.20
  30.9 4.6 gather_fusion.1
  35.5 5.7 reshape.144
  41.3 6.8 fusion
  48.1 102.1 %all_to_all.20 = bf16[16,34,3072]{2,1,0:T(8,128)(2,1)} all-to-all(bf16[16,34,3072]{2,1,0:T(8,128)(2,1)S(1)} %get-tuple-element.17), channel_id=1, replica_groups=mesh['pipe'=32,'expert'=16] {'expert'}, dimensions={0} | all-to-all | bytes 6684672 | tf_op jit(solution)/shard_map/all_to_all | solution.py:119
  150.1 4.6 all-to-all-start
  154.8 4.9 reshape.137
  159.6 5.0 fusion.6
  164.6 77.4 %all-to-all-done = bf16[16,34,3072]{2,1,0:T(8,128)(2,1)} async-done(((bf16[16,34,3072]{2,1,0:T(8,128)(2,1)}), bf16[16,34,3072]{2,1,0:T(8,128)(2,1)}, u32[]{:S(2)}, u32[]{:S(2)}) %all-to-all-start) | async-done | bytes 3342368 | tf_op jit(solution)/shard_map/all_to_all | solution.py:120
  242.0 4.8 reshape.136
  250.5 4.8 fusion.5
  255.2 6.5 reshape.138
  261.7 5.4 all-to-all-start.2
  271.7 167.7 %all-to-all-done.2 = f32[16,34,3072]{2,1,0:T(8,128)} async-done(((f32[16,34,3072]{2,1,0:T(8,128)}), f32[16,34,3072]{2,1,0:T(8,128)}, u32[]{:S(2)}, u32[]{:S(2)}) %all-to-all-start.2) | async-done | bytes 6684704 | tf_op jit(solution)/shard_map/all_to_all | solution.py:123
  439.4 5.5 all-to-all-start.3
  445.2 6.6 reshape.139
  451.8 10.2 %gather_fusion.3 = f32[512,3072]{1,0:T(8,128)} fusion(f32[544,3072]{1,0:T(8,128)} %reshape.139, s32[1024]{0:T(1024)S(1)} %pad_clamp_fusion), kind=kCustom, calls=%fused_computation.3 | custom fusion | bytes 12584960 | tf_op jit(solution)/shard_map/gather | solution.py:84
  462.0 7.6 reshape.140
  469.6 147.5 %all-to-all-done.3 = f32[16,34,3072]{2,1,0:T(8,128)} async-done(((f32[16,34,3072]{2,1,0:T(8,128)}), f32[16,34,3072]{2,1,0:T(8,128)}, u32[]{:S(2)}, u32[]{:S(2)}) %all-to-all-start.3) | async-done | bytes 6684704 | tf_op jit(solution)/shard_map/all_to_all | solution.py:126
  617.2 6.6 reshape.141
  623.8 10.3 %gather_fusion.4 = f32[512,3072]{1,0:T(8,128)} fusion(f32[544,3072]{1,0:T(8,128)} %reshape.141, s32[1024]{0:T(1024)S(1)} %pad_clamp_fusion), kind=kCustom, calls=%fused_computation.4 | custom fusion | bytes 12584960 | tf_op jit(solution)/shard_map/gather | solution.py:130
  634.0 7.6 reshape.142
  641.6 7.8 reduce_sum.79
  651.5 212.6 %all-reduce.5.cloned.1.call-done = (f32[128,4,3072]{2,1,0:T(4,128)}, f32[128,3072]{1,0:T(8,128)}) async-done(((f32[128,4,3072]{2,1,0:T(4,128)}, f32[128,3072]{1,0:T(8,128)}), (f32[128,4,3072]{2,1,0:T(4,128)}, f32[128,3072]{1,0:T(8,128)})) %all-reduce.5.cloned.1.call-update) | async-done | bytes 7864336
  (63 shorter events, 33.6 us)
Async XLA Ops:
  6.5 240.2 %copy-start = (bf16[1,168,3072]{2,1,0:T(8,128)(2,1)S(1)}, bf16[1,168,3072]{2,1,0:T(8,128)(2,1)}, u32[]{:S(2)}) copy-start(bf16[1,168,3072]{2,1,0:T(8,128)(2,1)} %param.15) | copy-start | bytes 3096580
  26.0 4.9 copy-start.2
  150.1 91.8 %all-to-all-start = ((bf16[16,34,3072]{2,1,0:T(8,128)(2,1)}), bf16[16,34,3072]{2,1,0:T(8,128)(2,1)}, u32[]{:S(2)}, u32[]{:S(2)}) async-start(bf16[16,34,3072]{2,1,0:T(8,128)(2,1)} %get-tuple-element.16), calls=%async_computation | async-start | bytes 7864320 | tf_op jit(solution)/shard_map/all_to_all | solution.py:120
  154.7 4.9 copy-start.3
  246.8 3.7 copy-start.4
  261.7 177.7 %all-to-all-start.2 = ((f32[16,34,3072]{2,1,0:T(8,128)}), f32[16,34,3072]{2,1,0:T(8,128)}, u32[]{:S(2)}, u32[]{:S(2)}) async-start(f32[16,34,3072]{2,1,0:T(8,128)} %reshape.138), calls=%async_computation.2 | async-start | bytes 15728640 | tf_op jit(solution)/shard_map/all_to_all | solution.py:123
  439.4 177.7 %all-to-all-start.3 = ((f32[16,34,3072]{2,1,0:T(8,128)}), f32[16,34,3072]{2,1,0:T(8,128)}, u32[]{:S(2)}, u32[]{:S(2)}) async-start(f32[16,34,3072]{2,1,0:T(8,128)} %fusion.7), calls=%async_computation.3 | async-start | bytes 15728640 | tf_op jit(solution)/shard_map/all_to_all | solution.py:126
  444.9 419.2 %all-reduce.5.cloned.1.call-start = ((), (), s32[]{:S(2)}) async-start(), calls=%async_computation.4 | async-start | bytes 15728640
  649.4 218.9 %copy-start.1 = (bf16[1,168,3072]{2,1,0:T(8,128)(2,1)S(1)}, bf16[1,168,3072]{2,1,0:T(8,128)(2,1)}, u32[]{:S(2)}) copy-start(bf16[1,168,3072]{2,1,0:T(8,128)(2,1)} %param.15) | copy-start | bytes 3096580
  649.4 216.1 %copy-start.5 = (bf16[3072,16]{0,1:T(8,128)(2,1)S(1)}, bf16[3072,16]{0,1:T(8,128)(2,1)}, u32[]{:S(2)}) copy-start(bf16[3072,16]{0,1:T(8,128)(2,1)} %param.11) | copy-start | bytes 294916
  649.4 216.1 %copy-start.6 = (f32[3072]{0:T(1024)S(1)}, f32[3072]{0:T(1024)}, u32[]{:S(2)}) copy-start(f32[3072]{0:T(1024)} %param.10) | copy-start | bytes 36868
Sparse Core Ops, SparseCore 0:
  649.5 214.5 all-reduce.4
where the time goes:
time: 877 us; the launch traced here: 875 us
  waiting for transfers between devices  605 us (69%)
  blocking collectives  102 us (12%)
  local copies, waits for them, and re-layouts  94.6 us (11%)
  other arithmetic  22.6 us (3%)
  matrix products  20.6 us (2%)
  starting transfers between devices  15.7 us (2%)
  between operations  14.3 us (2%)
    unnamed x2, waiting for transfers between devices  213 us
    all_to_all x1, waiting for transfers between devices, shards(): lax.all_to_all(dh_rows.reshape(experts, count, width), 'expert', split_ax...  168 us
    all_to_all x1, waiting for transfers between devices, shards(): lax.all_to_all(y_rows.reshape(experts, count, width), 'expert', split_axi...  148 us
    all_to_all x1, blocking collectives, shards(): lax.all_to_all(send_h, 'expert', split_axis=0, concat_axis=0, tiled=True)  102 us
    all_to_all x1, waiting for transfers between devices, shards(): lax.all_to_all(send_dy, 'expert', split_axis=0, concat_axis=0, tiled=True)  77.4 us
  transfers between devices with their start and end apart: 4, of which 4 were waited for; matrix products, arithmetic and copies ran while one was open for 5% of the time, Pallas kernels for 0%

commit v1 on v0

v1 whole, which is shorter than its diff:
```python
import jax
import jax.numpy as jnp
import numpy as np
from jax import lax
from jax.sharding import Mesh, PartitionSpec as P

eps = 1e-05
X = 4
CORES = 2
bf16 = jnp.bfloat16
f32 = jnp.float32


def token_weights(acts, gain, router, ids):
    wide = acts.astype(f32)
    recip = lax.rsqrt(jnp.mean(wide * wide, axis=-1, keepdims=True) + eps)
    h = (wide * recip * gain).astype(bf16)
    logits = jnp.dot(h, router, preferred_element_type=f32)
    experts = router.shape[1]
    select = (ids[:, :, None] == jnp.arange(experts, dtype=jnp.int32)[None, None, :]).astype(f32)
    picked = jnp.sum(select * logits[:, None, :], axis=-1)
    sig = jax.nn.sigmoid(picked)
    total = jnp.sum(sig, axis=1, keepdims=True)
    return h, sig, total, sig / total, select


def slots(ids, names, cap):
    tokens = ids.shape[0]
    member = jnp.any(ids[:, :, None] == names[None, None, :], axis=1)
    below = (jnp.arange(tokens)[:, None] > jnp.arange(tokens)[None, :]).astype(bf16)
    place = jnp.dot(below, member.astype(bf16), preferred_element_type=f32).astype(jnp.int32)
    place = jnp.where(member, place, cap)
    return place.T[:, None, :] == jnp.arange(cap, dtype=jnp.int32)[None, :, None]


def expert_rows(h, g, gate_rows, units):
    contract = (((1,), (1,)), ((), ()))
    dh = 0.0
    score = 0.0
    for wg, wu, wd in units:
        a = jnp.dot(h, wg, preferred_element_type=f32)
        b = jnp.dot(h, wu, preferred_element_type=f32)
        pulled = lax.dot_general(g, wd, contract, preferred_element_type=f32)
        sg = jax.nn.sigmoid(a)
        sa = a * sg
        act = (sa * b).astype(bf16).astype(f32)
        score = score + jnp.sum(act * pulled, axis=-1)
        dact = pulled * gate_rows
        da = (dact * b * sg * (1.0 + a * (1.0 - sg))).astype(bf16)
        db = (dact * sa).astype(bf16)
        dh = dh + lax.dot_general(da, wg, contract, preferred_element_type=f32)
        dh = dh + lax.dot_general(db, wu, contract, preferred_element_type=f32)
    return dh, score


def shards(acts, cotangent, gain, router, ids, w_gate, w_up, w_down):
    ny, nx, nz, nc = (lax.axis_size(n) for n in ("y", "x", "z", "core"))
    y, x, core = (lax.axis_index(n) for n in ("y", "x", "core"))
    tokens, width = acts.shape
    top = ids.shape[1]
    experts = nz * nc
    cap = min(tokens, (17 * tokens * top + 16 * experts - 1) // (16 * experts))
    part = width // ny
    parity = x % 2
    own = core == parity

    mine = (w_gate[0], w_up[0], w_down[0])
    pairs = []
    for m in range(nx // 2):
        i, j = (2 * m) * nc + 1, (2 * m + 1) * nc
        pairs += [(i, j), (j, i)]
    swapped = tuple(lax.ppermute(w, ("x", "core"), pairs) for w in mine)
    first = tuple(jnp.where(own, w, s) for w, s in zip(mine, swapped))
    second = tuple(lax.ppermute(w, "core", [(0, 1), (1, 0)]) for w in first)

    h, sig, total, weight, select = token_weights(acts, gain, router, ids)
    names = 2 * jnp.arange(nz, dtype=jnp.int32) + parity
    here = slots(ids, names, cap)
    pick = here.astype(bf16).reshape(nz * cap, tokens)
    h_part = lax.dynamic_slice_in_dim(h, y * part, part, 1)
    g_part = lax.dynamic_slice_in_dim(cotangent, y * part, part, 1)
    both = jnp.concatenate([h_part, g_part], axis=1)
    rows = jnp.dot(pick, both, preferred_element_type=f32).astype(bf16)
    rows = lax.all_to_all(rows.reshape(nz, cap, 2 * part), "z", 0, 0, tiled=True)
    gathered = lax.all_gather(rows.reshape(nz * cap, 2 * part), "y")
    chosen = jnp.any(ids[:, :, None] == names[None, None, :], axis=1)
    of_name = (ids[:, :, None] == names[None, None, :]).astype(f32)
    dense = jnp.sum(of_name * weight[:, :, None], axis=1)
    gate = jnp.sum(here.astype(f32) * dense.T[:, None, :], axis=-1).astype(bf16)
    gate = lax.all_to_all(gate, "z", 0, 0, tiled=True).reshape(nz * cap, 1).astype(f32)

    h_rows = jnp.concatenate([gathered[i, :, :part] for i in range(ny)], axis=1)
    g_rows = jnp.concatenate([gathered[i, :, part:] for i in range(ny)], axis=1)
    dh, score = expert_rows(h_rows, g_rows, gate, (first, second))

    dh = dh.astype(bf16).reshape(nz * cap, ny, part).swapaxes(0, 1)
    dh = lax.psum_scatter(dh, "y", scatter_dimension=0)
    score = lax.all_to_all(score.reshape(nz, cap), "z", 0, 0, tiled=True)
    score = jnp.sum(here.astype(f32) * score[:, :, None], axis=1)
    score = jnp.sum(of_name * score.T[:, None, :], axis=-1)
    dh = lax.all_to_all(dh.reshape(nz, cap, part), "z", 0, 0, tiled=True)
    dh_tok = lax.dot_general(
        pick, dh.reshape(nz * cap, part), (((0,), (0,)), ((), ())), preferred_element_type=f32
    )
    sections = ny * nx
    share = tokens // sections
    tail = jnp.zeros((tokens, 128), f32).at[:, :top].set(score)
    packet = jnp.concatenate([dh_tok, tail], axis=1).reshape(sections, share, part + 128)
    packet = lax.all_to_all(packet, ("y", "x"), 0, 0, tiled=True)
    packet = packet.reshape(ny, nx, share, part + 128).sum(axis=1)
    dh_share = jnp.concatenate([packet[i, :, :part] for i in range(ny)], axis=1)
    score_share = packet[:, :, part : part + top].sum(axis=0)

    start = (y * nx + x) * share
    cut = lambda v: lax.dynamic_slice_in_dim(v, start, share, 0)
    sig, total, weight, select = cut(sig), cut(total), cut(weight), cut(select)
    wide = cut(acts).astype(f32)
    g = cut(cotangent).astype(f32)
    dsig = (score_share - jnp.sum(weight * score_share, axis=1, keepdims=True)) / total
    dpick = dsig * sig * (1.0 - sig)
    dlogits = jnp.sum(dpick[:, :, None] * select, axis=1)
    dh_total = dh_share + lax.dot_general(
        dlogits, router.astype(f32), (((1,), (1,)), ((), ())), precision=lax.Precision.HIGHEST
    )
    recip = lax.rsqrt(jnp.mean(wide * wide, axis=-1, keepdims=True) + eps)
    scaled = dh_total * gain
    pulled = recip * scaled - wide * (recip * recip * recip) * jnp.mean(
        wide * scaled, axis=-1, keepdims=True
    )
    return (g + pulled)[None]


def solution(mesh):
    pipe, expert = mesh.devices.shape
    grid = Mesh(
        mesh.devices.reshape(pipe // X, X, expert // CORES, CORES), ("y", "x", "z", "core")
    )
    exp, pipe = ("z", "core"), ("y", "x")
    in_specs = (
        P(exp, None),
        P(exp, None),
        P(),
        P(),
        P(exp, None),
        P(exp, None, pipe),
        P(exp, None, pipe),
        P(exp, pipe, None),
    )
    return jax.shard_map(
        shards, mesh=grid, in_specs=in_specs, out_specs=P(pipe, exp, None), check_vma=False
    )
```

time: 877 us -> 221 us (0.25)
  the two profiles are of different devices: /device:TPU:1 before, /device:TPU:8 now
where the time goes in v1:
time: 221 us; the launch traced here: 220 us
  waiting for transfers between devices  66.1 us (30%)
  starting transfers between devices  61.4 us (28%)
  blocking collectives  37 us (17%)
  matrix products  19 us (9%)
  between operations  13.9 us (6%)
  local copies, waits for them, and re-layouts  12 us (5%)
  other arithmetic  10.6 us (5%)
    reduce_scatter x1, waiting for transfers between devices, shards(): dh = lax.psum_scatter(dh, 'y', scatter_dimension=0)  37 us
    ppermute x3, starting transfers between devices, shards(): second = tuple((lax.ppermute(w, 'core', [(0, 1), (1, 0)]) for w in first))  33.6 us
    all_to_all x1, blocking collectives, shards(): lax.all_to_all(rows.reshape(nz, cap, 2 * part), 'z', 0, 0, tiled=True)  26.9 us
    all_to_all x1, waiting for transfers between devices, shards(): packet = lax.all_to_all(packet, ('y', 'x'), 0, 0, tiled=True)  10.7 us
    all_to_all x1, blocking collectives, shards(): lax.all_to_all(gate, 'z', 0, 0, tiled=True).reshape(nz * cap, 1).astype(f32)  10 us
    all_to_all x1, waiting for transfers between devices, shards(): dh = lax.all_to_all(dh.reshape(nz, cap, part), 'z', 0, 0, tiled=True)  8.81 us
    all_to_all x1, starting transfers between devices, shards(): packet = lax.all_to_all(packet, ('y', 'x'), 0, 0, tiled=True)  7.98 us
    all_to_all x1, starting transfers between devices, shards(): dh = lax.all_to_all(dh.reshape(nz, cap, part), 'z', 0, 0, tiled=True)  7.5 us
  transfers between devices with their start and end apart: 11, of which 5 were waited for; matrix products, arithmetic and copies ran while one was open for 9% of the time, Pallas kernels for 0%

profile of v1, /device:TPU:8, one launch (start us, length us, event | category | flops | bytes accessed | tf_op | source)
XLA Modules:
  0.0 220.0 jit_solution(3683132165448547522)
XLA Ops:
  11.4 26.9 %all_to_all.27 = bf16[8,34,768]{2,1,0:T(8,128)(2,1)S(1)} all-to-all(bf16[8,34,768]{2,1,0:T(8,128)(2,1)S(1)} %reshape.151), channel_id=1, replica_groups=mesh['y'=8,'x'=4,'z'=8,'core'=2] {'z'}, dimensions={0} | all-to-all | bytes 835584 | tf_op jit(solution)/shard_map/all_to_all | solution.py:84
  39.2 1.7 collective-permute-start.1
  40.9 1.6 collective-permute-start.2
  42.5 1.6 collective-permute-start
  45.9 13.5 %collective-permute-start.4 = (bf16[3072,168]{0,1:T(8,128)(2,1)S(1)}, bf16[3072,168]{0,1:T(8,128)(2,1)}, u32[]{:S(2)}, u32[]{:S(2)}) collective-permute-start(bf16[3072,168]{0,1:T(8,128)(2,1)S(1)} %broadcast_select_fusion.1), channel_id=1, source_target_pairs={{0,1},{1,0},{2,3},{3,2},{4,5},{5,4},{6,7},{7,6},{8,9},{9,8},{10,11... | collective-permute-start | bytes 3096584 | tf_op jit(solution)/shard_map/ppermute | solution.py:74
  60.7 9.6 %collective-permute-start.5 = (bf16[3072,168]{0,1:T(8,128)(2,1)S(1)}, bf16[3072,168]{0,1:T(8,128)(2,1)}, u32[]{:S(2)}, u32[]{:S(2)}) collective-permute-start(bf16[3072,168]{0,1:T(8,128)(2,1)S(1)} %broadcast_select_fusion), channel_id=1, source_target_pairs={{0,1},{1,0},{2,3},{3,2},{4,5},{5,4},{6,7},{7,6},{8,9},{9,8},{10,11... | collective-permute-start | bytes 3096584 | tf_op jit(solution)/shard_map/ppermute | solution.py:74
  71.5 10.6 %collective-permute-start.3 = (bf16[168,3072]{1,0:T(8,128)(2,1)}, bf16[168,3072]{1,0:T(8,128)(2,1)}, u32[]{:S(2)}, u32[]{:S(2)}) collective-permute-start(bf16[168,3072]{1,0:T(8,128)(2,1)} %broadcast_select_fusion.2), channel_id=1, source_target_pairs={{0,1},{1,0},{2,3},{3,2},{4,5},{5,4},{6,7},{7,6},{8,9},{9,8},{10,11... | collective-permute-start | bytes 3096584 | tf_op jit(solution)/shard_map/ppermute | solution.py:74
  82.0 2.1 all-gather.2.cloned.1.call-done
  91.0 2.2 %fusion.63 = f32[272,168]{0,1:T(8,128)S(1)} fusion(bf16[272,3072]{1,0:T(8,128)(2,1)S(1)} %get-tuple-element.23, bf16[3072,168]{0,1:T(8,128)(2,1)} %collective-permute-done.4), kind=kOutput, calls=%fused_computation.145 | convolution fusion | flops 280756224 | bytes 2886144 | tf_op jit(solution)/shard_map/dot_general | solution.py:42
  93.3 2.2 %fusion.64 = f32[272,168]{0,1:T(8,128)S(1)} fusion(bf16[272,3072]{1,0:T(8,128)(2,1)S(1)} %get-tuple-element.23, bf16[3072,168]{0,1:T(8,128)(2,1)} %collective-permute-done.5), kind=kOutput, calls=%fused_computation.146 | convolution fusion | flops 280756224 | bytes 2886144 | tf_op jit(solution)/shard_map/dot_general | solution.py:41
  95.5 2.8 %multiply_reduce_fusion.1 = (f32[272]{0:T(512)S(1)}, f32[272,168]{0,1:T(8,128)}) fusion(f32[272,168]{0,1:T(8,128)S(1)} %fusion.61, f32[272,168]{0,1:T(8,128)S(1)} %fusion.62, bf16[272,3072]{1,0:T(8,128)(2,1)S(1)} %get-tuple-element.24, bf16[168,3072]{1,0:T(8,128)(2,1)} %broadcast_select_fusion.2), kind=kOutput, calls=%fused_computation.24 | convolution fusion | flops 281167232 | bytes 3252800 | tf_op jit(solution)/shard_map/dot_general | solution.py:43
  98.3 2.2 multiply_reduce_fusion
  101.2 7.4 %all-to-all-start.3 = ((f32[8,1,34]{2,1,0:T(1,128)}), f32[8,1,34]{2,1,0:T(1,128)S(1)}, u32[]{:S(2)}, u32[]{:S(2)}) async-start(f32[8,1,34]{2,1,0:T(1,128)} %add.123), calls=%async_computation.4 | async-start | bytes 8192 | tf_op jit(solution)/shard_map/all_to_all | solution.py:98
  108.7 7.5 %all-to-all-done.3 = f32[8,1,34]{2,1,0:T(1,128)S(1)} async-done(((f32[8,1,34]{2,1,0:T(1,128)}), f32[8,1,34]{2,1,0:T(1,128)S(1)}, u32[]{:S(2)}, u32[]{:S(2)}) %all-to-all-start.3) | async-done | bytes 1120 | tf_op jit(solution)/shard_map/all_to_all | solution.py:98
  116.4 10.0 %all_to_all.28 = bf16[8,1,34]{2,1,0:T(2,128)(2,1)S(1)} all-to-all(bf16[8,1,34]{2,1,0:T(2,128)(2,1)S(1)} %copy.49), channel_id=1, replica_groups=mesh['y'=8,'x'=4,'z'=8,'core'=2] {'z'}, dimensions={0} | all-to-all | bytes 1088 | tf_op jit(solution)/shard_map/all_to_all | solution.py:90
  126.5 1.8 fusion.30
  128.3 1.9 fusion.31
  130.2 1.9 fusion.32
  134.4 37.0 %reduce-scatter.2.cloned.1.call-done = bf16[1,272,384]{2,1,0:T(8,128)(2,1)} async-done(((bf16[8,272,384]{2,1,0:T(8,128)(2,1)}), bf16[1,272,384]{2,1,0:T(8,128)(2,1)}) %reduce-scatter.2.cloned.1.call-update) | async-done | bytes 208912 | tf_op jit(solution)/shard_map/reduce_scatter | solution.py:97
  171.3 1.7 reshape_reduce_scatter.3
  173.0 7.5 %all-to-all-start.2 = ((bf16[8,34,384]{2,1,0:T(8,128)(2,1)}), bf16[8,34,384]{2,1,0:T(8,128)(2,1)S(1)}, u32[]{:S(2)}, u32[]{:S(2)}) async-start(bf16[8,34,384]{2,1,0:T(8,128)(2,1)} %reshape_reduce_scatter.3), calls=%async_computation.3 | async-start | bytes 491520 | tf_op jit(solution)/shard_map/all_to_all | solution.py:101
  182.0 8.8 %all-to-all-done.2 = bf16[8,34,384]{2,1,0:T(8,128)(2,1)S(1)} async-done(((bf16[8,34,384]{2,1,0:T(8,128)(2,1)}), bf16[8,34,384]{2,1,0:T(8,128)(2,1)S(1)}, u32[]{:S(2)}, u32[]{:S(2)}) %all-to-all-start.2) | async-done | bytes 208928 | tf_op jit(solution)/shard_map/all_to_all | solution.py:101
  191.9 8.0 %all-to-all-start.4 = ((f32[32,4,512]{2,1,0:T(4,128)}), f32[32,4,512]{2,1,0:T(4,128)S(1)}, u32[]{:S(2)}, u32[]{:S(2)}) async-start(f32[32,4,512]{2,1,0:T(4,128)} %reshape.153), calls=%async_computation.5 | async-start | bytes 524288 | tf_op jit(solution)/shard_map/all_to_all | solution.py:109
  200.0 10.7 %all-to-all-done.4 = f32[32,4,512]{2,1,0:T(4,128)S(1)} async-done(((f32[32,4,512]{2,1,0:T(4,128)}), f32[32,4,512]{2,1,0:T(4,128)S(1)}, u32[]{:S(2)}, u32[]{:S(2)}) %all-to-all-start.4) | async-done | bytes 262176 | tf_op jit(solution)/shard_map/all_to_all | solution.py:109
  (103 shorter events, 25.0 us)
Async XLA Ops:
  6.5 37.6 %copy-start = (bf16[3072,16]{0,1:T(8,128)(2,1)S(1)}, bf16[3072,16]{0,1:T(8,128)(2,1)}, u32[]{:S(2)}) copy-start(bf16[3072,16]{0,1:T(8,128)(2,1)} %param.13) | copy-start | bytes 294916
  6.5 2.5 %copy-start.1 = (bf16[128,3072]{1,0:T(8,128)(2,1)S(1)}, bf16[128,3072]{1,0:T(8,128)(2,1)}, u32[]{:S(2)}) copy-start(bf16[128,3072]{1,0:T(8,128)(2,1)} %param.10) | copy-start | bytes 2359300
  6.5 77.6 %all-gather.2.cloned.1.call-start = ((), (), s32[]{:S(2)}) async-start(), calls=%async_computation.6 | async-start | bytes 3760128 | tf_op jit(solution)/shard_map/all_gather | solution.py:85
  11.4 33.0 %copy-start.11 = (s32[128,4]{0,1:T(4,128)S(1)}, s32[128,4]{0,1:T(4,128)}, u32[]{:S(2)}) copy-start(s32[128,4]{0,1:T(4,128)} %param.14) | copy-start | bytes 6148
  39.2 5.3 %collective-permute-start.1 = (bf16[3072,168]{0,1:T(8,128)(2,1)}, bf16[3072,168]{0,1:T(8,128)(2,1)}, u32[]{:S(2)}, u32[]{:S(2)}) collective-permute-start(bf16[3072,168]{0,1:T(8,128)(2,1)} %bitcast.147), channel_id=1, source_target_pairs={{1,16},{16,1},{33,48},{48,33},{3,18},{18,3},{35,50},{50,35},{5,20}... | collective-permute-start | bytes 3096584 | tf_op jit(solution)/shard_map/ppermute | solution.py:72
  40.9 18.5 %collective-permute-start.2 = (bf16[3072,168]{0,1:T(8,128)(2,1)}, bf16[3072,168]{0,1:T(8,128)(2,1)}, u32[]{:S(2)}, u32[]{:S(2)}) collective-permute-start(bf16[3072,168]{0,1:T(8,128)(2,1)} %bitcast.148), channel_id=1, source_target_pairs={{1,16},{16,1},{33,48},{48,33},{3,18},{18,3},{35,50},{50,35},{5,20}... | collective-permute-start | bytes 3096584 | tf_op jit(solution)/shard_map/ppermute | solution.py:72
  42.5 27.8 %collective-permute-start = (bf16[168,3072]{1,0:T(8,128)(2,1)}, bf16[168,3072]{1,0:T(8,128)(2,1)}, u32[]{:S(2)}, u32[]{:S(2)}) collective-permute-start(bf16[168,3072]{1,0:T(8,128)(2,1)} %bitcast.149), channel_id=1, source_target_pairs={{1,16},{16,1},{33,48},{48,33},{3,18},{18,3},{35,50},{50,35},{5,20}... | collective-permute-start | bytes 3096584 | tf_op jit(solution)/shard_map/ppermute | solution.py:72
  45.9 24.4 %copy-start.6 = (bf16[1,168,3072]{2,1,0:T(8,128)(2,1)S(1)}, bf16[1,168,3072]{2,1,0:T(8,128)(2,1)}, u32[]{:S(2)}) copy-start(bf16[1,168,3072]{2,1,0:T(8,128)(2,1)} %param.17) | copy-start | bytes 3096580
  45.9 45.1 %collective-permute-start.4 = (bf16[3072,168]{0,1:T(8,128)(2,1)S(1)}, bf16[3072,168]{0,1:T(8,128)(2,1)}, u32[]{:S(2)}, u32[]{:S(2)}) collective-permute-start(bf16[3072,168]{0,1:T(8,128)(2,1)S(1)} %broadcast_select_fusion.1), channel_id=1, source_target_pairs={{0,1},{1,0},{2,3},{3,2},{4,5},{5,4},{6,7},{7,6},{8,9},{9,8},{10,11... | collective-permute-start | bytes 3096584 | tf_op jit(solution)/shard_map/ppermute | solution.py:74
  60.7 32.5 %collective-permute-start.5 = (bf16[3072,168]{0,1:T(8,128)(2,1)S(1)}, bf16[3072,168]{0,1:T(8,128)(2,1)}, u32[]{:S(2)}, u32[]{:S(2)}) collective-permute-start(bf16[3072,168]{0,1:T(8,128)(2,1)S(1)} %broadcast_select_fusion), channel_id=1, source_target_pairs={{0,1},{1,0},{2,3},{3,2},{4,5},{5,4},{6,7},{7,6},{8,9},{9,8},{10,11... | collective-permute-start | bytes 3096584 | tf_op jit(solution)/shard_map/ppermute | solution.py:74
  71.5 26.9 %collective-permute-start.3 = (bf16[168,3072]{1,0:T(8,128)(2,1)}, bf16[168,3072]{1,0:T(8,128)(2,1)}, u32[]{:S(2)}, u32[]{:S(2)}) collective-permute-start(bf16[168,3072]{1,0:T(8,128)(2,1)} %broadcast_select_fusion.2), channel_id=1, source_target_pairs={{0,1},{1,0},{2,3},{3,2},{4,5},{5,4},{6,7},{7,6},{8,9},{9,8},{10,11... | collective-permute-start | bytes 3096584 | tf_op jit(solution)/shard_map/ppermute | solution.py:74
  84.1 4.7 %copy-start.2 = (bf16[8,272,768]{2,1,0:T(8,128)(2,1)S(1)}, bf16[8,272,768]{2,1,0:T(8,128)(2,1)}, u32[]{:S(2)}) copy-start(bf16[8,272,768]{2,1,0:T(8,128)(2,1)} %all-gather.2.cloned.1.call-done) | copy-start | bytes 10027012
  90.1 5.4 %copy-start.3 = (f32[272,168]{0,1:T(8,128)}, f32[272,168]{0,1:T(8,128)S(1)}, u32[]{:S(2)}) copy-start(f32[272,168]{0,1:T(8,128)S(1)} %fusion.62) | copy-start | bytes 548356
  91.0 4.5 %copy-start.9 = (f32[272,168]{0,1:T(8,128)}, f32[272,168]{0,1:T(8,128)S(1)}, u32[]{:S(2)}) copy-start(f32[272,168]{0,1:T(8,128)S(1)} %fusion.61) | copy-start | bytes 548356
  93.2 5.1 %copy-start.7 = (f32[272,168]{0,1:T(8,128)}, f32[272,168]{0,1:T(8,128)S(1)}, u32[]{:S(2)}) copy-start(f32[272,168]{0,1:T(8,128)S(1)} %fusion.63) | copy-start | bytes 548356
  101.2 15.0 %all-to-all-start.3 = ((f32[8,1,34]{2,1,0:T(1,128)}), f32[8,1,34]{2,1,0:T(1,128)S(1)}, u32[]{:S(2)}, u32[]{:S(2)}) async-start(f32[8,1,34]{2,1,0:T(1,128)} %add.123), calls=%async_computation.4 | async-start | bytes 8192 | tf_op jit(solution)/shard_map/all_to_all | solution.py:98
  108.6 62.8 %reduce-scatter.2.cloned.1.call-start = ((), (), s32[]{:S(2)}) async-start(), calls=%async_computation.7 | async-start | bytes 1880064 | tf_op jit(solution)/shard_map/reduce_scatter | solution.py:97
  126.5 1.8 copy-start.8
  130.2 2.0 copy-start.4
  130.2 2.0 copy-start.5
  130.2 2.0 copy-start.10
  173.0 38.2 %copy-start.12 = (f32[3072]{0:T(1024)S(1)}, f32[3072]{0:T(1024)}, u32[]{:S(2)}) copy-start(f32[3072]{0:T(1024)} %param.12) | copy-start | bytes 36868
  173.0 17.8 %all-to-all-start.2 = ((bf16[8,34,384]{2,1,0:T(8,128)(2,1)}), bf16[8,34,384]{2,1,0:T(8,128)(2,1)S(1)}, u32[]{:S(2)}, u32[]{:S(2)}) async-start(bf16[8,34,384]{2,1,0:T(8,128)(2,1)} %reshape_reduce_scatter.3), calls=%async_computation.3 | async-start | bytes 491520 | tf_op jit(solution)/shard_map/all_to_all | solution.py:101
  191.9 18.8 %all-to-all-start.4 = ((f32[32,4,512]{2,1,0:T(4,128)}), f32[32,4,512]{2,1,0:T(4,128)S(1)}, u32[]{:S(2)}, u32[]{:S(2)}) async-start(f32[32,4,512]{2,1,0:T(4,128)} %reshape.153), calls=%async_computation.5 | async-start | bytes 524288 | tf_op jit(solution)/shard_map/all_to_all | solution.py:109
Sparse Core Ops, SparseCore 0:
  39.3 44.7 all-gather.1
  134.5 36.8 reduce-scatter.1

commit v2 on v1

--- a/solution.py
+++ b/solution.py
@@ -1,7 +1,9 @@
+import functools
 import jax
 import jax.numpy as jnp
-import numpy as np
 from jax import lax
+from jax.experimental import pallas as pl
+from jax.experimental.pallas import tpu as pltpu
 from jax.sharding import Mesh, PartitionSpec as P
 
 eps = 1e-05
@@ -24,33 +26,101 @@
     return h, sig, total, sig / total, select
 
 
-def slots(ids, names, cap):
+def slots(ids, names, cap, rank):
     tokens = ids.shape[0]
     member = jnp.any(ids[:, :, None] == names[None, None, :], axis=1)
     below = (jnp.arange(tokens)[:, None] > jnp.arange(tokens)[None, :]).astype(bf16)
     place = jnp.dot(below, member.astype(bf16), preferred_element_type=f32).astype(jnp.int32)
-    place = jnp.where(member, place, cap)
-    return place.T[:, None, :] == jnp.arange(cap, dtype=jnp.int32)[None, :, None]
-
-
-def expert_rows(h, g, gate_rows, units):
+    place = jnp.where(member, place, rank)
+    return place.T[:, None, :] == jnp.arange(rank, dtype=jnp.int32)[None, :, None]
+
+
+def expert_kernel(cap, nz, rows_hbm, gate_ref, *refs):
+    weights, (out_ref, rows, wg, wu, wd, sem) = refs[:6], refs[6:]
+    ny, count, part = rows.shape[0], rows.shape[1], rows.shape[2] // 2
+    rank = out_ref.shape[2]
     contract = (((1,), (1,)), ((), ()))
-    dh = 0.0
+    copies = []
+    for i in range(ny):
+        band = pl.ds(i * part, part)
+        mine = [(rows_hbm.at[i], rows.at[i])]
+        for u in range(2):
+            g_hbm, u_hbm, d_hbm = weights[3 * u : 3 * u + 3]
+            mine.append((g_hbm.at[band, :], wg.at[u, band, :]))
+            mine.append((u_hbm.at[band, :], wu.at[u, band, :]))
+            mine.append((d_hbm.at[:, band], wd.at[u, :, band]))
+        mine = [pltpu.make_async_copy(s, d, sem.at[i, j]) for j, (s, d) in enumerate(mine)]
+        for copy in mine:
+            copy.start()
+        copies.append(mine)
+    a, b, pulled = [0.0, 0.0], [0.0, 0.0], [0.0, 0.0]
+    for i in range(ny):
+        band = pl.ds(i * part, part)
+        for copy in copies[i]:
+            copy.wait()
+        h = rows[i, :, :part]
+        g = rows[i, :, part:]
+        for u in range(2):
+            a[u] = a[u] + jnp.dot(h, wg[u, band, :], preferred_element_type=f32)
+            b[u] = b[u] + jnp.dot(h, wu[u, band, :], preferred_element_type=f32)
+            pulled[u] = pulled[u] + lax.dot_general(
+                g, wd[u, :, band], contract, preferred_element_type=f32
+            )
+    da, db = [], []
     score = 0.0
-    for wg, wu, wd in units:
-        a = jnp.dot(h, wg, preferred_element_type=f32)
-        b = jnp.dot(h, wu, preferred_element_type=f32)
-        pulled = lax.dot_general(g, wd, contract, preferred_element_type=f32)
-        sg = jax.nn.sigmoid(a)
-        sa = a * sg
-        act = (sa * b).astype(bf16).astype(f32)
-        score = score + jnp.sum(act * pulled, axis=-1)
-        dact = pulled * gate_rows
-        da = (dact * b * sg * (1.0 + a * (1.0 - sg))).astype(bf16)
-        db = (dact * sa).astype(bf16)
-        dh = dh + lax.dot_general(da, wg, contract, preferred_element_type=f32)
-        dh = dh + lax.dot_general(db, wu, contract, preferred_element_type=f32)
-    return dh, score
+    gate = gate_ref[...]
+    for u in range(2):
+        sg = jax.nn.sigmoid(a[u])
+        sa = a[u] * sg
+        act = (sa * b[u]).astype(bf16).astype(f32)
+        score = score + jnp.sum(act * pulled[u], axis=1, keepdims=True)
+        dact = pulled[u] * gate
+        da.append((dact * b[u] * sg * (1.0 + a[u] * (1.0 - sg))).astype(bf16))
+        db.append((dact * sa).astype(bf16))
+    lanes = lax.broadcasted_iota(jnp.int32, (cap, part), 1)
+    eye = lanes == lax.broadcasted_iota(jnp.int32, (cap, part), 0)
+    tails = []
+    for z in range(nz):
+        line = jnp.sum(jnp.where(eye, score[z * cap : (z + 1) * cap], 0.0), axis=0, keepdims=True)
+        high = line.astype(bf16).astype(f32)
+        rest = jnp.zeros((rank - cap - 2, part), f32)
+        tails.append(jnp.concatenate([high, line - high, rest], axis=0))
+    for i in range(ny):
+        band = pl.ds(i * part, part)
+        dh = 0.0
+        for u in range(2):
+            dh = dh + lax.dot_general(da[u], wg[u, band, :], contract, preferred_element_type=f32)
+            dh = dh + lax.dot_general(db[u], wu[u, band, :], contract, preferred_element_type=f32)
+        for z in range(nz):
+            block = jnp.concatenate([dh[z * cap : (z + 1) * cap], tails[z]], axis=0)
+            out_ref[i, z] = block.astype(bf16)
+
+
+def expert_rows(gathered, gate, first, second, nz, cap, rank):
+    ny, count, wide = gathered.shape
+    hidden = first[0].shape[1]
+    width = ny * wide // 2
+    hbm = pl.BlockSpec(memory_space=pl.ANY)
+    vmem = pl.BlockSpec(memory_space=pltpu.VMEM)
+    return pl.pallas_call(
+        functools.partial(expert_kernel, cap, nz),
+        out_shape=jax.ShapeDtypeStruct((ny, nz, rank, wide // 2), bf16),
+        in_specs=[hbm, vmem] + [hbm] * 6,
+        out_specs=vmem,
+        scratch_shapes=[
+            pltpu.VMEM((ny, count, wide), bf16),
+            pltpu.VMEM((2, width, hidden), bf16),
+            pltpu.VMEM((2, width, hidden), bf16),
+            pltpu.VMEM((2, hidden, width), bf16),
+            pltpu.SemaphoreType.DMA((ny, 7)),
+        ],
+        compiler_params=pltpu.CompilerParams(vmem_limit_bytes=40 * 1024 * 1024),
+        cost_estimate=pl.CostEstimate(
+            flops=12 * count * width * hidden * 2,
+            bytes_accessed=2 * (ny * count * wide + 6 * width * hidden + count * width),
+            transcendentals=2 * count * hidden,
+        ),
+    )(gathered, gate, *first, *second)
 
 
 def shards(acts, cotangent, gain, router, ids, w_gate, w_up, w_down):
@@ -75,33 +145,39 @@
 
     h, sig, total, weight, select = token_weights(acts, gain, router, ids)
     names = 2 * jnp.arange(nz, dtype=jnp.int32) + parity
-    here = slots(ids, names, cap)
-    pick = here.astype(bf16).reshape(nz * cap, tokens)
+    rank = -(-(cap + 2) // 8) * 8
+    here = slots(ids, names, cap, rank)
+    pick = here.astype(bf16)
+    of_name = (ids[:, :, None] == names[None, None, :]).astype(f32)
+    dense = jnp.sum(of_name * weight[:, :, None], axis=1)
+    gate = jnp.sum(here.astype(f32) * dense.T[:, None, :], axis=-1).astype(bf16)
     h_part = lax.dynamic_slice_in_dim(h, y * part, part, 1)
     g_part = lax.dynamic_slice_in_dim(cotangent, y * part, part, 1)
     both = jnp.concatenate([h_part, g_part], axis=1)
-    rows = jnp.dot(pick, both, preferred_element_type=f32).astype(bf16)
-    rows = lax.all_to_all(rows.reshape(nz, cap, 2 * part), "z", 0, 0, tiled=True)
-    gathered = lax.all_gather(rows.reshape(nz * cap, 2 * part), "y")
-    chosen = jnp.any(ids[:, :, None] == names[None, None, :], axis=1)
-    of_name = (ids[:, :, None] == names[None, None, :]).astype(f32)
-    dense = jnp.sum(of_name * weight[:, :, None], axis=1)
-    gate = jnp.sum(here.astype(f32) * dense.T[:, None, :], axis=-1).astype(bf16)
-    gate = lax.all_to_all(gate, "z", 0, 0, tiled=True).reshape(nz * cap, 1).astype(f32)
-
-    h_rows = jnp.concatenate([gathered[i, :, :part] for i in range(ny)], axis=1)
-    g_rows = jnp.concatenate([gathered[i, :, part:] for i in range(ny)], axis=1)
-    dh, score = expert_rows(h_rows, g_rows, gate, (first, second))
-
-    dh = dh.astype(bf16).reshape(nz * cap, ny, part).swapaxes(0, 1)
-    dh = lax.psum_scatter(dh, "y", scatter_dimension=0)
-    score = lax.all_to_all(score.reshape(nz, cap), "z", 0, 0, tiled=True)
+    rows = jnp.dot(pick.reshape(nz * rank, tokens), both, preferred_element_type=f32)
+    rows = rows.astype(bf16).reshape(nz, rank, 2 * part)
+    line = jnp.pad(gate, ((0, 0), (0, 2 * part - rank)))[:, None, :]
+    at_cap = (jnp.arange(rank) == cap)[None, :, None]
+    rows = jnp.where(at_cap, line, rows)
+    rows = lax.all_to_all(rows, "z", 0, 0, tiled=True)
+    gathered = lax.all_gather(rows[:, :cap].reshape(nz * cap, 2 * part), "y")
+    gate = rows[:, cap, :cap].astype(f32).reshape(nz * cap, 1)
+
+    back = expert_rows(gathered, gate, first, second, nz, cap, rank)
+
+    back = back.reshape(ny * nz, rank, part)
+    back = lax.all_to_all(back, ("y", "z"), 0, 0, tiled=True)
+    spread = jnp.broadcast_to(pick[None], (ny, nz, rank, tokens)).reshape(ny * nz * rank, tokens)
+    dh_tok = lax.dot_general(
+        spread,
+        back.reshape(ny * nz * rank, part),
+        (((0,), (0,)), ((), ())),
+        preferred_element_type=f32,
+    )
+    score = jnp.sum(back[:, cap : cap + 2, :rank].astype(f32), axis=1)
+    score = score.reshape(ny, nz, rank).sum(axis=0)
     score = jnp.sum(here.astype(f32) * score[:, :, None], axis=1)
     score = jnp.sum(of_name * score.T[:, None, :], axis=-1)
-    dh = lax.all_to_all(dh.reshape(nz, cap, part), "z", 0, 0, tiled=True)
-    dh_tok = lax.dot_general(
-        pick, dh.reshape(nz * cap, part), (((0,), (0,)), ((), ())), preferred_element_type=f32
-    )
     sections = ny * nx
     share = tokens // sections
     tail = jnp.zeros((tokens, 128), f32).at[:, :top].set(score)
@@ -109,7 +185,7 @@
     packet = lax.all_to_all(packet, ("y", "x"), 0, 0, tiled=True)
     packet = packet.reshape(ny, nx, share, part + 128).sum(axis=1)
     dh_share = jnp.concatenate([packet[i, :, :part] for i in range(ny)], axis=1)
-    score_share = packet[:, :, part : part + top].sum(axis=0)
+    score_share = packet[0, :, part : part + top]
 
     start = (y * nx + x) * share
     cut = lambda v: lax.dynamic_slice_in_dim(v, start, share, 0)

time: 221 us -> 206 us (0.932)
  the two profiles are of different devices: /device:TPU:8 before, /device:TPU:1 now
where the time goes in v2:
time: 206 us; the launch traced here: 203 us
  waiting for transfers between devices  66.6 us (32%)
  starting transfers between devices  37 us (18%)
  blocking collectives  26.2 us (13%)
  local copies, waits for them, and re-layouts  25.5 us (12%)
  Pallas kernels  16.8 us (8%)
  other arithmetic  14.6 us (7%)
  between operations  13.7 us (7%)
  matrix products  2.46 us (1%)
    all_to_all x1, waiting for transfers between devices, shards(): back = lax.all_to_all(back, ('y', 'z'), 0, 0, tiled=True)  45.8 us
    all_to_all x1, blocking collectives, shards(): rows = lax.all_to_all(rows, 'z', 0, 0, tiled=True)  26.2 us
    pallas_call x1, Pallas kernels, expert_rows(): pl.pallas_call(functools.partial(expert_kernel, cap, nz), out_shape=jax.S...  16.8 us
    all_to_all x1, starting transfers between devices, shards(): packet = lax.all_to_all(packet, ('y', 'x'), 0, 0, tiled=True)  12.5 us
    ppermute x3, starting transfers between devices, shards(): swapped = tuple((lax.ppermute(w, ('x', 'core'), pairs) for w in mine))  10.9 us
    ppermute x3, waiting for transfers between devices, shards(): swapped = tuple((lax.ppermute(w, ('x', 'core'), pairs) for w in mine))  10.5 us
    all_to_all x1, waiting for transfers between devices, shards(): packet = lax.all_to_all(packet, ('y', 'x'), 0, 0, tiled=True)  10.3 us
    unnamed x27, local copies, waits for them, and re-layouts  9.38 us
  transfers between devices with their start and end apart: 9, of which 5 were waited for; matrix products, arithmetic and copies ran while one was open for 12% of the time, Pallas kernels for 0%

profile of v2, /device:TPU:1, one launch (start us, length us, event | category | flops | bytes accessed | tf_op | source)
XLA Modules:
  0.0 202.9 jit_solution(2232449806239409702)
XLA Ops:
  12.4 26.2 %all_to_all.15 = bf16[8,40,768]{2,1,0:T(8,128)(2,1)S(1)} all-to-all(bf16[8,40,768]{2,1,0:T(8,128)(2,1)S(1)} %broadcast_select_fusion.1), channel_id=1, replica_groups=mesh['y'=8,'x'=4,'z'=8,'core'=2] {'z'}, dimensions={0} | all-to-all | bytes 983040 | tf_op jit(solution)/shard_map/all_to_all | solution.py:162
  39.6 5.4 %collective-permute-start = (bf16[3072,168]{0,1:T(8,128)(2,1)S(1)}, bf16[3072,168]{0,1:T(8,128)(2,1)}, u32[]{:S(2)}, u32[]{:S(2)}) collective-permute-start(bf16[3072,168]{0,1:T(8,128)(2,1)S(1)} %bitcast.72), channel_id=1, source_target_pairs={{1,16},{16,1},{33,48},{48,33},{3,18},{18,3},{35,50},{50,35},{5,20}... | collective-permute-start | bytes 3096584 | tf_op jit(solution)/shard_map/ppermute | solution.py:142
  45.0 1.9 collective-permute-start.1
  46.9 3.6 %collective-permute-start.2 = (bf16[168,3072]{1,0:T(8,128)(2,1)}, bf16[168,3072]{1,0:T(8,128)(2,1)}, u32[]{:S(2)}, u32[]{:S(2)}) collective-permute-start(bf16[168,3072]{1,0:T(8,128)(2,1)} %bitcast.9), channel_id=1, source_target_pairs={{1,16},{16,1},{33,48},{48,33},{3,18},{18,3},{35,50},{50,35},{5,20}... | collective-permute-start | bytes 3096584 | tf_op jit(solution)/shard_map/ppermute | solution.py:142
  51.2 2.6 %copy.61 = bf16[1,3072,168]{2,1,0:T(8,128)(2,1)} copy(bf16[1,3072,168]{1,2,0:T(8,128)(2,1)} %param.16) | data formatting | bytes 2064384 | tf_op args[6]
  53.8 3.8 %collective-permute-done = bf16[3072,168]{0,1:T(8,128)(2,1)} collective-permute-done((bf16[3072,168]{0,1:T(8,128)(2,1)S(1)}, bf16[3072,168]{0,1:T(8,128)(2,1)}, u32[]{:S(2)}, u32[]{:S(2)}) %collective-permute-start) | collective-permute-done | bytes 1032224 | tf_op jit(solution)/shard_map/ppermute | solution.py:142
  57.7 2.5 %copy.60 = bf16[3072,168]{1,0:T(8,128)(2,1)} copy(bf16[3072,168]{0,1:T(8,128)(2,1)} %collective-permute-done) | data formatting | bytes 2064384 | tf_op jit(solution)/shard_map/ppermute | solution.py:142
  60.2 1.6 bitcast_select_fusion.1.refs_0_
  63.2 1.9 collective-permute-start.3
  65.1 3.6 %collective-permute-done.1 = bf16[3072,168]{0,1:T(8,128)(2,1)} collective-permute-done((bf16[3072,168]{0,1:T(8,128)(2,1)}, bf16[3072,168]{0,1:T(8,128)(2,1)}, u32[]{:S(2)}, u32[]{:S(2)}) %collective-permute-start.1) | collective-permute-done | bytes 1032224 | tf_op jit(solution)/shard_map/ppermute | solution.py:142
  68.7 2.5 %copy.63 = bf16[3072,168]{1,0:T(8,128)(2,1)} copy(bf16[3072,168]{0,1:T(8,128)(2,1)} %collective-permute-done.1) | data formatting | bytes 2064384 | tf_op jit(solution)/shard_map/ppermute | solution.py:142
  71.2 2.1 %bitcast_select_fusion.refs_1_ = bf16[3072,168]{1,0:T(8,128)(2,1)S(1)} fusion(bf16[3072,168]{1,0:T(8,128)(2,1)} %copy.63, bf16[1,3072,168]{2,1,0:T(8,128)(2,1)} %copy.61, pred[]{:T(512)S(6)} %eq.92), kind=kLoop, calls=%fused_computation.7 | loop fusion | flops 516096 | bytes 3096577 | tf_op jit(solution)/shard_map/jit(_where)/select_n | solution.py:143
  74.8 1.9 collective-permute-start.4
  76.7 3.1 %collective-permute-done.2 = bf16[168,3072]{1,0:T(8,128)(2,1)} collective-permute-done((bf16[168,3072]{1,0:T(8,128)(2,1)}, bf16[168,3072]{1,0:T(8,128)(2,1)}, u32[]{:S(2)}, u32[]{:S(2)}) %collective-permute-start.2) | collective-permute-done | bytes 1032224 | tf_op jit(solution)/shard_map/ppermute | solution.py:142
  79.8 2.7 %broadcast_select_fusion.refs_2_ = bf16[168,3072]{1,0:T(8,128)(2,1)} fusion(bf16[168,3072]{1,0:T(8,128)(2,1)} %collective-permute-done.2, pred[]{:T(512)S(6)} %eq.92, bf16[1,168,3072]{2,1,0:T(8,128)(2,1)} %param.17), kind=kLoop, calls=%fused_computation.12 | loop fusion | flops 516096 | bytes 3096577 | tf_op jit(solution)/shard_map/jit(_where)/select_n | solution.py:143
  82.4 1.9 collective-permute-start.5
  85.2 2.5 %copy.67.refs_3_ = bf16[3072,168]{1,0:T(8,128)(2,1)} copy(bf16[3072,168]{0,1:T(8,128)(2,1)} %collective-permute-done.3) | data formatting | bytes 2064384 | tf_op jit(solution)/shard_map/ppermute | solution.py:144
  87.7 2.5 %copy.68.refs_4_ = bf16[3072,168]{1,0:T(8,128)(2,1)} copy(bf16[3072,168]{0,1:T(8,128)(2,1)} %collective-permute-done.4) | data formatting | bytes 2064384 | tf_op jit(solution)/shard_map/ppermute | solution.py:144
  93.0 1.9 copy-done.4
  94.9 16.8 %shard_map.82 = bf16[8,8,40,384]{3,2,1,0:T(8,128)(2,1)S(1)} custom-call(bf16[8,272,768]{2,1,0:T(8,128)(2,1)S(1)} %copy-done.4, f32[272,1]{1,0:T(8,128)S(1)} %reshape.145.gate_ref, bf16[3072,168]{1,0:T(8,128)(2,1)S(1)} %bitcast_select_fusion.1.refs_0_, bf16[3072,168]{1,0:T(8,128)(2,1)S(1)} %bitcast_select_fusion.refs_1_, ...), custom_call_target="tpu_custom_call" | custom-call | flops 3369074688 | bytes 11206656 | tf_op jit(solution)/shard_map/pallas_call | solution.py:105
  113.0 7.8 %all-to-all-start.1 = ((bf16[64,40,384]{2,1,0:T(8,128)(2,1)}), bf16[64,40,384]{2,1,0:T(8,128)(2,1)S(1)}, u32[]{:S(2)}, u32[]{:S(2)}) async-start(bf16[64,40,384]{2,1,0:T(8,128)(2,1)} %bitcast.67), calls=%async_computation.1 | async-start | bytes 3932160 | tf_op jit(solution)/shard_map/all_to_all | solution.py:169
  121.5 45.8 %all-to-all-done.1 = bf16[64,40,384]{2,1,0:T(8,128)(2,1)S(1)} async-done(((bf16[64,40,384]{2,1,0:T(8,128)(2,1)}), bf16[64,40,384]{2,1,0:T(8,128)(2,1)S(1)}, u32[]{:S(2)}, u32[]{:S(2)}) %all-to-all-start.1) | async-done | bytes 1966112 | tf_op jit(solution)/shard_map/all_to_all | solution.py:169
  169.9 12.5 %all-to-all-start.2 = ((f32[32,4,512]{2,1,0:T(4,128)}), f32[32,4,512]{2,1,0:T(4,128)S(1)}, u32[]{:S(2)}, u32[]{:S(2)}) async-start(f32[32,4,512]{2,1,0:T(4,128)} %reshape.142), calls=%async_computation.2 | async-start | bytes 524288 | tf_op jit(solution)/shard_map/all_to_all | solution.py:185
  182.5 10.3 %all-to-all-done.2 = f32[32,4,512]{2,1,0:T(4,128)S(1)} async-done(((f32[32,4,512]{2,1,0:T(4,128)}), f32[32,4,512]{2,1,0:T(4,128)S(1)}, u32[]{:S(2)}, u32[]{:S(2)}) %all-to-all-start.2) | async-done | bytes 262176 | tf_op jit(solution)/shard_map/all_to_all | solution.py:185
  (81 shorter events, 21.8 us)
Async XLA Ops:
  6.5 3.8 %copy-start = (bf16[3072,16]{0,1:T(8,128)(2,1)S(1)}, bf16[3072,16]{0,1:T(8,128)(2,1)}, u32[]{:S(2)}) copy-start(bf16[3072,16]{0,1:T(8,128)(2,1)} %param.13) | copy-start | bytes 294916
  6.5 83.6 %all-gather.2.cloned.1.call-start = ((), (), s32[]{:S(2)}) async-start(), calls=%async_computation.3 | async-start | bytes 3760128 | tf_op jit(solution)/shard_map/all_gather | solution.py:163
  7.5 3.1 %copy-start.7 = (s32[128,4]{0,1:T(4,128)S(1)}, s32[128,4]{0,1:T(4,128)}, u32[]{:S(2)}) copy-start(s32[128,4]{0,1:T(4,128)} %param.14) | copy-start | bytes 6148
  12.3 27.3 %copy-start.6 = (bf16[1,3072,168]{1,2,0:T(8,128)(2,1)S(1)}, bf16[1,3072,168]{1,2,0:T(8,128)(2,1)}, u32[]{:S(2)}) copy-start(bf16[1,3072,168]{1,2,0:T(8,128)(2,1)} %param.15) | copy-start | bytes 3096580
  38.6 12.6 %copy-start.5 = (bf16[8,40,768]{2,1,0:T(8,128)(2,1)}, bf16[8,40,768]{2,1,0:T(8,128)(2,1)S(1)}, u32[]{:S(2)}) copy-start(bf16[8,40,768]{2,1,0:T(8,128)(2,1)S(1)} %all_to_all.15) | copy-start | bytes 1474564
  39.6 18.1 %collective-permute-start = (bf16[3072,168]{0,1:T(8,128)(2,1)S(1)}, bf16[3072,168]{0,1:T(8,128)(2,1)}, u32[]{:S(2)}, u32[]{:S(2)}) collective-permute-start(bf16[3072,168]{0,1:T(8,128)(2,1)S(1)} %bitcast.72), channel_id=1, source_target_pairs={{1,16},{16,1},{33,48},{48,33},{3,18},{18,3},{35,50},{50,35},{5,20}... | collective-permute-start | bytes 3096584 | tf_op jit(solution)/shard_map/ppermute | solution.py:142
  45.0 23.8 %collective-permute-start.1 = (bf16[3072,168]{0,1:T(8,128)(2,1)}, bf16[3072,168]{0,1:T(8,128)(2,1)}, u32[]{:S(2)}, u32[]{:S(2)}) collective-permute-start(bf16[3072,168]{0,1:T(8,128)(2,1)} %bitcast.8), channel_id=1, source_target_pairs={{1,16},{16,1},{33,48},{48,33},{3,18},{18,3},{35,50},{50,35},{5,20}... | collective-permute-start | bytes 3096584 | tf_op jit(solution)/shard_map/ppermute | solution.py:142
  46.9 32.9 %collective-permute-start.2 = (bf16[168,3072]{1,0:T(8,128)(2,1)}, bf16[168,3072]{1,0:T(8,128)(2,1)}, u32[]{:S(2)}, u32[]{:S(2)}) collective-permute-start(bf16[168,3072]{1,0:T(8,128)(2,1)} %bitcast.9), channel_id=1, source_target_pairs={{1,16},{16,1},{33,48},{48,33},{3,18},{18,3},{35,50},{50,35},{5,20}... | collective-permute-start | bytes 3096584 | tf_op jit(solution)/shard_map/ppermute | solution.py:142
  63.2 22.0 %collective-permute-start.3 = (bf16[3072,168]{0,1:T(8,128)(2,1)}, bf16[3072,168]{0,1:T(8,128)(2,1)}, u32[]{:S(2)}, u32[]{:S(2)}) collective-permute-start(bf16[3072,168]{0,1:T(8,128)(2,1)} %copy.64), channel_id=1, source_target_pairs={{0,1},{1,0},{2,3},{3,2},{4,5},{5,4},{6,7},{7,6},{8,9},{9,8},{10,11... | collective-permute-start | bytes 3096584 | tf_op jit(solution)/shard_map/ppermute | solution.py:144
  74.8 12.9 %collective-permute-start.4 = (bf16[3072,168]{0,1:T(8,128)(2,1)}, bf16[3072,168]{0,1:T(8,128)(2,1)}, u32[]{:S(2)}, u32[]{:S(2)}) collective-permute-start(bf16[3072,168]{0,1:T(8,128)(2,1)} %copy.65), channel_id=1, source_target_pairs={{0,1},{1,0},{2,3},{3,2},{4,5},{5,4},{6,7},{7,6},{8,9},{9,8},{10,11... | collective-permute-start | bytes 3096584 | tf_op jit(solution)/shard_map/ppermute | solution.py:144
  82.4 7.7 %collective-permute-start.5 = (bf16[168,3072]{1,0:T(8,128)(2,1)}, bf16[168,3072]{1,0:T(8,128)(2,1)}, u32[]{:S(2)}, u32[]{:S(2)}) collective-permute-start(bf16[168,3072]{1,0:T(8,128)(2,1)} %broadcast_select_fusion.refs_2_), channel_id=1, source_target_pairs={{0,1},{1,0},{2,3},{3,2},{4,5},{5,4},{6,7},{7,6},{8,9},{9,8},{10,11... | collective-permute-start | bytes 3096584 | tf_op jit(solution)/shard_map/ppermute | solution.py:144
  90.2 1.4 copy-start.2
  91.6 1.4 copy-start.3
  93.0 1.9 copy-start.4
  111.8 1.3 copy-start.1
  113.0 54.3 %all-to-all-start.1 = ((bf16[64,40,384]{2,1,0:T(8,128)(2,1)}), bf16[64,40,384]{2,1,0:T(8,128)(2,1)S(1)}, u32[]{:S(2)}, u32[]{:S(2)}) async-start(bf16[64,40,384]{2,1,0:T(8,128)(2,1)} %bitcast.67), calls=%async_computation.1 | async-start | bytes 3932160 | tf_op jit(solution)/shard_map/all_to_all | solution.py:169
  169.1 24.2 %copy-start.8 = (f32[3072]{0:T(1024)S(1)}, f32[3072]{0:T(1024)}, u32[]{:S(2)}) copy-start(f32[3072]{0:T(1024)} %param.12) | copy-start | bytes 36868
  169.9 22.9 %all-to-all-start.2 = ((f32[32,4,512]{2,1,0:T(4,128)}), f32[32,4,512]{2,1,0:T(4,128)S(1)}, u32[]{:S(2)}, u32[]{:S(2)}) async-start(f32[32,4,512]{2,1,0:T(4,128)} %reshape.142), calls=%async_computation.2 | async-start | bytes 524288 | tf_op jit(solution)/shard_map/all_to_all | solution.py:185
Sparse Core Ops, SparseCore 0:
  39.7 47.0 all-gather.1

commit v3 on v1

v3 whole, which is shorter than its diff:
```python
import functools
import jax
import jax.numpy as jnp
from jax import lax
from jax.experimental import pallas as pl
from jax.experimental.pallas import tpu as pltpu
from jax.sharding import Mesh, PartitionSpec as P

eps = 1e-05
X = 4
CORES = 2
LANE = 128
bf16 = jnp.bfloat16
f32 = jnp.float32


def token_weights(acts, gain, router, ids):
    wide = acts.astype(f32)
    recip = lax.rsqrt(jnp.mean(wide * wide, axis=-1, keepdims=True) + eps)
    h = (wide * recip * gain).astype(bf16)
    logits = jnp.dot(h, router, preferred_element_type=f32)
    experts = router.shape[1]
    select = (ids[:, :, None] == jnp.arange(experts, dtype=jnp.int32)[None, None, :]).astype(f32)
    picked = jnp.sum(select * logits[:, None, :], axis=-1)
    sig = jax.nn.sigmoid(picked)
    total = jnp.sum(sig, axis=1, keepdims=True)
    return h, sig, total, sig / total, select


def places(ids, names):
    tokens = ids.shape[0]
    member = jnp.any(ids[:, :, None] == names[None, None, :], axis=1)
    below = (jnp.arange(tokens)[:, None] > jnp.arange(tokens)[None, :]).astype(bf16)
    place = jnp.dot(below, member.astype(bf16), preferred_element_type=f32).astype(jnp.int32)
    return jnp.where(member, place, -4096).T


def at_rows(place, count):
    return place[:, None, :] == jnp.arange(count, dtype=jnp.int32)[None, :, None]


def expert_kernel(cap, nz, info, rows_hbm, mine, far, left, right, keep_ref, give_ref, *scratch):
    h_ref, g_ref, w_ref, row_sem, w_sem = scratch
    ny, groups, count = rows_hbm.shape[0], rows_hbm.shape[1], rows_hbm.shape[2]
    part = rows_hbm.shape[3] // 2
    rank, lane = keep_ref.shape[2], keep_ref.shape[3]
    pieces = part // lane
    contract = (((1,), (1,)), ((), ()))
    own, core = info[0], info[1]

    def fetch(u, source):
        return pltpu.make_async_copy(source, w_ref.at[u], w_sem.at[u])

    @pl.when(own == 1)
    def _():
        fetch(0, mine).start()

    @pl.when(own == 0)
    def _():
        fetch(0, left).start()

    row_copies = []
    for j, ref in enumerate((h_ref, g_ref)):
        for i in range(ny):
            for k in range(groups):
                from_core = core if k == 0 else 1 - core
                row_copies.append(
                    pltpu.make_async_copy(
                        rows_hbm.at[i, from_core, :, pl.ds(j * part, part)],
                        ref.at[pl.ds(k * count, count), pl.ds(i * part, part)],
                        row_sem.at[j, i, k],
                    )
                )
    for copy in row_copies:
        copy.start()

    @pl.when(own == 1)
    def _():
        fetch(1, far).start()

    @pl.when(own == 0)
    def _():
        fetch(1, right).start()

    for copy in row_copies:
        copy.wait()
    score = 0.0
    pulls = []
    for u in range(2):
        fetch(u, mine).wait()
        a = lax.dot_general(h_ref[...], w_ref[u, 0], contract, preferred_element_type=f32)
        b = lax.dot_general(h_ref[...], w_ref[u, 1], contract, preferred_element_type=f32)
        dact = lax.dot_general(g_ref[...], w_ref[u, 2], contract, preferred_element_type=f32)
        sg = jax.nn.sigmoid(a)
        sa = a * sg
        act = (sa * b).astype(bf16).astype(f32)
        score = score + jnp.sum(act * dact, axis=1, keepdims=True)
        pulls.append((dact * b * sg * (1.0 + a * (1.0 - sg))).astype(bf16))
        pulls.append((dact * sa).astype(bf16))
    lanes = lax.broadcasted_iota(jnp.int32, (cap, lane), 1)
    eye = lanes == lax.broadcasted_iota(jnp.int32, (cap, lane), 0)
    gap = jnp.zeros((2, lane), f32)
    rest = jnp.zeros((rank - pieces * cap - 4, lane), f32)
    tails = []
    for k in range(groups):
        for z in range(nz):
            first = k * count + z * cap
            line = jnp.sum(jnp.where(eye, score[first : first + cap], 0.0), axis=0, keepdims=True)
            high = line.astype(bf16).astype(f32)
            pair = [high, line - high]
            tails.append(pair + [gap, rest] if k == 0 else [gap] + pair + [rest])
    for i in range(ny):
        band = pl.ds(i * part, part)
        dh = 0.0
        for u in range(2):
            for j in range(2):
                dh = dh + jnp.dot(pulls[2 * u + j], w_ref[u, j, :, band], preferred_element_type=f32)
        for k, ref in enumerate((keep_ref, give_ref)):
            for z in range(nz):
                first = k * count + z * cap
                block = dh[first : first + cap]
                block = [block[:, p * lane : (p + 1) * lane] for p in range(pieces)]
                block = jnp.concatenate(block + tails[k * nz + z], axis=0)
                ref[i, z] = block.astype(ref.dtype)


def expert_rows(info, gathered, slices, nz, cap, rank):
    ny, groups, count, wide = gathered.shape
    kinds, hidden, width = slices[0].shape
    hbm = pl.BlockSpec(memory_space=pl.ANY)
    vmem = pl.BlockSpec(memory_space=pltpu.VMEM)
    rows = groups * count
    return pl.pallas_call(
        functools.partial(expert_kernel, cap, nz),
        out_shape=(
            jax.ShapeDtypeStruct((ny, nz, rank, LANE), f32),
            jax.ShapeDtypeStruct((ny, nz, rank, LANE), bf16),
        ),
        in_specs=[pl.BlockSpec(memory_space=pltpu.SMEM)] + [hbm] * 5,
        out_specs=(vmem, vmem),
        scratch_shapes=[
            pltpu.VMEM((rows, width), bf16),
            pltpu.VMEM((rows, width), bf16),
            pltpu.VMEM((2, kinds, hidden, width), bf16),
            pltpu.SemaphoreType.DMA((2, ny, groups)),
            pltpu.SemaphoreType.DMA((2,)),
        ],
        compiler_params=pltpu.CompilerParams(vmem_limit_bytes=56 * 1024 * 1024),
        cost_estimate=pl.CostEstimate(
            flops=20 * rows * width * hidden,
            bytes_accessed=2 * (2 * rows * width + 6 * width * hidden + 2 * rows * width),
            transcendentals=2 * rows * hidden,
        ),
    )(info, gathered, *slices)


def shards(acts, cotangent, gain, router, ids, w_gate, w_up, w_down):
    ny, nx, nz, nc = (lax.axis_size(n) for n in ("y", "x", "z", "core"))
    y, x, core = (lax.axis_index(n) for n in ("y", "x", "core"))
    tokens, width = acts.shape
    top = ids.shape[1]
    experts = nz * nc
    cap = min(tokens, (17 * tokens * top + 16 * experts - 1) // (16 * experts))
    cap = -(-cap // 2)
    part = width // ny
    parity = x % 2

    mine = jnp.stack([w_gate[0].T, w_up[0].T, w_down[0]])
    ahead, behind, across = [], [], []
    for i in range(nx):
        a = i % 2
        ahead.append((i * nc + 1 - a, (i + 1) % nx * nc + a))
        behind.append((i * nc + 1 - a, (i - 1) % nx * nc + a))
        across.append((i * nc + a, (i + 2) % nx * nc + a))
    left = lax.ppermute(mine, ("x", "core"), behind)
    right = lax.ppermute(mine, ("x", "core"), ahead)
    info = jnp.stack([(core == parity).astype(jnp.int32), core.astype(jnp.int32)])

    h, sig, total, weight, select = token_weights(acts, gain, router, ids)
    names = 2 * jnp.arange(nz, dtype=jnp.int32) + parity
    place = places(ids, names) - x // 2 * cap
    place = jnp.where((place >= 0) & (place < cap), place, -4096)
    here = at_rows(place, cap)
    of_name = (ids[:, :, None] == names[None, None, :]).astype(f32)
    dense = jnp.sum(of_name * weight[:, :, None], axis=1).astype(bf16)
    h_part = lax.dynamic_slice_in_dim(h, y * part, part, 1)
    g_part = lax.dynamic_slice_in_dim(cotangent, y * part, part, 1)
    rank = -(-cap // 8) * 8
    pick = at_rows(place, rank).astype(bf16)
    scaled = pick * dense.T[:, None, :]
    h_rows = jnp.dot(pick.reshape(nz * rank, tokens), h_part, preferred_element_type=f32)
    dy_rows = jnp.dot(scaled.reshape(nz * rank, tokens), g_part, preferred_element_type=f32)
    rows = jnp.concatenate([h_rows.astype(bf16), dy_rows.astype(bf16)], axis=1)
    rows = lax.all_to_all(rows.reshape(nz, rank, 2 * part), "z", 0, 0, tiled=True)
    count = -(-nz * cap // 16) * 16
    rows = rows[:, :cap].reshape(nz * cap, 2 * part)
    rows = jnp.pad(rows, ((0, count - nz * cap), (0, 0)))
    gathered = lax.all_gather(rows, ("y", "core"), tiled=True)
    left, right, source, _ = lax.optimization_barrier((left, right, mine, rows))
    far = lax.ppermute(source, ("x", "core"), across)

    pieces = part // LANE
    rank = -(-(pieces * cap + 4) // 8) * 8
    keep, give = expert_rows(
        info, gathered.reshape(ny, nc, count, 2 * part), (mine, far, left, right), nz, cap, rank
    )
    got = lax.ppermute(give, "core", [(0, 1), (1, 0)])
    back = (keep + got.astype(f32)).astype(bf16)

    back = lax.all_to_all(back.reshape(ny * nz, rank, LANE), ("y", "z"), 0, 0, tiled=True)
    flat = back.reshape(ny * nz * rank, LANE)
    parts = []
    for k in range(pieces):
        spread = at_rows(place + k * cap, rank).astype(bf16)
        spread = jnp.broadcast_to(spread[None], (ny, nz, rank, tokens))
        parts.append(
            lax.dot_general(
                spread.reshape(ny * nz * rank, tokens),
                flat,
                (((0,), (0,)), ((), ())),
                preferred_element_type=f32,
            )
        )
    score = jnp.sum(back[:, pieces * cap : pieces * cap + 4, :cap].astype(f32), axis=1)
    score = score.reshape(ny, nz, cap).sum(axis=0)
    score = jnp.sum(here.astype(f32) * score[:, :, None], axis=1)
    score = jnp.sum(of_name * score.T[:, None, :], axis=-1)
    sections = ny * nx
    share = tokens // sections
    tail = jnp.zeros((tokens, LANE), f32).at[:, :top].set(score)
    packet = jnp.concatenate(parts + [tail], axis=1).reshape(sections, share, part + LANE)
    packet = lax.all_to_all(packet, ("y", "x"), 0, 0, tiled=True)
    packet = packet.reshape(ny, nx, share, part + LANE).sum(axis=1)
    dh_share = jnp.concatenate([packet[i, :, :part] for i in range(ny)], axis=1)
    score_share = packet[0, :, part : part + top]

    start = (y * nx + x) * share
    cut = lambda v: lax.dynamic_slice_in_dim(v, start, share, 0)
    sig, total, weight, select = cut(sig), cut(total), cut(weight), cut(select)
    wide = cut(acts).astype(f32)
    g = cut(cotangent).astype(f32)
    sent = weight.astype(bf16).astype(f32)
    score_share = jnp.where(sent > 0.0, score_share / jnp.where(sent > 0.0, sent, 1.0), 0.0)
    dsig = (score_share - jnp.sum(weight * score_share, axis=1, keepdims=True)) / total
    dpick = dsig * sig * (1.0 - sig)
    dlogits = jnp.sum(dpick[:, :, None] * select, axis=1)
    dh_total = dh_share + lax.dot_general(
        dlogits, router.astype(f32), (((1,), (1,)), ((), ())), precision=lax.Precision.HIGHEST
    )
    recip = lax.rsqrt(jnp.mean(wide * wide, axis=-1, keepdims=True) + eps)
    scaled = dh_total * gain
    pulled = recip * scaled - wide * (recip * recip * recip) * jnp.mean(
        wide * scaled, axis=-1, keepdims=True
    )
    return (g + pulled)[None]


def solution(mesh):
    pipe, expert = mesh.devices.shape
    grid = Mesh(
        mesh.devices.reshape(pipe // X, X, expert // CORES, CORES), ("y", "x", "z", "core")
    )
    exp, pipe = ("z", "core"), ("y", "x")
    in_specs = (
        P(exp, None),
        P(exp, None),
        P(),
        P(),
        P(exp, None),
        P(exp, None, pipe),
        P(exp, None, pipe),
        P(exp, pipe, None),
    )
    return jax.shard_map(
        shards, mesh=grid, in_specs=in_specs, out_specs=P(pipe, exp, None), check_vma=False
    )
```

time: 221 us -> 204 us (0.923)
  the two profiles are of different devices: /device:TPU:8 before, /device:TPU:1 now
where the time goes in v3:
time: 204 us; the launch traced here: 202 us
  waiting for transfers between devices  108 us (53%)
  starting transfers between devices  26.8 us (13%)
  blocking collectives  21.5 us (11%)
  between operations  13.7 us (7%)
  other arithmetic  12.2 us (6%)
  Pallas kernels  12 us (6%)
  matrix products  4.27 us (2%)
  local copies, waits for them, and re-layouts  4.13 us (2%)
    ppermute x1, waiting for transfers between devices, shards(): left = lax.ppermute(mine, ('x', 'core'), behind)  64.9 us
    all_to_all x1, waiting for transfers between devices, shards(): lax.all_to_all(back.reshape(ny * nz, rank, LANE), ('y', 'z'), 0, 0, tiled...  24.2 us
    all_to_all x1, blocking collectives, shards(): lax.all_to_all(rows.reshape(nz, rank, 2 * part), 'z', 0, 0, tiled=True)  21.5 us
    pallas_call x1, Pallas kernels, expert_rows(): pl.pallas_call(functools.partial(expert_kernel, cap, nz), out_shape=(jax....  12 us
    all_to_all x1, waiting for transfers between devices, shards(): packet = lax.all_to_all(packet, ('y', 'x'), 0, 0, tiled=True)  10.3 us
    all_to_all x1, starting transfers between devices, shards(): lax.all_to_all(back.reshape(ny * nz, rank, LANE), ('y', 'z'), 0, 0, tiled...  7.84 us
    ppermute x1, starting transfers between devices, shards(): left = lax.ppermute(mine, ('x', 'core'), behind)  6.97 us
    all_to_all x1, starting transfers between devices, shards(): packet = lax.all_to_all(packet, ('y', 'x'), 0, 0, tiled=True)  5.81 us
  transfers between devices with their start and end apart: 7, of which 5 were waited for; matrix products, arithmetic and copies ran while one was open for 2% of the time, Pallas kernels for 0%

profile of v3, /device:TPU:1, one launch (start us, length us, event | category | flops | bytes accessed | tf_op | source)
XLA Modules:
  0.0 202.3 jit_solution(8704174604305876975)
XLA Ops:
  6.5 1.4 fusion.1
  8.0 1.4 fusion.3
  10.6 1.1 convolution_convert_fusion
  11.7 21.5 %all_to_all.15 = bf16[8,24,768]{2,1,0:T(8,128)(2,1)S(1)} all-to-all(bf16[8,24,768]{2,1,0:T(8,128)(2,1)S(1)} %bitcast.94), channel_id=1, replica_groups=mesh['y'=8,'x'=4,'z'=8,'core'=2] {'z'}, dimensions={0} | all-to-all | bytes 589824 | tf_op jit(solution)/shard_map/all_to_all | solution.py:194
  33.3 0.7 pad.7
  34.0 2.2 %pad_maximum_fusion.mine = bf16[3,168,3072]{2,1,0:T(8,128)(2,1)S(1)} fusion(bf16[1,168,3072]{2,1,0:T(8,128)(2,1)} %param.17, bf16[1,168,3072]{2,1,0:T(8,128)(2,1)} %bitcast.96, bf16[1,168,3072]{2,1,0:T(8,128)(2,1)} %bitcast.97), kind=kLoop, calls=%fused_computation.2 | loop fusion | flops 3096576 | bytes 6193152 | tf_op jit(solution)/shard_map/stack | solution.py:168
  36.2 7.0 %collective-permute-start = (bf16[3,168,3072]{2,1,0:T(8,128)(2,1)S(1)}, bf16[3,168,3072]{2,1,0:T(8,128)(2,1)S(1)}, u32[]{:S(2)}, u32[]{:S(2)}) collective-permute-start(bf16[3,168,3072]{2,1,0:T(8,128)(2,1)S(1)} %pad_maximum_fusion.mine), channel_id=1, source_target_pairs={{1,48},{16,1},{33,16},{48,33},{3,50},{18,3},{35,18},{50,35},{5,52}... | collective-permute-start | bytes 9289736 | tf_op jit(solution)/shard_map/ppermute | solution.py:175
  43.2 1.9 collective-permute-start.1
  45.1 64.9 %collective-permute-done.left = bf16[3,168,3072]{2,1,0:T(8,128)(2,1)S(1)} collective-permute-done((bf16[3,168,3072]{2,1,0:T(8,128)(2,1)S(1)}, bf16[3,168,3072]{2,1,0:T(8,128)(2,1)S(1)}, u32[]{:S(2)}, u32[]{:S(2)}) %collective-permute-start) | collective-permute-done | bytes 3096608 | tf_op jit(solution)/shard_map/ppermute | solution.py:175
  110.0 5.6 %collective-permute-done.1.right = bf16[3,168,3072]{2,1,0:T(8,128)(2,1)S(1)} collective-permute-done((bf16[3,168,3072]{2,1,0:T(8,128)(2,1)S(1)}, bf16[3,168,3072]{2,1,0:T(8,128)(2,1)S(1)}, u32[]{:S(2)}, u32[]{:S(2)}) %collective-permute-start.1) | collective-permute-done | bytes 3096608 | tf_op jit(solution)/shard_map/ppermute | solution.py:176
  115.7 1.6 copy-done.3
  117.3 2.3 %collective-permute-start.2 = (bf16[3,168,3072]{2,1,0:T(8,128)(2,1)S(1)}, bf16[3,168,3072]{2,1,0:T(8,128)(2,1)}, u32[]{:S(2)}, u32[]{:S(2)}) collective-permute-start(bf16[3,168,3072]{2,1,0:T(8,128)(2,1)S(1)} %pad_maximum_fusion.mine), channel_id=1, source_target_pairs={{0,32},{17,49},{32,0},{49,17},{2,34},{19,51},{34,2},{51,19},{4,36}... | collective-permute-start | bytes 9289736 | tf_op jit(solution)/shard_map/ppermute | solution.py:200
  120.2 12.0 %shard_map.82 = (f32[8,8,56,128]{3,2,1,0:T(8,128)}, bf16[8,8,56,128]{3,2,1,0:T(8,128)(2,1)}) custom-call(s32[2]{0:T(128)} %pad_add_fusion.info, bf16[8,2,144,768]{3,2,1,0:T(8,128)(2,1)} %bitcast.93, bf16[3,168,3072]{2,1,0:T(8,128)(2,1)} %copy-done.1, bf16[3,168,3072]{2,1,0:T(8,128)(2,1)} %collective-permute-done.2.far, bf16[3,168,3072]{2,1,0:T(8,128)(2,1)} %copy-done.2, ...), custom_call_target="tpu_custom_call" | custom-call | flops 2972712960 | bytes 13271040 | tf_op jit(solution)/shard_map/pallas_call | solution.py:133
  132.2 1.9 collective-permute-start.3
  134.1 2.6 %collective-permute-done.3 = bf16[8,8,56,128]{3,2,1,0:T(8,128)(2,1)S(1)} collective-permute-done((bf16[8,8,56,128]{3,2,1,0:T(8,128)(2,1)}, bf16[8,8,56,128]{3,2,1,0:T(8,128)(2,1)S(1)}, u32[]{:S(2)}, u32[]{:S(2)}) %collective-permute-start.3) | collective-permute-done | bytes 917536 | tf_op jit(solution)/shard_map/ppermute | solution.py:207
  136.8 2.7 %add_convert_fusion = bf16[8,8,56,128]{3,2,1,0:T(8,128)(2,1)} fusion(f32[8,8,56,128]{3,2,1,0:T(8,128)} %get-tuple-element.25, bf16[8,8,56,128]{3,2,1,0:T(8,128)(2,1)S(1)} %collective-permute-done.3), kind=kLoop, calls=%fused_computation.5 | loop fusion | flops 1376256 | bytes 3670016 | tf_op jit(solution)/shard_map/convert_element_type | solution.py:208
  139.5 7.8 %all-to-all-start.1 = ((bf16[64,56,128]{2,1,0:T(8,128)(2,1)}), bf16[64,56,128]{2,1,0:T(8,128)(2,1)S(1)}, u32[]{:S(2)}, u32[]{:S(2)}) async-start(bf16[64,56,128]{2,1,0:T(8,128)(2,1)} %bitcast.15), calls=%async_computation.1 | async-start | bytes 1835008 | tf_op jit(solution)/shard_map/all_to_all | solution.py:210
  148.0 24.2 %all-to-all-done.1 = bf16[64,56,128]{2,1,0:T(8,128)(2,1)S(1)} async-done(((bf16[64,56,128]{2,1,0:T(8,128)(2,1)}), bf16[64,56,128]{2,1,0:T(8,128)(2,1)S(1)}, u32[]{:S(2)}, u32[]{:S(2)}) %all-to-all-start.1) | async-done | bytes 917536 | tf_op jit(solution)/shard_map/all_to_all | solution.py:210
  174.4 0.7 broadcast_select_fusion
  175.2 0.8 reshape.153
  176.0 5.8 %all-to-all-start.2 = ((f32[32,4,512]{2,1,0:T(4,128)}), f32[32,4,512]{2,1,0:T(4,128)S(1)}, u32[]{:S(2)}, u32[]{:S(2)}) async-start(f32[32,4,512]{2,1,0:T(4,128)} %reshape.153), calls=%async_computation.2 | async-start | bytes 524288 | tf_op jit(solution)/shard_map/all_to_all | solution.py:232
  181.9 10.3 %all-to-all-done.2 = f32[32,4,512]{2,1,0:T(4,128)S(1)} async-done(((f32[32,4,512]{2,1,0:T(4,128)}), f32[32,4,512]{2,1,0:T(4,128)S(1)}, u32[]{:S(2)}, u32[]{:S(2)}) %all-to-all-start.2) | async-done | bytes 262176 | tf_op jit(solution)/shard_map/all_to_all | solution.py:232
  192.7 1.2 fusion.11
  194.0 1.5 fusion.15
  (66 shorter events, 5.4 us)
Async XLA Ops:
  6.5 2.8 %copy-start = (bf16[3072,16]{0,1:T(8,128)(2,1)S(1)}, bf16[3072,16]{0,1:T(8,128)(2,1)}, u32[]{:S(2)}) copy-start(bf16[3072,16]{0,1:T(8,128)(2,1)} %param.13) | copy-start | bytes 294916
  6.5 3.1 %copy-start.4 = (s32[128,4]{0,1:T(4,128)S(1)}, s32[128,4]{0,1:T(4,128)}, u32[]{:S(2)}) copy-start(s32[128,4]{0,1:T(4,128)} %param.14) | copy-start | bytes 6148
  6.5 113.6 %all-gather.2.cloned.1.call-start = ((), (), s32[]{:S(2)}) async-start(), calls=%async_computation.3 | async-start | bytes 3760128 | tf_op jit(solution)/shard_map/all_gather | solution.py:198
  36.2 84.0 %copy-start.1 = (bf16[3,168,3072]{2,1,0:T(8,128)(2,1)}, bf16[3,168,3072]{2,1,0:T(8,128)(2,1)S(1)}, u32[]{:S(2)}) copy-start(bf16[3,168,3072]{2,1,0:T(8,128)(2,1)S(1)} %pad_maximum_fusion.mine) | copy-start | bytes 9289732
  36.2 73.8 %collective-permute-start = (bf16[3,168,3072]{2,1,0:T(8,128)(2,1)S(1)}, bf16[3,168,3072]{2,1,0:T(8,128)(2,1)S(1)}, u32[]{:S(2)}, u32[]{:S(2)}) collective-permute-start(bf16[3,168,3072]{2,1,0:T(8,128)(2,1)S(1)} %pad_maximum_fusion.mine), channel_id=1, source_target_pairs={{1,48},{16,1},{33,16},{48,33},{3,50},{18,3},{35,18},{50,35},{5,52}... | collective-permute-start | bytes 9289736 | tf_op jit(solution)/shard_map/ppermute | solution.py:175
  43.2 72.5 %collective-permute-start.1 = (bf16[3,168,3072]{2,1,0:T(8,128)(2,1)S(1)}, bf16[3,168,3072]{2,1,0:T(8,128)(2,1)S(1)}, u32[]{:S(2)}, u32[]{:S(2)}) collective-permute-start(bf16[3,168,3072]{2,1,0:T(8,128)(2,1)S(1)} %pad_maximum_fusion.mine), channel_id=1, source_target_pairs={{1,16},{16,33},{33,48},{48,1},{3,18},{18,35},{35,50},{50,3},{5,20}... | collective-permute-start | bytes 9289736 | tf_op jit(solution)/shard_map/ppermute | solution.py:176
  110.0 5.6 %copy-start.2 = (bf16[3,168,3072]{2,1,0:T(8,128)(2,1)}, bf16[3,168,3072]{2,1,0:T(8,128)(2,1)S(1)}, u32[]{:S(2)}) copy-start(bf16[3,168,3072]{2,1,0:T(8,128)(2,1)S(1)} %collective-permute-done.left) | copy-start | bytes 9289732
  115.7 1.6 copy-start.3
  117.3 2.9 %collective-permute-start.2 = (bf16[3,168,3072]{2,1,0:T(8,128)(2,1)S(1)}, bf16[3,168,3072]{2,1,0:T(8,128)(2,1)}, u32[]{:S(2)}, u32[]{:S(2)}) collective-permute-start(bf16[3,168,3072]{2,1,0:T(8,128)(2,1)S(1)} %pad_maximum_fusion.mine), channel_id=1, source_target_pairs={{0,32},{17,49},{32,0},{49,17},{2,34},{19,51},{34,2},{51,19},{4,36}... | collective-permute-start | bytes 9289736 | tf_op jit(solution)/shard_map/ppermute | solution.py:200
  132.2 4.6 %collective-permute-start.3 = (bf16[8,8,56,128]{3,2,1,0:T(8,128)(2,1)}, bf16[8,8,56,128]{3,2,1,0:T(8,128)(2,1)S(1)}, u32[]{:S(2)}, u32[]{:S(2)}) collective-permute-start(bf16[8,8,56,128]{3,2,1,0:T(8,128)(2,1)} %get-tuple-element.26), channel_id=1, source_target_pairs={{0,1},{1,0},{2,3},{3,2},{4,5},{5,4},{6,7},{7,6},{8,9},{9,8},{10,11... | collective-permute-start | bytes 2752520 | tf_op jit(solution)/shard_map/ppermute | solution.py:207
  139.5 32.8 %all-to-all-start.1 = ((bf16[64,56,128]{2,1,0:T(8,128)(2,1)}), bf16[64,56,128]{2,1,0:T(8,128)(2,1)S(1)}, u32[]{:S(2)}, u32[]{:S(2)}) async-start(bf16[64,56,128]{2,1,0:T(8,128)(2,1)} %bitcast.15), calls=%async_computation.1 | async-start | bytes 1835008 | tf_op jit(solution)/shard_map/all_to_all | solution.py:210
  173.9 18.8 %copy-start.5 = (f32[3072]{0:T(1024)S(1)}, f32[3072]{0:T(1024)}, u32[]{:S(2)}) copy-start(f32[3072]{0:T(1024)} %param.12) | copy-start | bytes 36868
  176.0 16.2 %all-to-all-start.2 = ((f32[32,4,512]{2,1,0:T(4,128)}), f32[32,4,512]{2,1,0:T(4,128)S(1)}, u32[]{:S(2)}, u32[]{:S(2)}) async-start(f32[32,4,512]{2,1,0:T(4,128)} %reshape.153), calls=%async_computation.2 | async-start | bytes 524288 | tf_op jit(solution)/shard_map/all_to_all | solution.py:232
Sparse Core Ops, SparseCore 0:
  34.1 42.5 all-gather.1

commit v4 on v3

--- a/solution.py
+++ b/solution.py
@@ -39,8 +39,9 @@
     return place[:, None, :] == jnp.arange(count, dtype=jnp.int32)[None, :, None]
 
 
-def expert_kernel(cap, nz, info, rows_hbm, mine, far, left, right, keep_ref, give_ref, *scratch):
-    h_ref, g_ref, w_ref, row_sem, w_sem = scratch
+def expert_kernel(cap, nz, info, rows_hbm, *refs):
+    slices, (left, right, keep_ref, give_ref) = refs[:6], refs[6:10]
+    h_ref, g_ref, w_ref, row_sem, w_sem = refs[10:]
     ny, groups, count = rows_hbm.shape[0], rows_hbm.shape[1], rows_hbm.shape[2]
     part = rows_hbm.shape[3] // 2
     rank, lane = keep_ref.shape[2], keep_ref.shape[3]
@@ -48,16 +49,24 @@
     contract = (((1,), (1,)), ((), ()))
     own, core = info[0], info[1]
 
-    def fetch(u, source):
-        return pltpu.make_async_copy(source, w_ref.at[u], w_sem.at[u])
-
-    @pl.when(own == 1)
-    def _():
-        fetch(0, mine).start()
-
-    @pl.when(own == 0)
-    def _():
-        fetch(0, left).start()
+    def fetch(u):
+        return [
+            pltpu.make_async_copy(slices[3 * u + j], w_ref.at[u, j], w_sem.at[u, j])
+            for j in range(3)
+        ]
+
+    def start(u, other):
+        @pl.when(own == 1)
+        def _():
+            for copy in fetch(u):
+                copy.start()
+
+        @pl.when(own == 0)
+        def _():
+            for j in range(3):
+                pltpu.make_async_copy(other.at[j], w_ref.at[u, j], w_sem.at[u, j]).start()
+
+    start(0, left)
 
     row_copies = []
     for j, ref in enumerate((h_ref, g_ref)):
@@ -73,21 +82,14 @@
                 )
     for copy in row_copies:
         copy.start()
-
-    @pl.when(own == 1)
-    def _():
-        fetch(1, far).start()
-
-    @pl.when(own == 0)
-    def _():
-        fetch(1, right).start()
-
+    start(1, right)
     for copy in row_copies:
         copy.wait()
     score = 0.0
     pulls = []
     for u in range(2):
-        fetch(u, mine).wait()
+        for copy in fetch(u):
+            copy.wait()
         a = lax.dot_general(h_ref[...], w_ref[u, 0], contract, preferred_element_type=f32)
         b = lax.dot_general(h_ref[...], w_ref[u, 1], contract, preferred_element_type=f32)
         dact = lax.dot_general(g_ref[...], w_ref[u, 2], contract, preferred_element_type=f32)
@@ -126,7 +128,7 @@
 
 def expert_rows(info, gathered, slices, nz, cap, rank):
     ny, groups, count, wide = gathered.shape
-    kinds, hidden, width = slices[0].shape
+    kinds, hidden, width = slices[-1].shape
     hbm = pl.BlockSpec(memory_space=pl.ANY)
     vmem = pl.BlockSpec(memory_space=pltpu.VMEM)
     rows = groups * count
@@ -136,14 +138,14 @@
             jax.ShapeDtypeStruct((ny, nz, rank, LANE), f32),
             jax.ShapeDtypeStruct((ny, nz, rank, LANE), bf16),
         ),
-        in_specs=[pl.BlockSpec(memory_space=pltpu.SMEM)] + [hbm] * 5,
+        in_specs=[pl.BlockSpec(memory_space=pltpu.SMEM)] + [hbm] * 9,
         out_specs=(vmem, vmem),
         scratch_shapes=[
             pltpu.VMEM((rows, width), bf16),
             pltpu.VMEM((rows, width), bf16),
             pltpu.VMEM((2, kinds, hidden, width), bf16),
             pltpu.SemaphoreType.DMA((2, ny, groups)),
-            pltpu.SemaphoreType.DMA((2,)),
+            pltpu.SemaphoreType.DMA((2, 3)),
         ],
         compiler_params=pltpu.CompilerParams(vmem_limit_bytes=56 * 1024 * 1024),
         cost_estimate=pl.CostEstimate(
@@ -165,7 +167,8 @@
     part = width // ny
     parity = x % 2
 
-    mine = jnp.stack([w_gate[0].T, w_up[0].T, w_down[0]])
+    own_slice = (w_gate[0].T, w_up[0].T, w_down[0])
+    mine = jnp.stack(own_slice)
     ahead, behind, across = [], [], []
     for i in range(nx):
         a = i % 2
@@ -197,12 +200,15 @@
     rows = jnp.pad(rows, ((0, count - nz * cap), (0, 0)))
     gathered = lax.all_gather(rows, ("y", "core"), tiled=True)
     left, right, source, _ = lax.optimization_barrier((left, right, mine, rows))
-    far = lax.ppermute(source, ("x", "core"), across)
+    far = []
+    for i in range(3):
+        far.append(lax.ppermute(source[i], ("x", "core"), across))
+        far[i], source = lax.optimization_barrier((far[i], source))
 
     pieces = part // LANE
     rank = -(-(pieces * cap + 4) // 8) * 8
     keep, give = expert_rows(
-        info, gathered.reshape(ny, nc, count, 2 * part), (mine, far, left, right), nz, cap, rank
+        info, gathered.reshape(ny, nc, count, 2 * part), (*own_slice, *far, left, right), nz, cap, rank
     )
     got = lax.ppermute(give, "core", [(0, 1), (1, 0)])
     back = (keep + got.astype(f32)).astype(bf16)

time: 204 us -> 197 us (0.966)
  waiting for transfers between devices: 108 us -> 70.5 us
  starting transfers between devices: 26.8 us -> 52.4 us
  local copies, waits for them, and re-layouts: 4.13 us -> 6.2 us
    ppermute x1, waiting for transfers between devices: 64.9 us -> 0.49 us  [shards(): left = lax.ppermute(mine, ('x', 'core'), behind)]
    all_gather x1, waiting for transfers between devices: 0.01 us -> 27.9 us  [shards(): gathered = lax.all_gather(rows, ('y', 'core'), tiled=True)]
    ppermute x1, starting transfers between devices: 1.92 us -> 18.3 us  [shards(): got = lax.ppermute(give, 'core', [(0, 1), (1, 0)])]
    all_to_all x1, starting transfers between devices: 7.84 us -> 14.6 us  [shards(): lax.all_to_all(back.reshape(ny * nz, rank, LANE), ('y', 'z'), 0, 0, tiled...]
  transfers between devices with their start and end apart: 7 -> 9, of which waited for: 5 -> 6; matrix products, arithmetic and copies ran while one was open for 2% -> 6% of each run, Pallas kernels for 0% -> 0%
where the time goes in v4:
time: 197 us; the launch traced here: 195 us
  waiting for transfers between devices  70.5 us (36%)
  starting transfers between devices  52.4 us (27%)
  blocking collectives  21.9 us (11%)
  between operations  13.7 us (7%)
  Pallas kernels  12.6 us (6%)
  other arithmetic  12.2 us (6%)
  local copies, waits for them, and re-layouts  6.2 us (3%)
  matrix products  5.17 us (3%)
    all_gather x1, waiting for transfers between devices, shards(): gathered = lax.all_gather(rows, ('y', 'core'), tiled=True)  27.9 us
    all_to_all x1, waiting for transfers between devices, shards(): lax.all_to_all(back.reshape(ny * nz, rank, LANE), ('y', 'z'), 0, 0, tiled...  23.5 us
    all_to_all x1, blocking collectives, shards(): lax.all_to_all(rows.reshape(nz, rank, 2 * part), 'z', 0, 0, tiled=True)  21.9 us
    ppermute x1, starting transfers between devices, shards(): got = lax.ppermute(give, 'core', [(0, 1), (1, 0)])  18.3 us
    all_to_all x1, starting transfers between devices, shards(): lax.all_to_all(back.reshape(ny * nz, rank, LANE), ('y', 'z'), 0, 0, tiled...  14.6 us
    pallas_call x1, Pallas kernels, expert_rows(): pl.pallas_call(functools.partial(expert_kernel, cap, nz), out_shape=(jax....  12.6 us
    all_to_all x1, waiting for transfers between devices, shards(): packet = lax.all_to_all(packet, ('y', 'x'), 0, 0, tiled=True)  10.3 us
    all_to_all x1, starting transfers between devices, shards(): packet = lax.all_to_all(packet, ('y', 'x'), 0, 0, tiled=True)  7.71 us
  transfers between devices with their start and end apart: 9, of which 6 were waited for; matrix products, arithmetic and copies ran while one was open for 6% of the time, Pallas kernels for 0%

profile of v4, /device:TPU:1, one launch (start us, length us, event | category | flops | bytes accessed | tf_op | source)
XLA Modules:
  0.0 194.6 jit_solution(8361482769120914442)
XLA Ops:
  6.5 2.2 %pad_maximum_fusion = bf16[3,168,3072]{2,1,0:T(8,128)(2,1)S(1)} fusion(bf16[1,168,3072]{2,1,0:T(8,128)(2,1)} %param.17, bf16[1,168,3072]{2,1,0:T(8,128)(2,1)} %bitcast.99, bf16[1,168,3072]{2,1,0:T(8,128)(2,1)} %bitcast.97), kind=kLoop, calls=%fused_computation.2 | loop fusion | flops 3096576 | bytes 6193152 | tf_op jit(solution)/shard_map/stack | solution.py:171
  8.8 5.8 %collective-permute-start = (bf16[3,168,3072]{2,1,0:T(8,128)(2,1)S(1)}, bf16[3,168,3072]{2,1,0:T(8,128)(2,1)}, u32[]{:S(2)}, u32[]{:S(2)}) collective-permute-start(bf16[3,168,3072]{2,1,0:T(8,128)(2,1)S(1)} %pad_maximum_fusion), channel_id=1, source_target_pairs={{1,48},{16,1},{33,16},{48,33},{3,50},{18,3},{35,18},{50,35},{5,52}... | collective-permute-start | bytes 9289736 | tf_op jit(solution)/shard_map/ppermute | solution.py:178
  14.5 1.9 collective-permute-start.1
  16.5 1.4 fusion.1
  18.0 1.4 fusion.3
  21.2 1.1 convolution_convert_fusion.1
  22.3 1.1 convolution_convert_fusion
  23.4 21.9 %all_to_all.15 = bf16[8,24,768]{2,1,0:T(8,128)(2,1)S(1)} all-to-all(bf16[8,24,768]{2,1,0:T(8,128)(2,1)S(1)} %bitcast.106), channel_id=1, replica_groups=mesh['y'=8,'x'=4,'z'=8,'core'=2] {'z'}, dimensions={0} | all-to-all | bytes 589824 | tf_op jit(solution)/shard_map/all_to_all | solution.py:197
  46.0 1.7 pad.7
  48.2 6.0 %collective-permute-done.1.refs_7_ = bf16[3,168,3072]{2,1,0:T(8,128)(2,1)} collective-permute-done((bf16[3,168,3072]{2,1,0:T(8,128)(2,1)S(1)}, bf16[3,168,3072]{2,1,0:T(8,128)(2,1)}, u32[]{:S(2)}, u32[]{:S(2)}) %collective-permute-start.1) | collective-permute-done | bytes 3096608 | tf_op jit(solution)/shard_map/ppermute | solution.py:179
  54.3 1.6 collective-permute-start.2
  56.0 1.7 collective-permute-start.3
  57.7 1.0 slice_bitcast_fusion
  60.1 27.9 %all-gather.2.cloned.1.call-done = bf16[2304,768]{1,0:T(8,128)(2,1)} async-done(((bf16[144,768]{1,0:T(8,128)(2,1)}), bf16[2304,768]{1,0:T(8,128)(2,1)}) %all-gather.2.cloned.1.call-update) | async-done | bytes 3538960 | tf_op jit(solution)/shard_map/all_gather | solution.py:201
  88.0 12.6 %shard_map.82 = (f32[8,8,56,128]{3,2,1,0:T(8,128)}, bf16[8,8,56,128]{3,2,1,0:T(8,128)(2,1)}) custom-call(s32[2]{0:T(128)} %pad_add_fusion.info, bf16[8,2,144,768]{3,2,1,0:T(8,128)(2,1)} %bitcast.105, bf16[168,3072]{1,0:T(8,128)(2,1)} %bitcast.98, bf16[168,3072]{1,0:T(8,128)(2,1)} %bitcast.100, bf16[168,3072]{1,0:T(8,128)(2,1)} %bitcast.101, ...), custom_call_target="tpu_custom_call" | custom-call | flops 2972712960 | bytes 13271040 | tf_op jit(solution)/shard_map/pallas_call | solution.py:135
  100.6 18.3 %collective-permute-start.5 = (bf16[8,8,56,128]{3,2,1,0:T(8,128)(2,1)}, bf16[8,8,56,128]{3,2,1,0:T(8,128)(2,1)S(1)}, u32[]{:S(2)}, u32[]{:S(2)}) collective-permute-start(bf16[8,8,56,128]{3,2,1,0:T(8,128)(2,1)} %get-tuple-element.36), channel_id=1, source_target_pairs={{0,1},{1,0},{2,3},{3,2},{4,5},{5,4},{6,7},{7,6},{8,9},{9,8},{10,11... | collective-permute-start | bytes 2752520 | tf_op jit(solution)/shard_map/ppermute | solution.py:213
  118.9 2.3 %collective-permute-done.5 = bf16[8,8,56,128]{3,2,1,0:T(8,128)(2,1)S(1)} collective-permute-done((bf16[8,8,56,128]{3,2,1,0:T(8,128)(2,1)}, bf16[8,8,56,128]{3,2,1,0:T(8,128)(2,1)S(1)}, u32[]{:S(2)}, u32[]{:S(2)}) %collective-permute-start.5) | collective-permute-done | bytes 917536 | tf_op jit(solution)/shard_map/ppermute | solution.py:213
  121.2 2.7 %add_convert_fusion = bf16[8,8,56,128]{3,2,1,0:T(8,128)(2,1)} fusion(f32[8,8,56,128]{3,2,1,0:T(8,128)} %get-tuple-element.35, bf16[8,8,56,128]{3,2,1,0:T(8,128)(2,1)S(1)} %collective-permute-done.5), kind=kLoop, calls=%fused_computation.5 | loop fusion | flops 1376256 | bytes 3670016 | tf_op jit(solution)/shard_map/convert_element_type | solution.py:214
  123.8 14.6 %all-to-all-start.1 = ((bf16[64,56,128]{2,1,0:T(8,128)(2,1)}), bf16[64,56,128]{2,1,0:T(8,128)(2,1)S(1)}, u32[]{:S(2)}, u32[]{:S(2)}) async-start(bf16[64,56,128]{2,1,0:T(8,128)(2,1)} %bitcast.21), calls=%async_computation.1 | async-start | bytes 1835008 | tf_op jit(solution)/shard_map/all_to_all | solution.py:216
  139.2 23.5 %all-to-all-done.1 = bf16[64,56,128]{2,1,0:T(8,128)(2,1)S(1)} async-done(((bf16[64,56,128]{2,1,0:T(8,128)(2,1)}), bf16[64,56,128]{2,1,0:T(8,128)(2,1)S(1)}, u32[]{:S(2)}, u32[]{:S(2)}) %all-to-all-start.1) | async-done | bytes 917536 | tf_op jit(solution)/shard_map/all_to_all | solution.py:216
  166.4 7.7 %all-to-all-start.2 = ((f32[32,4,512]{2,1,0:T(4,128)}), f32[32,4,512]{2,1,0:T(4,128)S(1)}, u32[]{:S(2)}, u32[]{:S(2)}) async-start(f32[32,4,512]{2,1,0:T(4,128)} %reshape.153), calls=%async_computation.2 | async-start | bytes 524288 | tf_op jit(solution)/shard_map/all_to_all | solution.py:238
  174.2 10.3 %all-to-all-done.2 = f32[32,4,512]{2,1,0:T(4,128)S(1)} async-done(((f32[32,4,512]{2,1,0:T(4,128)}), f32[32,4,512]{2,1,0:T(4,128)S(1)}, u32[]{:S(2)}, u32[]{:S(2)}) %all-to-all-start.2) | async-done | bytes 262176 | tf_op jit(solution)/shard_map/all_to_all | solution.py:238
  185.0 1.2 fusion.11
  186.3 1.5 fusion.15
  (71 shorter events, 9.6 us)
Async XLA Ops:
  6.5 13.7 %copy-start = (bf16[3072,16]{0,1:T(8,128)(2,1)S(1)}, bf16[3072,16]{0,1:T(8,128)(2,1)}, u32[]{:S(2)}) copy-start(bf16[3072,16]{0,1:T(8,128)(2,1)} %param.13) | copy-start | bytes 294916
  6.5 81.4 %all-gather.2.cloned.1.call-start = ((), (), s32[]{:S(2)}) async-start(), calls=%async_computation.3 | async-start | bytes 3760128 | tf_op jit(solution)/shard_map/all_gather | solution.py:201
  6.5 11.4 %copy-start.3 = (s32[128,4]{0,1:T(4,128)S(1)}, s32[128,4]{0,1:T(4,128)}, u32[]{:S(2)}) copy-start(s32[128,4]{0,1:T(4,128)} %param.14) | copy-start | bytes 6148
  6.5 11.4 %copy-start.4 = (f32[3072]{0:T(1024)S(1)}, f32[3072]{0:T(1024)}, u32[]{:S(2)}) copy-start(f32[3072]{0:T(1024)} %param.12) | copy-start | bytes 36868
  8.8 39.5 %collective-permute-start = (bf16[3,168,3072]{2,1,0:T(8,128)(2,1)S(1)}, bf16[3,168,3072]{2,1,0:T(8,128)(2,1)}, u32[]{:S(2)}, u32[]{:S(2)}) collective-permute-start(bf16[3,168,3072]{2,1,0:T(8,128)(2,1)S(1)} %pad_maximum_fusion), channel_id=1, source_target_pairs={{1,48},{16,1},{33,16},{48,33},{3,50},{18,3},{35,18},{50,35},{5,52}... | collective-permute-start | bytes 9289736 | tf_op jit(solution)/shard_map/ppermute | solution.py:178
  14.5 39.7 %collective-permute-start.1 = (bf16[3,168,3072]{2,1,0:T(8,128)(2,1)S(1)}, bf16[3,168,3072]{2,1,0:T(8,128)(2,1)}, u32[]{:S(2)}, u32[]{:S(2)}) collective-permute-start(bf16[3,168,3072]{2,1,0:T(8,128)(2,1)S(1)} %pad_maximum_fusion), channel_id=1, source_target_pairs={{1,16},{16,33},{33,48},{48,1},{3,18},{18,35},{35,50},{50,3},{5,20}... | collective-permute-start | bytes 9289736 | tf_op jit(solution)/shard_map/ppermute | solution.py:179
  19.4 0.9 copy-start.1
  54.3 1.6 collective-permute-start.2
  56.0 1.7 collective-permute-start.3
  58.8 1.3 collective-permute-start.4
  60.1 27.9 %copy-start.2 = (bf16[168,3072]{1,0:T(8,128)(2,1)}, bf16[168,3072]{1,0:T(8,128)(2,1)S(1)}, u32[]{:S(2)}) copy-start(bf16[168,3072]{1,0:T(8,128)(2,1)S(1)} %collective-permute-done.4.refs_5_) | copy-start | bytes 3096580
  100.6 20.6 %collective-permute-start.5 = (bf16[8,8,56,128]{3,2,1,0:T(8,128)(2,1)}, bf16[8,8,56,128]{3,2,1,0:T(8,128)(2,1)S(1)}, u32[]{:S(2)}, u32[]{:S(2)}) collective-permute-start(bf16[8,8,56,128]{3,2,1,0:T(8,128)(2,1)} %get-tuple-element.36), channel_id=1, source_target_pairs={{0,1},{1,0},{2,3},{3,2},{4,5},{5,4},{6,7},{7,6},{8,9},{9,8},{10,11... | collective-permute-start | bytes 2752520 | tf_op jit(solution)/shard_map/ppermute | solution.py:213
  123.8 38.8 %all-to-all-start.1 = ((bf16[64,56,128]{2,1,0:T(8,128)(2,1)}), bf16[64,56,128]{2,1,0:T(8,128)(2,1)S(1)}, u32[]{:S(2)}, u32[]{:S(2)}) async-start(bf16[64,56,128]{2,1,0:T(8,128)(2,1)} %bitcast.21), calls=%async_computation.1 | async-start | bytes 1835008 | tf_op jit(solution)/shard_map/all_to_all | solution.py:216
  166.4 18.1 %all-to-all-start.2 = ((f32[32,4,512]{2,1,0:T(4,128)}), f32[32,4,512]{2,1,0:T(4,128)S(1)}, u32[]{:S(2)}, u32[]{:S(2)}) async-start(f32[32,4,512]{2,1,0:T(4,128)} %reshape.153), calls=%async_computation.2 | async-start | bytes 524288 | tf_op jit(solution)/shard_map/all_to_all | solution.py:238
Sparse Core Ops, SparseCore 0:
  47.8 40.0 all-gather.1

commit v5 on v4

--- a/solution.py
+++ b/solution.py
@@ -40,8 +40,8 @@
 
 
 def expert_kernel(cap, nz, info, rows_hbm, *refs):
-    slices, (left, right, keep_ref, give_ref) = refs[:6], refs[6:10]
-    h_ref, g_ref, w_ref, row_sem, w_sem = refs[10:]
+    mine, (far, left, right, keep_ref, give_ref) = refs[:3], refs[3:8]
+    h_ref, g_ref, w_ref, row_sem, w_sem = refs[8:]
     ny, groups, count = rows_hbm.shape[0], rows_hbm.shape[1], rows_hbm.shape[2]
     part = rows_hbm.shape[3] // 2
     rank, lane = keep_ref.shape[2], keep_ref.shape[3]
@@ -49,24 +49,22 @@
     contract = (((1,), (1,)), ((), ()))
     own, core = info[0], info[1]
 
-    def fetch(u):
-        return [
-            pltpu.make_async_copy(slices[3 * u + j], w_ref.at[u, j], w_sem.at[u, j])
-            for j in range(3)
-        ]
-
-    def start(u, other):
+    def fetch(u, source):
+        return [pltpu.make_async_copy(source[j], w_ref.at[u, j], w_sem.at[u, j]) for j in range(3)]
+
+    def start(u, if_own, other):
         @pl.when(own == 1)
         def _():
-            for copy in fetch(u):
+            for copy in fetch(u, if_own):
                 copy.start()
 
         @pl.when(own == 0)
         def _():
-            for j in range(3):
-                pltpu.make_async_copy(other.at[j], w_ref.at[u, j], w_sem.at[u, j]).start()
-
-    start(0, left)
+            for copy in fetch(u, other):
+                copy.start()
+
+    left, right, far = ([ref.at[j] for j in range(3)] for ref in (left, right, far))
+    start(0, mine, left)
 
     row_copies = []
     for j, ref in enumerate((h_ref, g_ref)):
@@ -82,13 +80,13 @@
                 )
     for copy in row_copies:
         copy.start()
-    start(1, right)
+    start(1, far, right)
     for copy in row_copies:
         copy.wait()
     score = 0.0
     pulls = []
     for u in range(2):
-        for copy in fetch(u):
+        for copy in fetch(u, mine):
             copy.wait()
         a = lax.dot_general(h_ref[...], w_ref[u, 0], contract, preferred_element_type=f32)
         b = lax.dot_general(h_ref[...], w_ref[u, 1], contract, preferred_element_type=f32)
@@ -126,6 +124,22 @@
                 ref[i, z] = block.astype(ref.dtype)
 
 
+def after_kernel(info, left, right, far, out):
+    out[0] = info[0]
+    out[1] = info[1]
+
+
+def after(info, left, right, far):
+    smem = pl.BlockSpec(memory_space=pltpu.SMEM)
+    return pl.pallas_call(
+        after_kernel,
+        out_shape=jax.ShapeDtypeStruct(info.shape, info.dtype),
+        in_specs=[smem] + [pl.BlockSpec(memory_space=pl.ANY)] * 3,
+        out_specs=smem,
+        cost_estimate=pl.CostEstimate(flops=50000000000, bytes_accessed=0, transcendentals=0),
+    )(info, left, right, far)
+
+
 def expert_rows(info, gathered, slices, nz, cap, rank):
     ny, groups, count, wide = gathered.shape
     kinds, hidden, width = slices[-1].shape
@@ -138,7 +152,7 @@
             jax.ShapeDtypeStruct((ny, nz, rank, LANE), f32),
             jax.ShapeDtypeStruct((ny, nz, rank, LANE), bf16),
         ),
-        in_specs=[pl.BlockSpec(memory_space=pltpu.SMEM)] + [hbm] * 9,
+        in_specs=[pl.BlockSpec(memory_space=pltpu.SMEM)] + [hbm] * 7,
         out_specs=(vmem, vmem),
         scratch_shapes=[
             pltpu.VMEM((rows, width), bf16),
@@ -177,6 +191,7 @@
         across.append((i * nc + a, (i + 2) % nx * nc + a))
     left = lax.ppermute(mine, ("x", "core"), behind)
     right = lax.ppermute(mine, ("x", "core"), ahead)
+    far = lax.ppermute(mine, ("x", "core"), across)
     info = jnp.stack([(core == parity).astype(jnp.int32), core.astype(jnp.int32)])
 
     h, sig, total, weight, select = token_weights(acts, gain, router, ids)
@@ -199,16 +214,12 @@
     rows = rows[:, :cap].reshape(nz * cap, 2 * part)
     rows = jnp.pad(rows, ((0, count - nz * cap), (0, 0)))
     gathered = lax.all_gather(rows, ("y", "core"), tiled=True)
-    left, right, source, _ = lax.optimization_barrier((left, right, mine, rows))
-    far = []
-    for i in range(3):
-        far.append(lax.ppermute(source[i], ("x", "core"), across))
-        far[i], source = lax.optimization_barrier((far[i], source))
+    info = after(info, left, right, far)
 
     pieces = part // LANE
     rank = -(-(pieces * cap + 4) // 8) * 8
     keep, give = expert_rows(
-        info, gathered.reshape(ny, nc, count, 2 * part), (*own_slice, *far, left, right), nz, cap, rank
+        info, gathered.reshape(ny, nc, count, 2 * part), (*own_slice, far, left, right), nz, cap, rank
     )
     got = lax.ppermute(give, "core", [(0, 1), (1, 0)])
     back = (keep + got.astype(f32)).astype(bf16)

time: 197 us -> 183 us (0.929)
  starting transfers between devices: 52.4 us -> 34.3 us
  waiting for transfers between devices: 70.5 us -> 81 us
  local copies, waits for them, and re-layouts: 6.2 us -> 2.49 us
    ppermute x1, waiting for transfers between devices: 0.49 us -> 38.3 us  [shards(): left = lax.ppermute(mine, ('x', 'core'), behind)]
    all_gather x1, waiting for transfers between devices: 27.9 us -> 0.02 us  [shards(): gathered = lax.all_gather(rows, ('y', 'core'), tiled=True)]
    ppermute x1, starting transfers between devices: 18.3 us -> 1.92 us  [shards(): got = lax.ppermute(give, 'core', [(0, 1), (1, 0)])]
    ppermute x3 -> x1, starting transfers between devices: 4.06 us -> 2.31 us  [shards(): far = lax.ppermute(mine, ('x', 'core'), across)]
  transfers between devices with their start and end apart: 9 -> 7, of which waited for: 6 -> 5; matrix products, arithmetic and copies ran while one was open for 6% -> 3% of each run, Pallas kernels for 0% -> 1%
where the time goes in v5:
time: 183 us; the launch traced here: 181 us
  waiting for transfers between devices  81 us (44%)
  starting transfers between devices  34.3 us (19%)
  blocking collectives  20.3 us (11%)
  Pallas kernels  13.8 us (8%)
  between operations  13.7 us (7%)
  other arithmetic  11.6 us (6%)
  matrix products  3.44 us (2%)
  local copies, waits for them, and re-layouts  2.49 us (1%)
    ppermute x1, waiting for transfers between devices, shards(): left = lax.ppermute(mine, ('x', 'core'), behind)  38.3 us
    all_to_all x1, waiting for transfers between devices, shards(): lax.all_to_all(back.reshape(ny * nz, rank, LANE), ('y', 'z'), 0, 0, tiled...  24.2 us
    all_to_all x1, blocking collectives, shards(): lax.all_to_all(rows.reshape(nz, rank, 2 * part), 'z', 0, 0, tiled=True)  20.3 us
    all_to_all x1, starting transfers between devices, shards(): lax.all_to_all(back.reshape(ny * nz, rank, LANE), ('y', 'z'), 0, 0, tiled...  16.3 us
    pallas_call x1, Pallas kernels, expert_rows(): pl.pallas_call(functools.partial(expert_kernel, cap, nz), out_shape=(jax....  12.6 us
    all_to_all x1, waiting for transfers between devices, shards(): packet = lax.all_to_all(packet, ('y', 'x'), 0, 0, tiled=True)  10.3 us
    all_to_all x1, starting transfers between devices, shards(): packet = lax.all_to_all(packet, ('y', 'x'), 0, 0, tiled=True)  5.9 us
    ppermute x1, starting transfers between devices, shards(): left = lax.ppermute(mine, ('x', 'core'), behind)  5.9 us
  transfers between devices with their start and end apart: 7, of which 5 were waited for; matrix products, arithmetic and copies ran while one was open for 3% of the time, Pallas kernels for 1%

profile of v5, /device:TPU:1, one launch (start us, length us, event | category | flops | bytes accessed | tf_op | source)
XLA Modules:
  0.0 180.7 jit_solution(18362866722762774494)
XLA Ops:
  6.5 3.9 %pad_maximum_fusion = bf16[3,168,3072]{2,1,0:T(8,128)(2,1)} fusion(bf16[1,168,3072]{2,1,0:T(8,128)(2,1)} %param.17, bf16[1,168,3072]{2,1,0:T(8,128)(2,1)} %bitcast.92, bf16[1,168,3072]{2,1,0:T(8,128)(2,1)} %bitcast.94), kind=kLoop, calls=%fused_computation.2 | loop fusion | flops 3096576 | bytes 6193152 | tf_op jit(solution)/shard_map/stack | solution.py:185
  10.4 5.9 %collective-permute-start = (bf16[3,168,3072]{2,1,0:T(8,128)(2,1)}, bf16[3,168,3072]{2,1,0:T(8,128)(2,1)}, u32[]{:S(2)}, u32[]{:S(2)}) collective-permute-start(bf16[3,168,3072]{2,1,0:T(8,128)(2,1)} %pad_maximum_fusion), channel_id=1, source_target_pairs={{1,48},{16,1},{33,16},{48,33},{3,50},{18,3},{35,18},{50,35},{5,52}... | collective-permute-start | bytes 9289736 | tf_op jit(solution)/shard_map/ppermute | solution.py:192
  16.3 1.9 %collective-permute-start.1 = (bf16[3,168,3072]{2,1,0:T(8,128)(2,1)}, bf16[3,168,3072]{2,1,0:T(8,128)(2,1)}, u32[]{:S(2)}, u32[]{:S(2)}) collective-permute-start(bf16[3,168,3072]{2,1,0:T(8,128)(2,1)} %pad_maximum_fusion), channel_id=1, source_target_pairs={{1,16},{16,33},{33,48},{48,1},{3,18},{18,35},{35,50},{50,3},{5,20}... | collective-permute-start | bytes 9289736 | tf_op jit(solution)/shard_map/ppermute | solution.py:193
  18.3 2.3 %collective-permute-start.2 = (bf16[3,168,3072]{2,1,0:T(8,128)(2,1)}, bf16[3,168,3072]{2,1,0:T(8,128)(2,1)}, u32[]{:S(2)}, u32[]{:S(2)}) collective-permute-start(bf16[3,168,3072]{2,1,0:T(8,128)(2,1)} %pad_maximum_fusion), channel_id=1, source_target_pairs={{0,32},{17,49},{32,0},{49,17},{2,34},{19,51},{34,2},{51,19},{4,36}... | collective-permute-start | bytes 9289736 | tf_op jit(solution)/shard_map/ppermute | solution.py:194
  22.3 1.1 convolution_convert_fusion
  23.4 20.3 %all_to_all.15 = bf16[8,24,768]{2,1,0:T(8,128)(2,1)S(1)} all-to-all(bf16[8,24,768]{2,1,0:T(8,128)(2,1)S(1)} %bitcast.100), channel_id=1, replica_groups=mesh['y'=8,'x'=4,'z'=8,'core'=2] {'z'}, dimensions={0} | all-to-all | bytes 589824 | tf_op jit(solution)/shard_map/all_to_all | solution.py:212
  43.8 0.7 pad.7
  44.6 0.7 pad_add_fusion.info
  45.2 38.3 %collective-permute-done.left.refs_4_ = bf16[3,168,3072]{2,1,0:T(8,128)(2,1)} collective-permute-done((bf16[3,168,3072]{2,1,0:T(8,128)(2,1)}, bf16[3,168,3072]{2,1,0:T(8,128)(2,1)}, u32[]{:S(2)}, u32[]{:S(2)}) %collective-permute-start) | collective-permute-done | bytes 3096608 | tf_op jit(solution)/shard_map/ppermute | solution.py:192
  83.5 5.6 %collective-permute-done.1.right.refs_5_ = bf16[3,168,3072]{2,1,0:T(8,128)(2,1)} collective-permute-done((bf16[3,168,3072]{2,1,0:T(8,128)(2,1)}, bf16[3,168,3072]{2,1,0:T(8,128)(2,1)}, u32[]{:S(2)}, u32[]{:S(2)}) %collective-permute-start.1) | collective-permute-done | bytes 3096608 | tf_op jit(solution)/shard_map/ppermute | solution.py:193
  89.1 1.2 shard_map.82.info
  90.3 12.6 %shard_map.83 = (f32[8,8,56,128]{3,2,1,0:T(8,128)}, bf16[8,8,56,128]{3,2,1,0:T(8,128)(2,1)}) custom-call(s32[2]{0:T(128)} %shard_map.82.info, bf16[8,2,144,768]{3,2,1,0:T(8,128)(2,1)} %bitcast.99, bf16[168,3072]{1,0:T(8,128)(2,1)} %bitcast.95, bf16[168,3072]{1,0:T(8,128)(2,1)} %bitcast.93, bf16[168,3072]{1,0:T(8,128)(2,1)} %bitcast.91, ...), custom_call_target="tpu_custom_call" | custom-call | flops 2972712960 | bytes 13271040 | tf_op jit(solution)/shard_map/pallas_call | solution.py:149
  102.9 1.9 %collective-permute-start.3 = (bf16[8,8,56,128]{3,2,1,0:T(8,128)(2,1)}, bf16[8,8,56,128]{3,2,1,0:T(8,128)(2,1)S(1)}, u32[]{:S(2)}, u32[]{:S(2)}) collective-permute-start(bf16[8,8,56,128]{3,2,1,0:T(8,128)(2,1)} %get-tuple-element.20), channel_id=1, source_target_pairs={{0,1},{1,0},{2,3},{3,2},{4,5},{5,4},{6,7},{7,6},{8,9},{9,8},{10,11... | collective-permute-start | bytes 2752520 | tf_op jit(solution)/shard_map/ppermute | solution.py:224
  104.9 2.6 %collective-permute-done.3 = bf16[8,8,56,128]{3,2,1,0:T(8,128)(2,1)S(1)} collective-permute-done((bf16[8,8,56,128]{3,2,1,0:T(8,128)(2,1)}, bf16[8,8,56,128]{3,2,1,0:T(8,128)(2,1)S(1)}, u32[]{:S(2)}, u32[]{:S(2)}) %collective-permute-start.3) | collective-permute-done | bytes 917536 | tf_op jit(solution)/shard_map/ppermute | solution.py:224
  107.5 2.6 %add_convert_fusion = bf16[8,8,56,128]{3,2,1,0:T(8,128)(2,1)} fusion(f32[8,8,56,128]{3,2,1,0:T(8,128)} %get-tuple-element.19, bf16[8,8,56,128]{3,2,1,0:T(8,128)(2,1)S(1)} %collective-permute-done.3), kind=kLoop, calls=%fused_computation.5 | loop fusion | flops 1376256 | bytes 3670016 | tf_op jit(solution)/shard_map/convert_element_type | solution.py:225
  110.1 16.3 %all-to-all-start.1 = ((bf16[64,56,128]{2,1,0:T(8,128)(2,1)}), bf16[64,56,128]{2,1,0:T(8,128)(2,1)S(1)}, u32[]{:S(2)}, u32[]{:S(2)}) async-start(bf16[64,56,128]{2,1,0:T(8,128)(2,1)} %bitcast.16), calls=%async_computation.1 | async-start | bytes 1835008 | tf_op jit(solution)/shard_map/all_to_all | solution.py:227
  126.5 0.6 compare_reduce_fusion.1
  127.2 24.2 %all-to-all-done.1 = bf16[64,56,128]{2,1,0:T(8,128)(2,1)S(1)} async-done(((bf16[64,56,128]{2,1,0:T(8,128)(2,1)}), bf16[64,56,128]{2,1,0:T(8,128)(2,1)S(1)}, u32[]{:S(2)}, u32[]{:S(2)}) %all-to-all-start.1) | async-done | bytes 917536 | tf_op jit(solution)/shard_map/all_to_all | solution.py:227
  153.1 0.4 fusion.29
  153.5 0.7 broadcast_select_fusion
  154.4 0.8 reshape.153
  155.1 5.9 %all-to-all-start.2 = ((f32[32,4,512]{2,1,0:T(4,128)}), f32[32,4,512]{2,1,0:T(4,128)S(1)}, u32[]{:S(2)}, u32[]{:S(2)}) async-start(f32[32,4,512]{2,1,0:T(4,128)} %reshape.153), calls=%async_computation.2 | async-start | bytes 524288 | tf_op jit(solution)/shard_map/all_to_all | solution.py:249
  161.1 10.3 %all-to-all-done.2 = f32[32,4,512]{2,1,0:T(4,128)S(1)} async-done(((f32[32,4,512]{2,1,0:T(4,128)}), f32[32,4,512]{2,1,0:T(4,128)S(1)}, u32[]{:S(2)}, u32[]{:S(2)}) %all-to-all-start.2) | async-done | bytes 262176 | tf_op jit(solution)/shard_map/all_to_all | solution.py:249
  172.4 1.5 fusion.15
  (63 shorter events, 4.6 us)
Async XLA Ops:
  6.5 14.6 %copy-start = (bf16[3072,16]{0,1:T(8,128)(2,1)S(1)}, bf16[3072,16]{0,1:T(8,128)(2,1)}, u32[]{:S(2)}) copy-start(bf16[3072,16]{0,1:T(8,128)(2,1)} %param.13) | copy-start | bytes 294916
  6.5 83.8 %all-gather.2.cloned.1.call-start = ((), (), s32[]{:S(2)}) async-start(), calls=%async_computation.3 | async-start | bytes 3760128 | tf_op jit(solution)/shard_map/all_gather | solution.py:216
  6.5 14.0 %copy-start.1 = (bf16[128,3072]{1,0:T(8,128)(2,1)S(1)}, bf16[128,3072]{1,0:T(8,128)(2,1)}, u32[]{:S(2)}) copy-start(bf16[128,3072]{1,0:T(8,128)(2,1)} %param.10) | copy-start | bytes 2359300
  6.5 14.3 %copy-start.3 = (f32[3072]{0:T(1024)S(1)}, f32[3072]{0:T(1024)}, u32[]{:S(2)}) copy-start(f32[3072]{0:T(1024)} %param.12) | copy-start | bytes 36868
  10.4 11.0 %copy-start.2 = (s32[128,4]{0,1:T(4,128)S(1)}, s32[128,4]{0,1:T(4,128)}, u32[]{:S(2)}) copy-start(s32[128,4]{0,1:T(4,128)} %param.14) | copy-start | bytes 6148
  10.4 73.1 %collective-permute-start = (bf16[3,168,3072]{2,1,0:T(8,128)(2,1)}, bf16[3,168,3072]{2,1,0:T(8,128)(2,1)}, u32[]{:S(2)}, u32[]{:S(2)}) collective-permute-start(bf16[3,168,3072]{2,1,0:T(8,128)(2,1)} %pad_maximum_fusion), channel_id=1, source_target_pairs={{1,48},{16,1},{33,16},{48,33},{3,50},{18,3},{35,18},{50,35},{5,52}... | collective-permute-start | bytes 9289736 | tf_op jit(solution)/shard_map/ppermute | solution.py:192
  16.3 72.8 %collective-permute-start.1 = (bf16[3,168,3072]{2,1,0:T(8,128)(2,1)}, bf16[3,168,3072]{2,1,0:T(8,128)(2,1)}, u32[]{:S(2)}, u32[]{:S(2)}) collective-permute-start(bf16[3,168,3072]{2,1,0:T(8,128)(2,1)} %pad_maximum_fusion), channel_id=1, source_target_pairs={{1,16},{16,33},{33,48},{48,1},{3,18},{18,35},{35,50},{50,3},{5,20}... | collective-permute-start | bytes 9289736 | tf_op jit(solution)/shard_map/ppermute | solution.py:193
  18.3 70.8 %collective-permute-start.2 = (bf16[3,168,3072]{2,1,0:T(8,128)(2,1)}, bf16[3,168,3072]{2,1,0:T(8,128)(2,1)}, u32[]{:S(2)}, u32[]{:S(2)}) collective-permute-start(bf16[3,168,3072]{2,1,0:T(8,128)(2,1)} %pad_maximum_fusion), channel_id=1, source_target_pairs={{0,32},{17,49},{32,0},{49,17},{2,34},{19,51},{34,2},{51,19},{4,36}... | collective-permute-start | bytes 9289736 | tf_op jit(solution)/shard_map/ppermute | solution.py:194
  102.9 4.6 %collective-permute-start.3 = (bf16[8,8,56,128]{3,2,1,0:T(8,128)(2,1)}, bf16[8,8,56,128]{3,2,1,0:T(8,128)(2,1)S(1)}, u32[]{:S(2)}, u32[]{:S(2)}) collective-permute-start(bf16[8,8,56,128]{3,2,1,0:T(8,128)(2,1)} %get-tuple-element.20), channel_id=1, source_target_pairs={{0,1},{1,0},{2,3},{3,2},{4,5},{5,4},{6,7},{7,6},{8,9},{9,8},{10,11... | collective-permute-start | bytes 2752520 | tf_op jit(solution)/shard_map/ppermute | solution.py:224
  110.1 41.2 %all-to-all-start.1 = ((bf16[64,56,128]{2,1,0:T(8,128)(2,1)}), bf16[64,56,128]{2,1,0:T(8,128)(2,1)S(1)}, u32[]{:S(2)}, u32[]{:S(2)}) async-start(bf16[64,56,128]{2,1,0:T(8,128)(2,1)} %bitcast.16), calls=%async_computation.1 | async-start | bytes 1835008 | tf_op jit(solution)/shard_map/all_to_all | solution.py:227
  155.1 16.3 %all-to-all-start.2 = ((f32[32,4,512]{2,1,0:T(4,128)}), f32[32,4,512]{2,1,0:T(4,128)S(1)}, u32[]{:S(2)}, u32[]{:S(2)}) async-start(f32[32,4,512]{2,1,0:T(4,128)} %reshape.153), calls=%async_computation.2 | async-start | bytes 524288 | tf_op jit(solution)/shard_map/all_to_all | solution.py:249
Sparse Core Ops, SparseCore 0:
  44.7 41.6 all-gather.1

commit v6 on v3

v6 whole, which is shorter than its diff:
```python
import functools
import jax
import jax.numpy as jnp
from jax import lax
from jax.experimental import pallas as pl
from jax.experimental.pallas import tpu as pltpu
from jax.sharding import Mesh, PartitionSpec as P

eps = 1e-05
X = 4
CORES = 2
LANE = 128
bf16 = jnp.bfloat16
f32 = jnp.float32


def token_weights(acts, gain, router, ids):
    wide = acts.astype(f32)
    recip = lax.rsqrt(jnp.mean(wide * wide, axis=-1, keepdims=True) + eps)
    h = (wide * recip * gain).astype(bf16)
    logits = jnp.dot(h, router, preferred_element_type=f32)
    experts = router.shape[1]
    select = (ids[:, :, None] == jnp.arange(experts, dtype=jnp.int32)[None, None, :]).astype(f32)
    picked = jnp.sum(select * logits[:, None, :], axis=-1)
    sig = jax.nn.sigmoid(picked)
    total = jnp.sum(sig, axis=1, keepdims=True)
    return h, sig, total, sig / total, select


def places(ids, names):
    tokens = ids.shape[0]
    member = jnp.any(ids[:, :, None] == names[None, None, :], axis=1)
    below = (jnp.arange(tokens)[:, None] > jnp.arange(tokens)[None, :]).astype(bf16)
    place = jnp.dot(below, member.astype(bf16), preferred_element_type=f32).astype(jnp.int32)
    return jnp.where(member, place, -4096).T


def at_rows(place, count):
    return place[:, None, :] == jnp.arange(count, dtype=jnp.int32)[None, :, None]


def expert_kernel(cap, nz, rows_hbm, first, second, out_hbm, *scratch):
    h_ref, g_ref, w_ref, out_ref, row_sem, w_sem, out_sem = scratch
    ny, part = rows_hbm.shape[0], rows_hbm.shape[2] // 2
    rank, lane = out_ref.shape[2], out_ref.shape[3]
    pieces = part // lane
    contract = (((1,), (1,)), ((), ()))

    def rows_of(j, ref):
        return [
            pltpu.make_async_copy(
                rows_hbm.at[i, :, pl.ds(j * part, part)],
                ref.at[:, pl.ds(i * part, part)],
                row_sem.at[j, i],
            )
            for i in range(ny)
        ]

    h_copies, g_copies = rows_of(0, h_ref), rows_of(1, g_ref)
    w_copies = [
        [pltpu.make_async_copy(s.at[j], w_ref.at[u, j], w_sem.at[u, j]) for j in range(3)]
        for u, s in enumerate((first, second))
    ]
    def begin(copies):
        for copy in copies:
            copy.start()

    def end(copies):
        for copy in copies:
            copy.wait()

    def times(u, j, ref):
        return lax.dot_general(ref[...], w_ref[u, j], contract, preferred_element_type=f32)

    a, b, dact = [None, None], [None, None], [None, None]
    begin(h_copies + w_copies[0][:1])
    begin(w_copies[0][1:2])
    end(h_copies + w_copies[0][:1])
    begin(g_copies + w_copies[0][2:])
    a[0] = times(0, 0, h_ref)
    end(w_copies[0][1:2])
    begin(w_copies[1][:1])
    b[0] = times(0, 1, h_ref)
    end(g_copies + w_copies[0][2:])
    begin(w_copies[1][1:])
    dact[0] = times(0, 2, g_ref)
    end(w_copies[1][:1])
    a[1] = times(1, 0, h_ref)
    end(w_copies[1][1:])
    b[1] = times(1, 1, h_ref)
    dact[1] = times(1, 2, g_ref)
    score = 0.0
    pulls = []
    for u in range(2):
        sg = jax.nn.sigmoid(a[u])
        sa = a[u] * sg
        act = (sa * b[u]).astype(bf16).astype(f32)
        score = score + jnp.sum(act * dact[u], axis=1, keepdims=True)
        pulls.append((dact[u] * b[u] * sg * (1.0 + a[u] * (1.0 - sg))).astype(bf16))
        pulls.append((dact[u] * sa).astype(bf16))
    lanes = lax.broadcasted_iota(jnp.int32, (cap, lane), 1)
    eye = lanes == lax.broadcasted_iota(jnp.int32, (cap, lane), 0)
    tails = []
    for z in range(nz):
        line = jnp.sum(jnp.where(eye, score[z * cap : (z + 1) * cap], 0.0), axis=0, keepdims=True)
        high = line.astype(bf16).astype(f32)
        tail = [high, line - high]
        if rank > pieces * cap + 2:
            tail.append(jnp.zeros((rank - pieces * cap - 2, lane), f32))
        tails.append(tail)
    stores = []
    for i in range(ny):
        band = pl.ds(i * part, part)
        dh = 0.0
        for u in range(2):
            for j in range(2):
                dh = dh + jnp.dot(pulls[2 * u + j], w_ref[u, j, :, band], preferred_element_type=f32)
        for z in range(nz):
            block = dh[z * cap : (z + 1) * cap]
            block = [block[:, p * lane : (p + 1) * lane] for p in range(pieces)]
            out_ref[i, z] = jnp.concatenate(block + tails[z], axis=0).astype(bf16)
        stores.append(pltpu.make_async_copy(out_ref.at[i], out_hbm.at[i], out_sem.at[i]))
        stores[i].start()
    for copy in stores:
        copy.wait()


def expert_rows(gathered, first, second, nz, cap, rank):
    ny, rows, wide = gathered.shape
    kinds, hidden, width = first.shape
    hbm = pl.BlockSpec(memory_space=pl.ANY)
    return pl.pallas_call(
        functools.partial(expert_kernel, cap, nz),
        out_shape=jax.ShapeDtypeStruct((ny, nz, rank, LANE), bf16),
        in_specs=[hbm] * 3,
        out_specs=hbm,
        scratch_shapes=[
            pltpu.VMEM((rows, width), bf16),
            pltpu.VMEM((rows, width), bf16),
            pltpu.VMEM((2, kinds, hidden, width), bf16),
            pltpu.VMEM((ny, nz, rank, LANE), bf16),
            pltpu.SemaphoreType.DMA((2, ny)),
            pltpu.SemaphoreType.DMA((2, 3)),
            pltpu.SemaphoreType.DMA((ny,)),
        ],
        compiler_params=pltpu.CompilerParams(vmem_limit_bytes=56 * 1024 * 1024),
        cost_estimate=pl.CostEstimate(
            flops=20 * rows * width * hidden,
            bytes_accessed=2 * (3 * rows * width + 6 * width * hidden),
            transcendentals=2 * rows * hidden,
        ),
    )(gathered, first, second)


def shards(acts, cotangent, gain, router, ids, w_gate, w_up, w_down):
    ny, nx, nz, nc = (lax.axis_size(n) for n in ("y", "x", "z", "core"))
    y, x, core = (lax.axis_index(n) for n in ("y", "x", "core"))
    tokens, width = acts.shape
    top = ids.shape[1]
    experts = nz * nc
    cap = min(tokens, (17 * tokens * top + 16 * experts - 1) // (16 * experts))
    part = width // ny
    parity = x % 2

    mine = jnp.stack([w_gate[0].T, w_up[0].T, w_down[0]])
    pairs = []
    for m in range(nx // 2):
        i, j = (2 * m) * nc + 1, (2 * m + 1) * nc
        pairs += [(i, j), (j, i)]
    swapped = lax.ppermute(mine, ("x", "core"), pairs)
    first = jnp.where(core == parity, mine, swapped)
    second = lax.ppermute(first, "core", [(0, 1), (1, 0)])

    h, sig, total, weight, select = token_weights(acts, gain, router, ids)
    names = 2 * jnp.arange(nz, dtype=jnp.int32) + parity
    place = places(ids, names)
    here = at_rows(place, cap)
    of_name = (ids[:, :, None] == names[None, None, :]).astype(f32)
    dense = jnp.sum(of_name * weight[:, :, None], axis=1).astype(bf16)
    h_part = lax.dynamic_slice_in_dim(h, y * part, part, 1)
    g_part = lax.dynamic_slice_in_dim(cotangent, y * part, part, 1)
    rank = -(-cap // 8) * 8
    pick = at_rows(place, rank).astype(bf16)
    scaled = pick * dense.T[:, None, :]
    h_rows = jnp.dot(pick.reshape(nz * rank, tokens), h_part, preferred_element_type=f32)
    dy_rows = jnp.dot(scaled.reshape(nz * rank, tokens), g_part, preferred_element_type=f32)
    rows = jnp.concatenate([h_rows.astype(bf16), dy_rows.astype(bf16)], axis=1)
    rows = lax.all_to_all(rows.reshape(nz, rank, 2 * part), "z", 0, 0, tiled=True)
    rows = rows[:, :cap].reshape(nz * cap, 2 * part)
    gathered = lax.all_gather(rows, "y")

    pieces = part // LANE
    rank = -(-(pieces * cap + 2) // 8) * 8
    back = expert_rows(gathered, first, second, nz, cap, rank)

    back = lax.all_to_all(back.reshape(ny * nz, rank, LANE), ("y", "z"), 0, 0, tiled=True)
    flat = back.reshape(ny * nz * rank, LANE)
    parts = []
    for k in range(pieces):
        spread = at_rows(place + k * cap, rank).astype(bf16)
        spread = jnp.broadcast_to(spread[None], (ny, nz, rank, tokens))
        parts.append(
            lax.dot_general(
                spread.reshape(ny * nz * rank, tokens),
                flat,
                (((0,), (0,)), ((), ())),
                preferred_element_type=f32,
            )
        )
    score = jnp.sum(back[:, pieces * cap : pieces * cap + 2, :cap].astype(f32), axis=1)
    score = score.reshape(ny, nz, cap).sum(axis=0)
    score = jnp.sum(here.astype(f32) * score[:, :, None], axis=1)
    score = jnp.sum(of_name * score.T[:, None, :], axis=-1)
    sections = ny * nx
    share = tokens // sections
    tail = jnp.zeros((tokens, LANE), f32).at[:, :top].set(score)
    packet = jnp.concatenate(parts + [tail], axis=1).reshape(sections, share, part + LANE)
    packet = lax.all_to_all(packet, ("y", "x"), 0, 0, tiled=True)
    packet = packet.reshape(ny, nx, share, part + LANE).sum(axis=1)
    dh_share = jnp.concatenate([packet[i, :, :part] for i in range(ny)], axis=1)
    score_share = packet[0, :, part : part + top]

    start = (y * nx + x) * share
    cut = lambda v: lax.dynamic_slice_in_dim(v, start, share, 0)
    sig, total, weight, select = cut(sig), cut(total), cut(weight), cut(select)
    wide = cut(acts).astype(f32)
    g = cut(cotangent).astype(f32)
    sent = weight.astype(bf16).astype(f32)
    score_share = jnp.where(sent > 0.0, score_share / jnp.where(sent > 0.0, sent, 1.0), 0.0)
    dsig = (score_share - jnp.sum(weight * score_share, axis=1, keepdims=True)) / total
    dpick = dsig * sig * (1.0 - sig)
    dlogits = jnp.sum(dpick[:, :, None] * select, axis=1)
    dh_total = dh_share + lax.dot_general(
        dlogits, router.astype(f32), (((1,), (1,)), ((), ())), precision=lax.Precision.HIGHEST
    )
    recip = lax.rsqrt(jnp.mean(wide * wide, axis=-1, keepdims=True) + eps)
    scaled = dh_total * gain
    pulled = recip * scaled - wide * (recip * recip * recip) * jnp.mean(
        wide * scaled, axis=-1, keepdims=True
    )
    return (g + pulled)[None]


def solution(mesh):
    pipe, expert = mesh.devices.shape
    grid = Mesh(
        mesh.devices.reshape(pipe // X, X, expert // CORES, CORES), ("y", "x", "z", "core")
    )
    exp, pipe = ("z", "core"), ("y", "x")
    in_specs = (
        P(exp, None),
        P(exp, None),
        P(),
        P(),
        P(exp, None),
        P(exp, None, pipe),
        P(exp, None, pipe),
        P(exp, pipe, None),
    )
    return jax.shard_map(
        shards, mesh=grid, in_specs=in_specs, out_specs=P(pipe, exp, None), check_vma=False
    )
```

time: 204 us -> 191 us (0.936)
  waiting for transfers between devices: 108 us -> 89.8 us
  blocking collectives: 21.5 us -> 27.2 us
    ppermute x4 -> x2, waiting for transfers between devices: 73.2 us -> 9.34 us  [the longest x1 5.69 us: shards(): second = lax.ppermute(first, 'core', [(0, 1), (1, 0)])]
    all_gather x1, waiting for transfers between devices: 0.01 us -> 30.7 us  [shards(): gathered = lax.all_gather(rows, 'y')]
    all_to_all x1, waiting for transfers between devices: 24.2 us -> 39.4 us  [shards(): lax.all_to_all(back.reshape(ny * nz, rank, LANE), ('y', 'z'), 0, 0, tiled...]
    ppermute x4 -> x2, starting transfers between devices: 13.2 us -> 6.55 us  [the longest x1 4.63 us: shards(): swapped = lax.ppermute(mine, ('x', 'core'), pairs)]
    all_to_all x1, blocking collectives: 21.5 us -> 27.2 us  [shards(): lax.all_to_all(rows.reshape(nz, rank, 2 * part), 'z', 0, 0, tiled=True)]
    all_to_all x1, starting transfers between devices: 5.81 us -> 11.4 us  [shards(): packet = lax.all_to_all(packet, ('y', 'x'), 0, 0, tiled=True)]
    select_n x0 -> x1, other arithmetic: none -> 2.97 us  [shards(): first = jnp.where(core == parity, mine, swapped)]
    all_to_all x1, starting transfers between devices: 7.84 us -> 10.7 us  [shards(): lax.all_to_all(back.reshape(ny * nz, rank, LANE), ('y', 'z'), 0, 0, tiled...]
  transfers between devices with their start and end apart: 7 -> 5, of which waited for: 5 -> 5; matrix products, arithmetic and copies ran while one was open for 2% -> 4% of each run, Pallas kernels for 0% -> 0%
where the time goes in v6:
time: 191 us; the launch traced here: 189 us
  waiting for transfers between devices  89.8 us (47%)
  starting transfers between devices  28.7 us (15%)
  blocking collectives  27.2 us (14%)
  between operations  13.7 us (7%)
  other arithmetic  11.5 us (6%)
  Pallas kernels  10.3 us (5%)
  matrix products  5.03 us (3%)
  local copies, waits for them, and re-layouts  2.86 us (1%)
    all_to_all x1, waiting for transfers between devices, shards(): lax.all_to_all(back.reshape(ny * nz, rank, LANE), ('y', 'z'), 0, 0, tiled...  39.4 us
    all_gather x1, waiting for transfers between devices, shards(): gathered = lax.all_gather(rows, 'y')  30.7 us
    all_to_all x1, blocking collectives, shards(): lax.all_to_all(rows.reshape(nz, rank, 2 * part), 'z', 0, 0, tiled=True)  27.2 us
    all_to_all x1, starting transfers between devices, shards(): packet = lax.all_to_all(packet, ('y', 'x'), 0, 0, tiled=True)  11.4 us
    all_to_all x1, starting transfers between devices, shards(): lax.all_to_all(back.reshape(ny * nz, rank, LANE), ('y', 'z'), 0, 0, tiled...  10.7 us
    all_to_all x1, waiting for transfers between devices, shards(): packet = lax.all_to_all(packet, ('y', 'x'), 0, 0, tiled=True)  10.4 us
    pallas_call x1, Pallas kernels, expert_rows(): pl.pallas_call(functools.partial(expert_kernel, cap, nz), out_shape=jax.S...  10.3 us
    ppermute x1, waiting for transfers between devices, shards(): second = lax.ppermute(first, 'core', [(0, 1), (1, 0)])  5.69 us
  transfers between devices with their start and end apart: 5, of which 5 were waited for; matrix products, arithmetic and copies ran while one was open for 4% of the time, Pallas kernels for 0%

profile of v6, /device:TPU:1, one launch (start us, length us, event | category | flops | bytes accessed | tf_op | source)
XLA Modules:
  0.0 189.2 jit_solution(16537927734220394140)
XLA Ops:
  6.5 3.9 %pad_maximum_fusion = bf16[3,168,3072]{2,1,0:T(8,128)(2,1)} fusion(bf16[1,168,3072]{2,1,0:T(8,128)(2,1)} %param.17, bf16[1,168,3072]{2,1,0:T(8,128)(2,1)} %bitcast.89, bf16[1,168,3072]{2,1,0:T(8,128)(2,1)} %bitcast.91), kind=kLoop, calls=%fused_computation.2 | loop fusion | flops 3096576 | bytes 6193152 | tf_op jit(solution)/shard_map/stack | solution.py:165
  10.5 4.6 %collective-permute-start = (bf16[3,168,3072]{2,1,0:T(8,128)(2,1)}, bf16[3,168,3072]{2,1,0:T(8,128)(2,1)}, u32[]{:S(2)}, u32[]{:S(2)}) collective-permute-start(bf16[3,168,3072]{2,1,0:T(8,128)(2,1)} %pad_maximum_fusion), channel_id=1, source_target_pairs={{1,16},{16,1},{33,48},{48,33},{3,18},{18,3},{35,50},{50,35},{5,20}... | collective-permute-start | bytes 9289736 | tf_op jit(solution)/shard_map/ppermute | solution.py:170
  15.7 0.3 fusion.27
  16.9 1.1 convolution_convert_fusion
  18.1 27.2 %all_to_all.15 = bf16[8,40,768]{2,1,0:T(8,128)(2,1)S(1)} all-to-all(bf16[8,40,768]{2,1,0:T(8,128)(2,1)S(1)} %bitcast.94), channel_id=1, replica_groups=mesh['y'=8,'x'=4,'z'=8,'core'=2] {'z'}, dimensions={0} | all-to-all | bytes 983040 | tf_op jit(solution)/shard_map/all_to_all | solution.py:188
  45.3 0.9 all_gather_reshape.3
  46.2 3.7 %collective-permute-done = bf16[3,168,3072]{2,1,0:T(8,128)(2,1)} collective-permute-done((bf16[3,168,3072]{2,1,0:T(8,128)(2,1)}, bf16[3,168,3072]{2,1,0:T(8,128)(2,1)}, u32[]{:S(2)}, u32[]{:S(2)}) %collective-permute-start) | collective-permute-done | bytes 3096608 | tf_op jit(solution)/shard_map/ppermute | solution.py:170
  49.8 3.0 %broadcast_select_fusion.first = bf16[3,168,3072]{2,1,0:T(8,128)(2,1)S(1)} fusion(bf16[3,168,3072]{2,1,0:T(8,128)(2,1)} %collective-permute-done, pred[]{:T(512)S(6)} %eq.138, bf16[1,168,3072]{2,1,0:T(8,128)(2,1)} %param.17, bf16[1,168,3072]{2,1,0:T(8,128)(2,1)} %bitcast.90, bf16[1,168,3072]{2,1,0:T(8,128)(2,1)} %bitcast.92), kind=kLoop, calls=%fused_computation.3 | loop fusion | flops 4644864 | bytes 9289729 | tf_op jit(solution)/shard_map/jit(_where)/select_n | solution.py:171
  52.8 1.9 %collective-permute-start.1 = (bf16[3,168,3072]{2,1,0:T(8,128)(2,1)S(1)}, bf16[3,168,3072]{2,1,0:T(8,128)(2,1)}, u32[]{:S(2)}, u32[]{:S(2)}) collective-permute-start(bf16[3,168,3072]{2,1,0:T(8,128)(2,1)S(1)} %broadcast_select_fusion.first), channel_id=1, source_target_pairs={{0,1},{1,0},{2,3},{3,2},{4,5},{5,4},{6,7},{7,6},{8,9},{9,8},{10,11... | collective-permute-start | bytes 9289736 | tf_op jit(solution)/shard_map/ppermute | solution.py:172
  54.8 5.7 %collective-permute-done.1.second = bf16[3,168,3072]{2,1,0:T(8,128)(2,1)} collective-permute-done((bf16[3,168,3072]{2,1,0:T(8,128)(2,1)S(1)}, bf16[3,168,3072]{2,1,0:T(8,128)(2,1)}, u32[]{:S(2)}, u32[]{:S(2)}) %collective-permute-start.1) | collective-permute-done | bytes 3096608 | tf_op jit(solution)/shard_map/ppermute | solution.py:172
  60.4 30.7 %all-gather.2.cloned.1.call-done.rows_hbm = bf16[8,272,768]{2,1,0:T(8,128)(2,1)} async-done(((bf16[1,272,768]{2,1,0:T(8,128)(2,1)}), bf16[8,272,768]{2,1,0:T(8,128)(2,1)}) %all-gather.2.cloned.1.call-update) | async-done | bytes 3342352 | tf_op jit(solution)/shard_map/all_gather | solution.py:190
  91.1 10.3 %shard_map.82 = bf16[8,8,104,128]{3,2,1,0:T(8,128)(2,1)} custom-call(bf16[8,272,768]{2,1,0:T(8,128)(2,1)} %all-gather.2.cloned.1.call-done.rows_hbm, bf16[3,168,3072]{2,1,0:T(8,128)(2,1)} %copy-done.1, bf16[3,168,3072]{2,1,0:T(8,128)(2,1)} %collective-permute-done.1.second), custom_call_target="tpu_custom_call" | custom-call | flops 2807562240 | bytes 11206656 | tf_op jit(solution)/shard_map/pallas_call | solution.py:132
  101.5 10.7 %all-to-all-start.1 = ((bf16[64,104,128]{2,1,0:T(8,128)(2,1)}), bf16[64,104,128]{2,1,0:T(8,128)(2,1)S(1)}, u32[]{:S(2)}, u32[]{:S(2)}) async-start(bf16[64,104,128]{2,1,0:T(8,128)(2,1)} %bitcast.85), calls=%async_computation.1 | async-start | bytes 3407872 | tf_op jit(solution)/shard_map/all_to_all | solution.py:196
  112.2 0.6 compare_reduce_fusion.1
  113.0 39.4 %all-to-all-done.1 = bf16[64,104,128]{2,1,0:T(8,128)(2,1)S(1)} async-done(((bf16[64,104,128]{2,1,0:T(8,128)(2,1)}), bf16[64,104,128]{2,1,0:T(8,128)(2,1)S(1)}, u32[]{:S(2)}, u32[]{:S(2)}) %all-to-all-start.1) | async-done | bytes 1703968 | tf_op jit(solution)/shard_map/all_to_all | solution.py:196
  153.0 0.7 fusion.30
  153.9 0.7 fusion.29
  154.9 0.7 fusion.28
  155.5 0.7 broadcast_select_fusion.1
  156.4 0.8 reshape.148
  157.1 11.4 %all-to-all-start.2 = ((f32[32,4,512]{2,1,0:T(4,128)}), f32[32,4,512]{2,1,0:T(4,128)S(1)}, u32[]{:S(2)}, u32[]{:S(2)}) async-start(f32[32,4,512]{2,1,0:T(4,128)} %reshape.148), calls=%async_computation.2 | async-start | bytes 524288 | tf_op jit(solution)/shard_map/all_to_all | solution.py:218
  168.7 10.4 %all-to-all-done.2 = f32[32,4,512]{2,1,0:T(4,128)S(1)} async-done(((f32[32,4,512]{2,1,0:T(4,128)}), f32[32,4,512]{2,1,0:T(4,128)S(1)}, u32[]{:S(2)}, u32[]{:S(2)}) %all-to-all-start.2) | async-done | bytes 262176 | tf_op jit(solution)/shard_map/all_to_all | solution.py:218
  179.6 1.2 fusion.10
  180.8 1.5 fusion.14
  (58 shorter events, 3.4 us)
Async XLA Ops:
  6.5 9.1 %copy-start = (bf16[3072,16]{0,1:T(8,128)(2,1)S(1)}, bf16[3072,16]{0,1:T(8,128)(2,1)}, u32[]{:S(2)}) copy-start(bf16[3072,16]{0,1:T(8,128)(2,1)} %param.13) | copy-start | bytes 294916
  6.5 84.6 %all-gather.2.cloned.1.call-start = ((), (), s32[]{:S(2)}) async-start(), calls=%async_computation.3 | async-start | bytes 3760128 | tf_op jit(solution)/shard_map/all_gather | solution.py:190
  6.5 8.6 %copy-start.2 = (bf16[128,3072]{1,0:T(8,128)(2,1)S(1)}, bf16[128,3072]{1,0:T(8,128)(2,1)}, u32[]{:S(2)}) copy-start(bf16[128,3072]{1,0:T(8,128)(2,1)} %param.10) | copy-start | bytes 2359300
  6.5 8.9 %copy-start.4 = (f32[3072]{0:T(1024)S(1)}, f32[3072]{0:T(1024)}, u32[]{:S(2)}) copy-start(f32[3072]{0:T(1024)} %param.12) | copy-start | bytes 36868
  10.5 5.5 %copy-start.3 = (s32[128,4]{0,1:T(4,128)S(1)}, s32[128,4]{0,1:T(4,128)}, u32[]{:S(2)}) copy-start(s32[128,4]{0,1:T(4,128)} %param.14) | copy-start | bytes 6148
  10.5 39.4 %collective-permute-start = (bf16[3,168,3072]{2,1,0:T(8,128)(2,1)}, bf16[3,168,3072]{2,1,0:T(8,128)(2,1)}, u32[]{:S(2)}, u32[]{:S(2)}) collective-permute-start(bf16[3,168,3072]{2,1,0:T(8,128)(2,1)} %pad_maximum_fusion), channel_id=1, source_target_pairs={{1,16},{16,1},{33,48},{48,33},{3,18},{18,3},{35,50},{50,35},{5,20}... | collective-permute-start | bytes 9289736 | tf_op jit(solution)/shard_map/ppermute | solution.py:170
  52.8 38.3 %copy-start.1 = (bf16[3,168,3072]{2,1,0:T(8,128)(2,1)}, bf16[3,168,3072]{2,1,0:T(8,128)(2,1)S(1)}, u32[]{:S(2)}) copy-start(bf16[3,168,3072]{2,1,0:T(8,128)(2,1)S(1)} %broadcast_select_fusion.first) | copy-start | bytes 9289732
  52.8 7.6 %collective-permute-start.1 = (bf16[3,168,3072]{2,1,0:T(8,128)(2,1)S(1)}, bf16[3,168,3072]{2,1,0:T(8,128)(2,1)}, u32[]{:S(2)}, u32[]{:S(2)}) collective-permute-start(bf16[3,168,3072]{2,1,0:T(8,128)(2,1)S(1)} %broadcast_select_fusion.first), channel_id=1, source_target_pairs={{0,1},{1,0},{2,3},{3,2},{4,5},{5,4},{6,7},{7,6},{8,9},{9,8},{10,11... | collective-permute-start | bytes 9289736 | tf_op jit(solution)/shard_map/ppermute | solution.py:172
  101.5 50.9 %all-to-all-start.1 = ((bf16[64,104,128]{2,1,0:T(8,128)(2,1)}), bf16[64,104,128]{2,1,0:T(8,128)(2,1)S(1)}, u32[]{:S(2)}, u32[]{:S(2)}) async-start(bf16[64,104,128]{2,1,0:T(8,128)(2,1)} %bitcast.85), calls=%async_computation.1 | async-start | bytes 3407872 | tf_op jit(solution)/shard_map/all_to_all | solution.py:196
  157.1 22.0 %all-to-all-start.2 = ((f32[32,4,512]{2,1,0:T(4,128)}), f32[32,4,512]{2,1,0:T(4,128)S(1)}, u32[]{:S(2)}, u32[]{:S(2)}) async-start(f32[32,4,512]{2,1,0:T(4,128)} %reshape.148), calls=%async_computation.2 | async-start | bytes 524288 | tf_op jit(solution)/shard_map/all_to_all | solution.py:218
Sparse Core Ops, SparseCore 0:
  46.3 44.7 all-gather.1

commit v7 on v6

v7 whole, which is shorter than its diff:
```python
import functools
import jax
import jax.numpy as jnp
from jax import lax
from jax.experimental import pallas as pl
from jax.experimental.pallas import tpu as pltpu
from jax.sharding import Mesh, PartitionSpec as P

eps = 1e-05
X = 4
CORES = 2
LANE = 128
MAIN = 16
bf16 = jnp.bfloat16
f32 = jnp.float32


def token_weights(acts, gain, router, ids):
    wide = acts.astype(f32)
    recip = lax.rsqrt(jnp.mean(wide * wide, axis=-1, keepdims=True) + eps)
    h = (wide * recip * gain).astype(bf16)
    logits = jnp.dot(h, router, preferred_element_type=f32)
    experts = router.shape[1]
    select = (ids[:, :, None] == jnp.arange(experts, dtype=jnp.int32)[None, None, :]).astype(f32)
    picked = jnp.sum(select * logits[:, None, :], axis=-1)
    sig = jax.nn.sigmoid(picked)
    total = jnp.sum(sig, axis=1, keepdims=True)
    return h, sig, total, sig / total, select


def places(ids, names):
    tokens = ids.shape[0]
    member = jnp.any(ids[:, :, None] == names[None, None, :], axis=1)
    below = (jnp.arange(tokens)[:, None] > jnp.arange(tokens)[None, :]).astype(bf16)
    place = jnp.dot(below, member.astype(bf16), preferred_element_type=f32).astype(jnp.int32)
    return jnp.where(member, place, -4096).T


def at_rows(place, count):
    return place[:, None, :] == jnp.arange(count, dtype=jnp.int32)[None, :, None]


def expert_kernel(nz, info, rows_hbm, others_hbm, *refs):
    mine, (across, left, right, keep_ref, give_ref) = refs[:3], refs[3:8]
    h_ref, g_ref, e_ref, w_ref, row_sem, w_sem = refs[8:]
    ny, rank, lane = keep_ref.shape[0], keep_ref.shape[2], keep_ref.shape[3]
    width = h_ref.shape[2]
    part, fold = width // ny, e_ref.shape[2]
    pieces = part // lane
    count = 2 * nz * MAIN
    contract = (((1,), (1,)), ((), ()))
    own = info[0]
    left, right, across = ([ref.at[j] for j in range(3)] for ref in (left, right, across))

    def fetch(u, j, source):
        return pltpu.make_async_copy(source[j], w_ref.at[u, j], w_sem.at[u, j])

    def start(u, j, if_own, other):
        @pl.when(own == 1)
        def _():
            fetch(u, j, if_own).start()

        @pl.when(own == 0)
        def _():
            fetch(u, j, other).start()

    def begin(copies):
        for copy in copies:
            copy.start()

    def end(copies):
        for copy in copies:
            copy.wait()

    rows = []
    for j, (ref, first, size) in enumerate(
        ((h_ref, 0, width), (g_ref, width, width), (e_ref, 2 * width, fold))
    ):
        rows.append(
            [
                pltpu.make_async_copy(
                    source.at[:, :, pl.ds(first, size)],
                    ref.at[pl.ds(k * nz, nz)],
                    row_sem.at[j, k],
                )
                for k, source in enumerate((rows_hbm, others_hbm))
            ]
        )
    begin(rows[0] + rows[2])
    start(0, 0, mine, left)
    start(0, 1, mine, left)
    end(rows[0] + rows[2])
    begin(rows[1])
    start(0, 2, mine, left)
    half = MAIN // 2
    for i in range(half):
        band = pl.ds(i * fold, fold)
        h_ref[2 * nz, : 2 * nz, band] = e_ref[:, i, :]
    h = h_ref[...].reshape(count + MAIN, width)

    def times(u, j, value):
        return lax.dot_general(value, w_ref[u, j], contract, preferred_element_type=f32)

    a, b, dact = [None, None], [None, None], [None, None]
    fetch(0, 0, mine).wait()
    a[0] = times(0, 0, h)
    fetch(0, 1, mine).wait()
    start(1, 0, across, right)
    start(1, 1, across, right)
    b[0] = times(0, 1, h)
    end(rows[1])
    for i in range(half):
        band = pl.ds(i * fold, fold)
        g_ref[2 * nz, : 2 * nz, band] = e_ref[:, half + i, :]
    g = g_ref[...].reshape(count + MAIN, width)
    fetch(0, 2, mine).wait()
    start(1, 2, across, right)
    dact[0] = times(0, 2, g)
    fetch(1, 0, mine).wait()
    a[1] = times(1, 0, h)
    fetch(1, 1, mine).wait()
    b[1] = times(1, 1, h)
    fetch(1, 2, mine).wait()
    dact[1] = times(1, 2, g)
    score = 0.0
    pulls = []
    for u in range(2):
        sg = jax.nn.sigmoid(a[u])
        sa = a[u] * sg
        act = (sa * b[u]).astype(bf16).astype(f32)
        score = score + jnp.sum(act * dact[u], axis=1, keepdims=True)
        pulls.append((dact[u] * b[u] * sg * (1.0 + a[u] * (1.0 - sg))).astype(bf16))
        pulls.append((dact[u] * sa).astype(bf16))
    lanes = lax.broadcasted_iota(jnp.int32, (MAIN, lane), 1)
    eye = lanes == lax.broadcasted_iota(jnp.int32, (MAIN, lane), 0)
    last = lax.broadcasted_iota(jnp.int32, (1, lane), 1) == MAIN
    gap = jnp.zeros((2, lane), f32)
    over = rank - pieces * (MAIN + 1) - 4
    rest = [jnp.zeros((over, lane), f32)] if over else []
    tails = []
    for n in range(2 * nz):
        line = jnp.where(eye, score[n * MAIN : (n + 1) * MAIN], 0.0)
        line = jnp.sum(line, axis=0, keepdims=True)
        line = line + jnp.where(last, score[count + n : count + n + 1], 0.0)
        high = line.astype(bf16).astype(f32)
        pair = [high, line - high]
        tails.append((pair + [gap] if n < nz else [gap] + pair) + rest)
    for i in range(ny):
        band = pl.ds(i * part, part)
        dh = 0.0
        for u in range(2):
            for j in range(2):
                dh = dh + jnp.dot(pulls[2 * u + j], w_ref[u, j, :, band], preferred_element_type=f32)
        for n in range(2 * nz):
            ref = keep_ref if n < nz else give_ref
            for p in range(pieces):
                cut = slice(p * lane, (p + 1) * lane)
                main = dh[n * MAIN : (n + 1) * MAIN, cut]
                ref[i, n % nz, p * MAIN : (p + 1) * MAIN] = main.astype(ref.dtype)
            end_rows = [
                dh[count + n : count + n + 1, p * lane : (p + 1) * lane] for p in range(pieces)
            ]
            ref[i, n % nz, pieces * MAIN :] = jnp.concatenate(end_rows + tails[n], axis=0).astype(
                ref.dtype
            )


def expert_rows(info, rows, others, slices, ny, rank):
    nz = rows.shape[0]
    kinds, hidden, width = slices[-1].shape
    hbm = pl.BlockSpec(memory_space=pl.ANY)
    vmem = pl.BlockSpec(memory_space=pltpu.VMEM)
    count = (2 * nz + 1) * MAIN
    return pl.pallas_call(
        functools.partial(expert_kernel, nz),
        out_shape=(
            jax.ShapeDtypeStruct((ny, nz, rank, LANE), f32),
            jax.ShapeDtypeStruct((ny, nz, rank, LANE), bf16),
        ),
        in_specs=[pl.BlockSpec(memory_space=pltpu.SMEM)] + [hbm] * 8,
        out_specs=(vmem, vmem),
        scratch_shapes=[
            pltpu.VMEM((2 * nz + 1, MAIN, width), bf16),
            pltpu.VMEM((2 * nz + 1, MAIN, width), bf16),
            pltpu.VMEM((2 * nz, MAIN, 2 * width // MAIN), bf16),
            pltpu.VMEM((2, kinds, hidden, width), bf16),
            pltpu.SemaphoreType.DMA((3, 2)),
            pltpu.SemaphoreType.DMA((2, 3)),
        ],
        compiler_params=pltpu.CompilerParams(vmem_limit_bytes=56 * 1024 * 1024),
        cost_estimate=pl.CostEstimate(
            flops=20 * count * width * hidden,
            bytes_accessed=2 * (4 * count * width + 6 * width * hidden),
            transcendentals=2 * count * hidden,
        ),
    )(info, rows, others, *slices)


def shards(acts, cotangent, gain, router, ids, w_gate, w_up, w_down):
    ny, nx, nz, nc = (lax.axis_size(n) for n in ("y", "x", "z", "core"))
    y, x, core = (lax.axis_index(n) for n in ("y", "x", "core"))
    tokens, width = acts.shape
    top = ids.shape[1]
    experts = nz * nc
    cap = min(tokens, (17 * tokens * top + 16 * experts - 1) // (16 * experts))
    cap = -(-cap // 2)
    assert cap == MAIN + 1 and 2 * nz <= MAIN and ny % 2 == 0
    part = width // ny
    parity = x % 2
    swap = [(0, 1), (1, 0)]

    mine_parts = (w_gate[0].T, w_up[0].T, w_down[0])
    mine = jnp.stack(mine_parts)
    ahead, behind, beside = [], [], []
    for j in range(ny):
        for i in range(nx):
            a = i % 2
            at = lambda yy, xx, cc: (yy * nx + xx % nx) * nc + cc
            ahead.append((at(j, i, 1 - a), at(j, i + 1, a)))
            behind.append((at(j, i, 1 - a), at(j, i - 1, a)))
            beside.append((at(j, i, a), at(j ^ 1, i, a)))
    left = lax.ppermute(mine, ("y", "x", "core"), behind)
    right = lax.ppermute(mine, ("y", "x", "core"), ahead)
    across = lax.ppermute(mine, ("y", "x", "core"), beside)
    info = (core == parity).astype(jnp.int32).reshape(1)

    h, sig, total, weight, select = token_weights(acts, gain, router, ids)
    names = 2 * jnp.arange(nz, dtype=jnp.int32) + parity
    place = places(ids, names)
    halves = [
        jnp.where((place >= n * cap) & (place < (n + 1) * cap), place - n * cap, -4096)
        for n in (0, 1)
    ]
    odd = (x // 2 + y) % 2 == 1
    here = jnp.where(odd, halves[1], halves[0])
    of_name = (ids[:, :, None] == names[None, None, :]).astype(f32)
    dense = jnp.sum(of_name * weight[:, :, None], axis=1).astype(bf16).T

    def picked(scale, values):
        main = (at_rows(here, MAIN).astype(bf16) * scale[:, None, :]).reshape(nz * MAIN, tokens)
        extra = (here == MAIN).astype(bf16) * scale
        main = jnp.dot(main, values, preferred_element_type=f32).astype(bf16)
        extra = jnp.dot(extra, values, preferred_element_type=f32).astype(bf16)
        return main.reshape(nz, MAIN, width), extra.reshape(nz, MAIN // 2, 2 * width // MAIN)

    h_main, h_extra = picked(jnp.ones_like(dense), h)
    dy_main, dy_extra = picked(dense, cotangent)
    extra = jnp.concatenate([h_extra, dy_extra], axis=1)
    rows = jnp.concatenate([h_main, dy_main, extra], axis=2)
    rows = lax.all_to_all(rows, "z", 0, 0, tiled=True)
    others = lax.ppermute(rows, "core", swap)

    pieces = part // LANE
    rank = -(-(pieces * cap + 4) // 8) * 8
    keep, give = expert_rows(info, rows, others, (*mine_parts, across, left, right), ny, rank)
    got = lax.ppermute(give, "core", swap)
    back = (keep + got.astype(f32)).astype(bf16)

    back = lax.all_to_all(back.reshape(ny * nz, rank, LANE), ("y", "z"), 0, 0, tiled=True)
    flat = back.reshape(ny * nz * rank, LANE)
    by_y = [jnp.where(x // 2 % 2 == 1, halves[1 - n], halves[n]) for n in (0, 1)]
    parts = []
    for p in range(pieces):
        spread = []
        for slot in by_y:
            row = jnp.where(slot == MAIN, pieces * MAIN + p, slot + p * MAIN)
            spread.append(at_rows(jnp.where(slot >= 0, row, -1), rank).astype(bf16))
        spread = jnp.broadcast_to(jnp.stack(spread)[None], (ny // 2, 2, nz, rank, tokens))
        parts.append(
            lax.dot_general(
                spread.reshape(ny * nz * rank, tokens),
                flat,
                (((0,), (0,)), ((), ())),
                preferred_element_type=f32,
            )
        )
    score = jnp.sum(back[:, pieces * cap : pieces * cap + 4, :cap].astype(f32), axis=1)
    score = score.reshape(ny // 2, 2, nz, cap).sum(axis=0)
    slots = jnp.stack([at_rows(slot, cap) for slot in by_y]).astype(f32)
    score = jnp.sum(slots * score[:, :, :, None], axis=(0, 2))
    score = jnp.sum(of_name * score.T[:, None, :], axis=-1)
    sections = ny * nx
    share = tokens // sections
    tail = jnp.zeros((tokens, LANE), f32).at[:, :top].set(score)
    packet = jnp.concatenate(parts + [tail], axis=1).reshape(sections, share, part + LANE)
    packet = lax.all_to_all(packet, ("y", "x"), 0, 0, tiled=True)
    packet = packet.reshape(ny, nx, share, part + LANE).sum(axis=1)
    dh_share = jnp.concatenate([packet[i, :, :part] for i in range(ny)], axis=1)
    score_share = packet[0, :, part : part + top]

    start = (y * nx + x) * share
    cut = lambda v: lax.dynamic_slice_in_dim(v, start, share, 0)
    sig, total, weight, select = cut(sig), cut(total), cut(weight), cut(select)
    wide = cut(acts).astype(f32)
    g = cut(cotangent).astype(f32)
    sent = weight.astype(bf16).astype(f32)
    score_share = jnp.where(sent > 0.0, score_share / jnp.where(sent > 0.0, sent, 1.0), 0.0)
    dsig = (score_share - jnp.sum(weight * score_share, axis=1, keepdims=True)) / total
    dpick = dsig * sig * (1.0 - sig)
    dlogits = jnp.sum(dpick[:, :, None] * select, axis=1)
    dh_total = dh_share + lax.dot_general(
        dlogits, router.astype(f32), (((1,), (1,)), ((), ())), precision=lax.Precision.HIGHEST
    )
    recip = lax.rsqrt(jnp.mean(wide * wide, axis=-1, keepdims=True) + eps)
    scaled = dh_total * gain
    pulled = recip * scaled - wide * (recip * recip * recip) * jnp.mean(
        wide * scaled, axis=-1, keepdims=True
    )
    return (g + pulled)[None]


def solution(mesh):
    pipe, expert = mesh.devices.shape
    grid = Mesh(
        mesh.devices.reshape(pipe // X, X, expert // CORES, CORES), ("y", "x", "z", "core")
    )
    exp, pipe = ("z", "core"), ("y", "x")
    in_specs = (
        P(exp, None),
        P(exp, None),
        P(),
        P(),
        P(exp, None),
        P(exp, None, pipe),
        P(exp, None, pipe),
        P(exp, pipe, None),
    )
    return jax.shard_map(
        shards, mesh=grid, in_specs=in_specs, out_specs=P(pipe, exp, None), check_vma=False
    )
```

time: 191 us -> 153 us (0.80)
  blocking collectives: 27.2 us -> 0 us
  waiting for transfers between devices: 89.8 us -> 71.8 us
  starting transfers between devices: 28.7 us -> 43.9 us
  between operations: 13.7 us -> 0.49 us
  other arithmetic: 11.5 us -> 14 us
    all_gather x1 -> x0, waiting for transfers between devices: 30.7 us -> none  [shards(): gathered = lax.all_gather(rows, 'y')]
    all_to_all x0 -> x1, waiting for transfers between devices: none -> 29.6 us  [shards(): rows = lax.all_to_all(rows, 'z', 0, 0, tiled=True)]
    all_to_all x1 -> x0, blocking collectives: 27.2 us -> none  [shards(): lax.all_to_all(rows.reshape(nz, rank, 2 * part), 'z', 0, 0, tiled=True)]
    all_to_all x1, waiting for transfers between devices: 39.4 us -> 23.6 us  [shards(): lax.all_to_all(back.reshape(ny * nz, rank, LANE), ('y', 'z'), 0, 0, tiled...]
    all_to_all x0 -> x1, starting transfers between devices: none -> 11 us  [shards(): rows = lax.all_to_all(rows, 'z', 0, 0, tiled=True)]
    ppermute x2 -> x5, starting transfers between devices: 6.55 us -> 13.8 us  [the longest x1 5.22 us: shards(): left = lax.ppermute(mine, ('y', 'x', 'core'), behind)]
    all_to_all x1, starting transfers between devices: 11.4 us -> 5.82 us  [shards(): packet = lax.all_to_all(packet, ('y', 'x'), 0, 0, tiled=True)]
    select_n x1, other arithmetic: 2.97 us -> 0.01 us  [shards(): spread.append(at_rows(jnp.where(slot >= 0, row, -1), rank).astype(bf16))]
  transfers between devices with their start and end apart: 5 -> 8, of which waited for: 5 -> 5; matrix products, arithmetic and copies ran while one was open for 4% -> 3% of each run, Pallas kernels for 0% -> 0%
where the time goes in v7:
time: 153 us; the launch traced here: 151 us
  waiting for transfers between devices  71.8 us (47%)
  starting transfers between devices  43.9 us (29%)
  other arithmetic  14 us (9%)
  Pallas kernels  12.2 us (8%)
  matrix products  5.59 us (4%)
  local copies, waits for them, and re-layouts  2.9 us (2%)
    all_to_all x1, waiting for transfers between devices, shards(): rows = lax.all_to_all(rows, 'z', 0, 0, tiled=True)  29.6 us
    all_to_all x1, waiting for transfers between devices, shards(): lax.all_to_all(back.reshape(ny * nz, rank, LANE), ('y', 'z'), 0, 0, tiled...  23.6 us
    all_to_all x1, starting transfers between devices, shards(): lax.all_to_all(back.reshape(ny * nz, rank, LANE), ('y', 'z'), 0, 0, tiled...  13.4 us
    pallas_call x1, Pallas kernels, expert_rows(): pl.pallas_call(functools.partial(expert_kernel, nz), out_shape=(jax.Shape...  12.2 us
    all_to_all x1, starting transfers between devices, shards(): rows = lax.all_to_all(rows, 'z', 0, 0, tiled=True)  11 us
    all_to_all x1, waiting for transfers between devices, shards(): packet = lax.all_to_all(packet, ('y', 'x'), 0, 0, tiled=True)  10.3 us
    all_to_all x1, starting transfers between devices, shards(): packet = lax.all_to_all(packet, ('y', 'x'), 0, 0, tiled=True)  5.82 us
    ppermute x1, waiting for transfers between devices, shards(): right = lax.ppermute(mine, ('y', 'x', 'core'), ahead)  5.61 us
  transfers between devices with their start and end apart: 8, of which 5 were waited for; matrix products, arithmetic and copies ran while one was open for 3% of the time, Pallas kernels for 0%

profile of v7, /device:TPU:1, one launch (start us, length us, event | category | flops | bytes accessed | tf_op | source)
XLA Modules:
  0.0 151.0 jit_solution(13164366663632135992)
XLA Ops:
  0.1 1.5 fusion.1
  1.6 0.8 compare_reduce_fusion
  2.4 1.5 %fusion.24 = f32[128,16]{0,1:T(8,128)S(1)} fusion(bf16[3072,16]{0,1:T(8,128)(2,1)S(1)} %copy-done, bf16[128,3072]{1,0:T(8,128)(2,1)} %param.10, f32[3072]{0:T(1024)} %param.12, f32[128]{0:T(128)S(1)} %add_rsqrt_fusion), kind=kOutput, calls=%fused_computation.109 | convolution fusion | flops 14155776 | bytes 905728 | tf_op jit(solution)/shard_map/dot_general | solution.py:22
  6.0 1.4 maximum_maximum_fusion
  7.4 11.0 %all-to-all-start = ((bf16[8,16,6528]{2,1,0:T(8,128)(2,1)}), bf16[8,16,6528]{2,1,0:T(8,128)(2,1)S(1)}, u32[]{:S(2)}, u32[]{:S(2)}) async-start(bf16[8,16,6528]{2,1,0:T(8,128)(2,1)} %maximum_maximum_fusion), calls=%async_computation | async-start | bytes 3342336 | tf_op jit(solution)/shard_map/all_to_all | solution.py:250
  18.4 3.5 %pad_maximum_fusion = bf16[3,168,3072]{2,1,0:T(8,128)(2,1)} fusion(bf16[1,168,3072]{2,1,0:T(8,128)(2,1)} %param.17, bf16[1,168,3072]{2,1,0:T(8,128)(2,1)} %bitcast.100, bf16[1,168,3072]{2,1,0:T(8,128)(2,1)S(1)} %bitcast.99), kind=kLoop, calls=%fused_computation.6 | loop fusion | flops 3096576 | bytes 6193152 | tf_op jit(solution)/shard_map/stack | solution.py:213
  21.8 2.3 %collective-permute-start.1 = (bf16[3,168,3072]{2,1,0:T(8,128)(2,1)}, bf16[3,168,3072]{2,1,0:T(8,128)(2,1)}, u32[]{:S(2)}, u32[]{:S(2)}) collective-permute-start(bf16[3,168,3072]{2,1,0:T(8,128)(2,1)} %pad_maximum_fusion), channel_id=1, source_target_pairs={{0,64},{17,81},{32,96},{49,113},{64,0},{81,17},{96,32},{113,49},{1... | collective-permute-start | bytes 9289736 | tf_op jit(solution)/shard_map/ppermute | solution.py:224
  24.2 5.2 %collective-permute-start.2 = (bf16[3,168,3072]{2,1,0:T(8,128)(2,1)}, bf16[3,168,3072]{2,1,0:T(8,128)(2,1)}, u32[]{:S(2)}, u32[]{:S(2)}) collective-permute-start(bf16[3,168,3072]{2,1,0:T(8,128)(2,1)} %pad_maximum_fusion), channel_id=1, source_target_pairs={{1,48},{16,1},{33,16},{48,33},{65,112},{80,65},{97,80},{112,97},{1... | collective-permute-start | bytes 9289736 | tf_op jit(solution)/shard_map/ppermute | solution.py:222
  29.4 1.9 %collective-permute-start.3 = (bf16[3,168,3072]{2,1,0:T(8,128)(2,1)}, bf16[3,168,3072]{2,1,0:T(8,128)(2,1)}, u32[]{:S(2)}, u32[]{:S(2)}) collective-permute-start(bf16[3,168,3072]{2,1,0:T(8,128)(2,1)} %pad_maximum_fusion), channel_id=1, source_target_pairs={{1,16},{16,33},{33,48},{48,1},{65,80},{80,97},{97,112},{112,65},{1... | collective-permute-start | bytes 9289736 | tf_op jit(solution)/shard_map/ppermute | solution.py:223
  31.3 29.6 %all-to-all-done.rows_hbm = bf16[8,16,6528]{2,1,0:T(8,128)(2,1)S(1)} async-done(((bf16[8,16,6528]{2,1,0:T(8,128)(2,1)}), bf16[8,16,6528]{2,1,0:T(8,128)(2,1)S(1)}, u32[]{:S(2)}, u32[]{:S(2)}) %all-to-all-start) | async-done | bytes 1671200 | tf_op jit(solution)/shard_map/all_to_all | solution.py:250
  60.9 2.4 %collective-permute-start = (bf16[8,16,6528]{2,1,0:T(8,128)(2,1)S(1)}, bf16[8,16,6528]{2,1,0:T(8,128)(2,1)S(1)}, u32[]{:S(2)}, u32[]{:S(2)}) collective-permute-start(bf16[8,16,6528]{2,1,0:T(8,128)(2,1)S(1)} %all-to-all-done.rows_hbm), channel_id=1, source_target_pairs={{0,1},{1,0},{2,3},{3,2},{4,5},{5,4},{6,7},{7,6},{8,9},{9,8},{10,11... | collective-permute-start | bytes 5013512 | tf_op jit(solution)/shard_map/ppermute | solution.py:251
  63.4 5.6 %collective-permute-done.3.refs_5_ = bf16[3,168,3072]{2,1,0:T(8,128)(2,1)} collective-permute-done((bf16[3,168,3072]{2,1,0:T(8,128)(2,1)}, bf16[3,168,3072]{2,1,0:T(8,128)(2,1)}, u32[]{:S(2)}, u32[]{:S(2)}) %collective-permute-start.3) | collective-permute-done | bytes 3096608 | tf_op jit(solution)/shard_map/ppermute | solution.py:223
  69.0 1.2 copy-done.5
  70.1 12.2 %shard_map.82 = (f32[8,8,56,128]{3,2,1,0:T(8,128)}, bf16[8,8,56,128]{3,2,1,0:T(8,128)(2,1)}) custom-call(s32[1]{0:T(128)} %bitcast.2.info, bf16[8,16,6528]{2,1,0:T(8,128)(2,1)} %copy-done.1, bf16[8,16,6528]{2,1,0:T(8,128)(2,1)} %copy-done.5, bf16[168,3072]{1,0:T(8,128)(2,1)} %bitcast.98, bf16[168,3072]{1,0:T(8,128)(2,1)} %bitcast.101, ...), custom_call_target="tpu_custom_call" | custom-call | flops 2807562240 | bytes 12877824 | tf_op jit(solution)/shard_map/pallas_call | solution.py:174
  82.3 1.9 %collective-permute-start.4 = (bf16[8,8,56,128]{3,2,1,0:T(8,128)(2,1)}, bf16[8,8,56,128]{3,2,1,0:T(8,128)(2,1)S(1)}, u32[]{:S(2)}, u32[]{:S(2)}) collective-permute-start(bf16[8,8,56,128]{3,2,1,0:T(8,128)(2,1)} %get-tuple-element.20), channel_id=1, source_target_pairs={{0,1},{1,0},{2,3},{3,2},{4,5},{5,4},{6,7},{7,6},{8,9},{9,8},{10,11... | collective-permute-start | bytes 2752520 | tf_op jit(solution)/shard_map/ppermute | solution.py:256
  84.3 2.6 %collective-permute-done.4 = bf16[8,8,56,128]{3,2,1,0:T(8,128)(2,1)S(1)} collective-permute-done((bf16[8,8,56,128]{3,2,1,0:T(8,128)(2,1)}, bf16[8,8,56,128]{3,2,1,0:T(8,128)(2,1)S(1)}, u32[]{:S(2)}, u32[]{:S(2)}) %collective-permute-start.4) | collective-permute-done | bytes 917536 | tf_op jit(solution)/shard_map/ppermute | solution.py:256
  86.9 2.7 %add_convert_fusion = bf16[8,8,56,128]{3,2,1,0:T(8,128)(2,1)} fusion(f32[8,8,56,128]{3,2,1,0:T(8,128)} %get-tuple-element.19, bf16[8,8,56,128]{3,2,1,0:T(8,128)(2,1)S(1)} %collective-permute-done.4), kind=kLoop, calls=%fused_computation.9 | loop fusion | flops 1376256 | bytes 3670016 | tf_op jit(solution)/shard_map/convert_element_type | solution.py:257
  89.6 13.4 %all-to-all-start.1 = ((bf16[64,56,128]{2,1,0:T(8,128)(2,1)}), bf16[64,56,128]{2,1,0:T(8,128)(2,1)S(1)}, u32[]{:S(2)}, u32[]{:S(2)}) async-start(bf16[64,56,128]{2,1,0:T(8,128)(2,1)} %bitcast.17), calls=%async_computation.1 | async-start | bytes 1835008 | tf_op jit(solution)/shard_map/all_to_all | solution.py:259
  104.1 23.6 %all-to-all-done.1 = bf16[64,56,128]{2,1,0:T(8,128)(2,1)S(1)} async-done(((bf16[64,56,128]{2,1,0:T(8,128)(2,1)}), bf16[64,56,128]{2,1,0:T(8,128)(2,1)S(1)}, u32[]{:S(2)}, u32[]{:S(2)}) %all-to-all-start.1) | async-done | bytes 917536 | tf_op jit(solution)/shard_map/all_to_all | solution.py:259
  130.7 0.8 reshape.227
  131.5 5.8 %all-to-all-start.2 = ((f32[32,4,512]{2,1,0:T(4,128)}), f32[32,4,512]{2,1,0:T(4,128)S(1)}, u32[]{:S(2)}, u32[]{:S(2)}) async-start(f32[32,4,512]{2,1,0:T(4,128)} %reshape.227), calls=%async_computation.2 | async-start | bytes 524288 | tf_op jit(solution)/shard_map/all_to_all | solution.py:286
  137.4 10.3 %all-to-all-done.2 = f32[32,4,512]{2,1,0:T(4,128)S(1)} async-done(((f32[32,4,512]{2,1,0:T(4,128)}), f32[32,4,512]{2,1,0:T(4,128)S(1)}, u32[]{:S(2)}, u32[]{:S(2)}) %all-to-all-start.2) | async-done | bytes 262176 | tf_op jit(solution)/shard_map/all_to_all | solution.py:286
  148.2 1.2 fusion.5
  149.4 1.5 %fusion.9 = f32[1,4,3072]{2,1,0:T(4,128)} fusion(f32[4,3072]{1,0:T(4,128)S(1)} %get-tuple-element.40, f32[4]{0:T(128)S(1)} %broadcast_multiply_fusion, f32[4]{0:T(128)S(1)} %get-tuple-element.38, f32[4]{0:T(128)S(1)} %get-tuple-element.37, bf16[128,3072]{1,0:T(8,128)(2,1)} %param.11, s32[]{:T(128)S(6)} %select_n.105, bf16[128,3072]{1,0:T(8,128)(2,1)} %param.10), kind=kLoop, calls=%fused_computation.41 | loop fusion | flops 86016 | bytes 147508 | tf_op jit(solution)/shard_map/broadcast_in_dim | solution.py:309
  (78 shorter events, 6.6 us)
Async XLA Ops:
  0.0 2.4 %copy-start = (bf16[3072,16]{0,1:T(8,128)(2,1)S(1)}, bf16[3072,16]{0,1:T(8,128)(2,1)}, u32[]{:S(2)}) copy-start(bf16[3072,16]{0,1:T(8,128)(2,1)} %param.13) | copy-start | bytes 294916
  0.0 4.5 %copy-start.3 = (bf16[128,3072]{1,0:T(8,128)(2,1)S(1)}, bf16[128,3072]{1,0:T(8,128)(2,1)}, u32[]{:S(2)}) copy-start(bf16[128,3072]{1,0:T(8,128)(2,1)} %param.10) | copy-start | bytes 2359300
  0.0 3.9 %copy-start.6 = (s32[128,4]{0,1:T(4,128)S(1)}, s32[128,4]{0,1:T(4,128)}, u32[]{:S(2)}) copy-start(s32[128,4]{0,1:T(4,128)} %param.14) | copy-start | bytes 6148
  0.0 4.5 %copy-start.7 = (f32[3072]{0:T(1024)S(1)}, f32[3072]{0:T(1024)}, u32[]{:S(2)}) copy-start(f32[3072]{0:T(1024)} %param.12) | copy-start | bytes 36868
  1.6 3.4 %copy-start.4 = (bf16[128,3072]{1,0:T(8,128)(2,1)S(1)}, bf16[128,3072]{1,0:T(8,128)(2,1)}, u32[]{:S(2)}) copy-start(bf16[128,3072]{1,0:T(8,128)(2,1)} %param.11) | copy-start | bytes 2359300
  7.4 11.0 %copy-start.2 = (bf16[1,3072,168]{1,2,0:T(8,128)(2,1)S(1)}, bf16[1,3072,168]{1,2,0:T(8,128)(2,1)}, u32[]{:S(2)}) copy-start(bf16[1,3072,168]{1,2,0:T(8,128)(2,1)} %param.15) | copy-start | bytes 3096580
  7.4 53.5 %all-to-all-start = ((bf16[8,16,6528]{2,1,0:T(8,128)(2,1)}), bf16[8,16,6528]{2,1,0:T(8,128)(2,1)S(1)}, u32[]{:S(2)}, u32[]{:S(2)}) async-start(bf16[8,16,6528]{2,1,0:T(8,128)(2,1)} %maximum_maximum_fusion), calls=%async_computation | async-start | bytes 3342336 | tf_op jit(solution)/shard_map/all_to_all | solution.py:250
  21.8 41.5 %collective-permute-start.1 = (bf16[3,168,3072]{2,1,0:T(8,128)(2,1)}, bf16[3,168,3072]{2,1,0:T(8,128)(2,1)}, u32[]{:S(2)}, u32[]{:S(2)}) collective-permute-start(bf16[3,168,3072]{2,1,0:T(8,128)(2,1)} %pad_maximum_fusion), channel_id=1, source_target_pairs={{0,64},{17,81},{32,96},{49,113},{64,0},{81,17},{96,32},{113,49},{1... | collective-permute-start | bytes 9289736 | tf_op jit(solution)/shard_map/ppermute | solution.py:224
  24.2 39.2 %collective-permute-start.2 = (bf16[3,168,3072]{2,1,0:T(8,128)(2,1)}, bf16[3,168,3072]{2,1,0:T(8,128)(2,1)}, u32[]{:S(2)}, u32[]{:S(2)}) collective-permute-start(bf16[3,168,3072]{2,1,0:T(8,128)(2,1)} %pad_maximum_fusion), channel_id=1, source_target_pairs={{1,48},{16,1},{33,16},{48,33},{65,112},{80,65},{97,80},{112,97},{1... | collective-permute-start | bytes 9289736 | tf_op jit(solution)/shard_map/ppermute | solution.py:222
  29.4 39.6 %collective-permute-start.3 = (bf16[3,168,3072]{2,1,0:T(8,128)(2,1)}, bf16[3,168,3072]{2,1,0:T(8,128)(2,1)}, u32[]{:S(2)}, u32[]{:S(2)}) collective-permute-start(bf16[3,168,3072]{2,1,0:T(8,128)(2,1)} %pad_maximum_fusion), channel_id=1, source_target_pairs={{1,16},{16,33},{33,48},{48,1},{65,80},{80,97},{97,112},{112,65},{1... | collective-permute-start | bytes 9289736 | tf_op jit(solution)/shard_map/ppermute | solution.py:223
  60.9 8.1 %copy-start.1 = (bf16[8,16,6528]{2,1,0:T(8,128)(2,1)}, bf16[8,16,6528]{2,1,0:T(8,128)(2,1)S(1)}, u32[]{:S(2)}) copy-start(bf16[8,16,6528]{2,1,0:T(8,128)(2,1)S(1)} %all-to-all-done.rows_hbm) | copy-start | bytes 5013508
  60.9 8.1 %collective-permute-start = (bf16[8,16,6528]{2,1,0:T(8,128)(2,1)S(1)}, bf16[8,16,6528]{2,1,0:T(8,128)(2,1)S(1)}, u32[]{:S(2)}, u32[]{:S(2)}) collective-permute-start(bf16[8,16,6528]{2,1,0:T(8,128)(2,1)S(1)} %all-to-all-done.rows_hbm), channel_id=1, source_target_pairs={{0,1},{1,0},{2,3},{3,2},{4,5},{5,4},{6,7},{7,6},{8,9},{9,8},{10,11... | collective-permute-start | bytes 5013512 | tf_op jit(solution)/shard_map/ppermute | solution.py:251
  69.0 1.2 copy-start.5
  82.3 4.6 %collective-permute-start.4 = (bf16[8,8,56,128]{3,2,1,0:T(8,128)(2,1)}, bf16[8,8,56,128]{3,2,1,0:T(8,128)(2,1)S(1)}, u32[]{:S(2)}, u32[]{:S(2)}) collective-permute-start(bf16[8,8,56,128]{3,2,1,0:T(8,128)(2,1)} %get-tuple-element.20), channel_id=1, source_target_pairs={{0,1},{1,0},{2,3},{3,2},{4,5},{5,4},{6,7},{7,6},{8,9},{9,8},{10,11... | collective-permute-start | bytes 2752520 | tf_op jit(solution)/shard_map/ppermute | solution.py:256
  89.6 38.1 %all-to-all-start.1 = ((bf16[64,56,128]{2,1,0:T(8,128)(2,1)}), bf16[64,56,128]{2,1,0:T(8,128)(2,1)S(1)}, u32[]{:S(2)}, u32[]{:S(2)}) async-start(bf16[64,56,128]{2,1,0:T(8,128)(2,1)} %bitcast.17), calls=%async_computation.1 | async-start | bytes 1835008 | tf_op jit(solution)/shard_map/all_to_all | solution.py:259
  131.5 16.2 %all-to-all-start.2 = ((f32[32,4,512]{2,1,0:T(4,128)}), f32[32,4,512]{2,1,0:T(4,128)S(1)}, u32[]{:S(2)}, u32[]{:S(2)}) async-start(f32[32,4,512]{2,1,0:T(4,128)} %reshape.227), calls=%async_computation.2 | async-start | bytes 524288 | tf_op jit(solution)/shard_map/all_to_all | solution.py:286

commit v8 on v7

--- a/solution.py
+++ b/solution.py
@@ -41,8 +41,8 @@
 
 
 def expert_kernel(nz, info, rows_hbm, others_hbm, *refs):
-    mine, (across, left, right, keep_ref, give_ref) = refs[:3], refs[3:8]
-    h_ref, g_ref, e_ref, w_ref, row_sem, w_sem = refs[8:]
+    mine, (left, other, keep_hbm, give_hbm) = refs[:3], refs[3:7]
+    h_ref, g_ref, e_ref, w_ref, keep_ref, give_ref, row_sem, w_sem, out_sem = refs[7:]
     ny, rank, lane = keep_ref.shape[0], keep_ref.shape[2], keep_ref.shape[3]
     width = h_ref.shape[2]
     part, fold = width // ny, e_ref.shape[2]
@@ -50,19 +50,19 @@
     count = 2 * nz * MAIN
     contract = (((1,), (1,)), ((), ()))
     own = info[0]
-    left, right, across = ([ref.at[j] for j in range(3)] for ref in (left, right, across))
+    left, other = ([ref.at[j] for j in range(3)] for ref in (left, other))
 
     def fetch(u, j, source):
         return pltpu.make_async_copy(source[j], w_ref.at[u, j], w_sem.at[u, j])
 
-    def start(u, j, if_own, other):
+    def start_first(j):
         @pl.when(own == 1)
         def _():
-            fetch(u, j, if_own).start()
+            fetch(0, j, mine).start()
 
         @pl.when(own == 0)
         def _():
-            fetch(u, j, other).start()
+            fetch(0, j, left).start()
 
     def begin(copies):
         for copy in copies:
@@ -87,11 +87,11 @@
             ]
         )
     begin(rows[0] + rows[2])
-    start(0, 0, mine, left)
-    start(0, 1, mine, left)
+    start_first(0)
+    start_first(1)
     end(rows[0] + rows[2])
     begin(rows[1])
-    start(0, 2, mine, left)
+    start_first(2)
     half = MAIN // 2
     for i in range(half):
         band = pl.ds(i * fold, fold)
@@ -105,8 +105,8 @@
     fetch(0, 0, mine).wait()
     a[0] = times(0, 0, h)
     fetch(0, 1, mine).wait()
-    start(1, 0, across, right)
-    start(1, 1, across, right)
+    fetch(1, 0, other).start()
+    fetch(1, 1, other).start()
     b[0] = times(0, 1, h)
     end(rows[1])
     for i in range(half):
@@ -114,13 +114,13 @@
         g_ref[2 * nz, : 2 * nz, band] = e_ref[:, half + i, :]
     g = g_ref[...].reshape(count + MAIN, width)
     fetch(0, 2, mine).wait()
-    start(1, 2, across, right)
+    fetch(1, 2, other).start()
     dact[0] = times(0, 2, g)
-    fetch(1, 0, mine).wait()
+    fetch(1, 0, other).wait()
     a[1] = times(1, 0, h)
-    fetch(1, 1, mine).wait()
+    fetch(1, 1, other).wait()
     b[1] = times(1, 1, h)
-    fetch(1, 2, mine).wait()
+    fetch(1, 2, other).wait()
     dact[1] = times(1, 2, g)
     score = 0.0
     pulls = []
@@ -145,6 +145,7 @@
         high = line.astype(bf16).astype(f32)
         pair = [high, line - high]
         tails.append((pair + [gap] if n < nz else [gap] + pair) + rest)
+    stores = []
     for i in range(ny):
         band = pl.ds(i * part, part)
         dh = 0.0
@@ -163,13 +164,16 @@
             ref[i, n % nz, pieces * MAIN :] = jnp.concatenate(end_rows + tails[n], axis=0).astype(
                 ref.dtype
             )
+        for j, (ref, hbm) in enumerate(((give_ref, give_hbm), (keep_ref, keep_hbm))):
+            stores.append(pltpu.make_async_copy(ref.at[i], hbm.at[i], out_sem.at[i, j]))
+            stores[-1].start()
+    end(stores)
 
 
 def expert_rows(info, rows, others, slices, ny, rank):
     nz = rows.shape[0]
     kinds, hidden, width = slices[-1].shape
     hbm = pl.BlockSpec(memory_space=pl.ANY)
-    vmem = pl.BlockSpec(memory_space=pltpu.VMEM)
     count = (2 * nz + 1) * MAIN
     return pl.pallas_call(
         functools.partial(expert_kernel, nz),
@@ -177,17 +181,20 @@
             jax.ShapeDtypeStruct((ny, nz, rank, LANE), f32),
             jax.ShapeDtypeStruct((ny, nz, rank, LANE), bf16),
         ),
-        in_specs=[pl.BlockSpec(memory_space=pltpu.SMEM)] + [hbm] * 8,
-        out_specs=(vmem, vmem),
+        in_specs=[pl.BlockSpec(memory_space=pltpu.SMEM)] + [hbm] * 7,
+        out_specs=(hbm, hbm),
         scratch_shapes=[
             pltpu.VMEM((2 * nz + 1, MAIN, width), bf16),
             pltpu.VMEM((2 * nz + 1, MAIN, width), bf16),
             pltpu.VMEM((2 * nz, MAIN, 2 * width // MAIN), bf16),
             pltpu.VMEM((2, kinds, hidden, width), bf16),
+            pltpu.VMEM((ny, nz, rank, LANE), f32),
+            pltpu.VMEM((ny, nz, rank, LANE), bf16),
             pltpu.SemaphoreType.DMA((3, 2)),
             pltpu.SemaphoreType.DMA((2, 3)),
+            pltpu.SemaphoreType.DMA((ny, 2)),
         ],
-        compiler_params=pltpu.CompilerParams(vmem_limit_bytes=56 * 1024 * 1024),
+        compiler_params=pltpu.CompilerParams(vmem_limit_bytes=52 * 1024 * 1024),
         cost_estimate=pl.CostEstimate(
             flops=20 * count * width * hidden,
             bytes_accessed=2 * (4 * count * width + 6 * width * hidden),
@@ -211,17 +218,16 @@
 
     mine_parts = (w_gate[0].T, w_up[0].T, w_down[0])
     mine = jnp.stack(mine_parts)
-    ahead, behind, beside = [], [], []
+    ahead, behind = [], []
     for j in range(ny):
         for i in range(nx):
             a = i % 2
             at = lambda yy, xx, cc: (yy * nx + xx % nx) * nc + cc
             ahead.append((at(j, i, 1 - a), at(j, i + 1, a)))
             behind.append((at(j, i, 1 - a), at(j, i - 1, a)))
-            beside.append((at(j, i, a), at(j ^ 1, i, a)))
+            ahead.append((at(j, i, a), at(j ^ 1, i, a)))
     left = lax.ppermute(mine, ("y", "x", "core"), behind)
-    right = lax.ppermute(mine, ("y", "x", "core"), ahead)
-    across = lax.ppermute(mine, ("y", "x", "core"), beside)
+    other = lax.ppermute(mine, ("y", "x", "core"), ahead)
     info = (core == parity).astype(jnp.int32).reshape(1)
 
     h, sig, total, weight, select = token_weights(acts, gain, router, ids)
@@ -252,7 +258,7 @@
 
     pieces = part // LANE
     rank = -(-(pieces * cap + 4) // 8) * 8
-    keep, give = expert_rows(info, rows, others, (*mine_parts, across, left, right), ny, rank)
+    keep, give = expert_rows(info, rows, others, (*mine_parts, left, other), ny, rank)
     got = lax.ppermute(give, "core", swap)
     back = (keep + got.astype(f32)).astype(bf16)
 
@@ -281,12 +287,17 @@
     score = jnp.sum(of_name * score.T[:, None, :], axis=-1)
     sections = ny * nx
     share = tokens // sections
-    tail = jnp.zeros((tokens, LANE), f32).at[:, :top].set(score)
-    packet = jnp.concatenate(parts + [tail], axis=1).reshape(sections, share, part + LANE)
+    high = score.astype(bf16)
+    low = (score - high.astype(f32)).astype(bf16)
+    tail = jnp.pad(jnp.concatenate([high, low], axis=1), ((0, 0), (0, LANE - 2 * top)))
+    packet = [v.astype(bf16).reshape(sections, share, LANE) for v in parts] + [
+        tail.reshape(sections, share, LANE)
+    ]
+    packet = jnp.stack(packet, axis=1).reshape(sections, (pieces + 1) * share, LANE)
     packet = lax.all_to_all(packet, ("y", "x"), 0, 0, tiled=True)
-    packet = packet.reshape(ny, nx, share, part + LANE).sum(axis=1)
-    dh_share = jnp.concatenate([packet[i, :, :part] for i in range(ny)], axis=1)
-    score_share = packet[0, :, part : part + top]
+    packet = packet.reshape(ny, nx, pieces + 1, share, LANE).astype(f32).sum(axis=1)
+    dh_share = packet[:, :pieces].transpose(2, 0, 1, 3).reshape(share, width)
+    score_share = packet[0, pieces, :, :top] + packet[0, pieces, :, top : 2 * top]
 
     start = (y * nx + x) * share
     cut = lambda v: lax.dynamic_slice_in_dim(v, start, share, 0)

time: 153 us -> 149 us (0.974)
  starting transfers between devices: 43.9 us -> 41.7 us
    ppermute x2 -> x1, starting transfers between devices: 4.23 us -> 1.92 us  [shards(): other = lax.ppermute(mine, ('y', 'x', 'core'), ahead)]
    all_to_all x1, waiting for transfers between devices: 29.6 us -> 31.8 us  [shards(): rows = lax.all_to_all(rows, 'z', 0, 0, tiled=True)]
    ppermute x2 -> x1, waiting for transfers between devices: 5.61 us -> 3.42 us  [shards(): other = lax.ppermute(mine, ('y', 'x', 'core'), ahead)]
  transfers between devices with their start and end apart: 8 -> 7, of which waited for: 5 -> 5; matrix products, arithmetic and copies ran while one was open for 3% -> 3% of each run, Pallas kernels for 0% -> 0%
where the time goes in v8:
time: 149 us; the launch traced here: 147 us
  waiting for transfers between devices  71.3 us (48%)
  starting transfers between devices  41.7 us (28%)
  Pallas kernels  13.7 us (9%)
  other arithmetic  12.9 us (9%)
  matrix products  5.58 us (4%)
  local copies, waits for them, and re-layouts  1.79 us (1%)
    all_to_all x1, waiting for transfers between devices, shards(): rows = lax.all_to_all(rows, 'z', 0, 0, tiled=True)  31.8 us
    all_to_all x1, waiting for transfers between devices, shards(): lax.all_to_all(back.reshape(ny * nz, rank, LANE), ('y', 'z'), 0, 0, tiled...  24.3 us
    pallas_call x1, Pallas kernels, expert_rows(): pl.pallas_call(functools.partial(expert_kernel, nz), out_shape=(jax.Shape...  13.7 us
    all_to_all x1, starting transfers between devices, shards(): lax.all_to_all(back.reshape(ny * nz, rank, LANE), ('y', 'z'), 0, 0, tiled...  13.4 us
    all_to_all x1, starting transfers between devices, shards(): rows = lax.all_to_all(rows, 'z', 0, 0, tiled=True)  11 us
    all_to_all x1, waiting for transfers between devices, shards(): packet = lax.all_to_all(packet, ('y', 'x'), 0, 0, tiled=True)  9.35 us
    all_to_all x1, starting transfers between devices, shards(): packet = lax.all_to_all(packet, ('y', 'x'), 0, 0, tiled=True)  5.81 us
    ppermute x1, starting transfers between devices, shards(): left = lax.ppermute(mine, ('y', 'x', 'core'), behind)  5.22 us
  transfers between devices with their start and end apart: 7, of which 5 were waited for; matrix products, arithmetic and copies ran while one was open for 3% of the time, Pallas kernels for 0%

profile of v8, /device:TPU:1, one launch (start us, length us, event | category | flops | bytes accessed | tf_op | source)
XLA Modules:
  0.0 147.3 jit_solution(9495958698108217413)
XLA Ops:
  0.1 1.5 fusion.1
  1.6 0.8 compare_reduce_fusion
  2.4 1.5 %fusion.24 = f32[128,16]{0,1:T(8,128)S(1)} fusion(bf16[3072,16]{0,1:T(8,128)(2,1)S(1)} %copy-done, bf16[128,3072]{1,0:T(8,128)(2,1)} %param.8, f32[3072]{0:T(1024)} %param.10, f32[128]{0:T(128)S(1)} %add_rsqrt_fusion), kind=kOutput, calls=%fused_computation.95 | convolution fusion | flops 14155776 | bytes 905728 | tf_op jit(solution)/shard_map/dot_general | solution.py:22
  5.5 0.4 convolution_convert_fusion.1
  6.0 1.3 maximum_maximum_fusion
  7.3 11.0 %all-to-all-start = ((bf16[8,16,6528]{2,1,0:T(8,128)(2,1)}), bf16[8,16,6528]{2,1,0:T(8,128)(2,1)S(1)}, u32[]{:S(2)}, u32[]{:S(2)}) async-start(bf16[8,16,6528]{2,1,0:T(8,128)(2,1)} %maximum_maximum_fusion), calls=%async_computation | async-start | bytes 3342336 | tf_op jit(solution)/shard_map/all_to_all | solution.py:256
  18.3 3.6 %pad_maximum_fusion = bf16[3,168,3072]{2,1,0:T(8,128)(2,1)} fusion(bf16[1,168,3072]{2,1,0:T(8,128)(2,1)} %param.15, bf16[1,168,3072]{2,1,0:T(8,128)(2,1)} %bitcast.77, bf16[1,168,3072]{2,1,0:T(8,128)(2,1)S(1)} %bitcast.72), kind=kLoop, calls=%fused_computation.6 | loop fusion | flops 3096576 | bytes 6193152 | tf_op jit(solution)/shard_map/stack | solution.py:220
  21.9 5.2 %collective-permute-start.1 = (bf16[3,168,3072]{2,1,0:T(8,128)(2,1)}, bf16[3,168,3072]{2,1,0:T(8,128)(2,1)}, u32[]{:S(2)}, u32[]{:S(2)}) collective-permute-start(bf16[3,168,3072]{2,1,0:T(8,128)(2,1)} %pad_maximum_fusion), channel_id=1, source_target_pairs={{1,48},{16,1},{33,16},{48,33},{65,112},{80,65},{97,80},{112,97},{1... | collective-permute-start | bytes 9289736 | tf_op jit(solution)/shard_map/ppermute | solution.py:229
  27.1 1.9 %collective-permute-start.2 = (bf16[3,168,3072]{2,1,0:T(8,128)(2,1)}, bf16[3,168,3072]{2,1,0:T(8,128)(2,1)}, u32[]{:S(2)}, u32[]{:S(2)}) collective-permute-start(bf16[3,168,3072]{2,1,0:T(8,128)(2,1)} %pad_maximum_fusion), channel_id=1, source_target_pairs={{1,16},{0,64},{16,33},{17,81},{33,48},{32,96},{48,1},{49,113},{65,... | collective-permute-start | bytes 9289736 | tf_op jit(solution)/shard_map/ppermute | solution.py:230
  29.0 31.8 %all-to-all-done.rows_hbm = bf16[8,16,6528]{2,1,0:T(8,128)(2,1)S(1)} async-done(((bf16[8,16,6528]{2,1,0:T(8,128)(2,1)}), bf16[8,16,6528]{2,1,0:T(8,128)(2,1)S(1)}, u32[]{:S(2)}, u32[]{:S(2)}) %all-to-all-start) | async-done | bytes 1671200 | tf_op jit(solution)/shard_map/all_to_all | solution.py:256
  60.8 2.4 %collective-permute-start = (bf16[8,16,6528]{2,1,0:T(8,128)(2,1)S(1)}, bf16[8,16,6528]{2,1,0:T(8,128)(2,1)}, u32[]{:S(2)}, u32[]{:S(2)}) collective-permute-start(bf16[8,16,6528]{2,1,0:T(8,128)(2,1)S(1)} %all-to-all-done.rows_hbm), channel_id=1, source_target_pairs={{0,1},{1,0},{2,3},{3,2},{4,5},{5,4},{6,7},{7,6},{8,9},{9,8},{10,11... | collective-permute-start | bytes 5013512 | tf_op jit(solution)/shard_map/ppermute | solution.py:257
  63.3 3.4 %collective-permute-done.2.refs_4_ = bf16[3,168,3072]{2,1,0:T(8,128)(2,1)} collective-permute-done((bf16[3,168,3072]{2,1,0:T(8,128)(2,1)}, bf16[3,168,3072]{2,1,0:T(8,128)(2,1)}, u32[]{:S(2)}, u32[]{:S(2)}) %collective-permute-start.2) | collective-permute-done | bytes 3096608 | tf_op jit(solution)/shard_map/ppermute | solution.py:230
  66.7 13.7 %shard_map.82 = (f32[8,8,56,128]{3,2,1,0:T(8,128)}, bf16[8,8,56,128]{3,2,1,0:T(8,128)(2,1)S(1)}) custom-call(s32[1]{0:T(128)} %bitcast.2.info, bf16[8,16,6528]{2,1,0:T(8,128)(2,1)} %copy-done.2, bf16[8,16,6528]{2,1,0:T(8,128)(2,1)} %collective-permute-done.others_hbm, bf16[168,3072]{1,0:T(8,128)(2,1)S(1)} %bitcast.73, bf16[168,3072]{1,0:T(8,128)(2,1)} %bitcast.78, ...), custom_call_target="tpu_custom_call" | custom-call | flops 2807562240 | bytes 12877824 | tf_op jit(solution)/shard_map/pallas_call | solution.py:178
  80.4 1.9 %collective-permute-start.3 = (bf16[8,8,56,128]{3,2,1,0:T(8,128)(2,1)S(1)}, bf16[8,8,56,128]{3,2,1,0:T(8,128)(2,1)S(1)}, u32[]{:S(2)}, u32[]{:S(2)}) collective-permute-start(bf16[8,8,56,128]{3,2,1,0:T(8,128)(2,1)S(1)} %get-tuple-element.8), channel_id=1, source_target_pairs={{0,1},{1,0},{2,3},{3,2},{4,5},{5,4},{6,7},{7,6},{8,9},{9,8},{10,11... | collective-permute-start | bytes 2752520 | tf_op jit(solution)/shard_map/ppermute | solution.py:262
  82.3 2.4 %collective-permute-done.3 = bf16[8,8,56,128]{3,2,1,0:T(8,128)(2,1)S(1)} collective-permute-done((bf16[8,8,56,128]{3,2,1,0:T(8,128)(2,1)S(1)}, bf16[8,8,56,128]{3,2,1,0:T(8,128)(2,1)S(1)}, u32[]{:S(2)}, u32[]{:S(2)}) %collective-permute-start.3) | collective-permute-done | bytes 917536 | tf_op jit(solution)/shard_map/ppermute | solution.py:262
  84.7 2.7 %add_convert_fusion = bf16[8,8,56,128]{3,2,1,0:T(8,128)(2,1)} fusion(f32[8,8,56,128]{3,2,1,0:T(8,128)} %get-tuple-element.7, bf16[8,8,56,128]{3,2,1,0:T(8,128)(2,1)S(1)} %collective-permute-done.3), kind=kLoop, calls=%fused_computation.9 | loop fusion | flops 1376256 | bytes 3670016 | tf_op jit(solution)/shard_map/convert_element_type | solution.py:263
  87.4 13.4 %all-to-all-start.1 = ((bf16[64,56,128]{2,1,0:T(8,128)(2,1)}), bf16[64,56,128]{2,1,0:T(8,128)(2,1)S(1)}, u32[]{:S(2)}, u32[]{:S(2)}) async-start(bf16[64,56,128]{2,1,0:T(8,128)(2,1)} %bitcast.17), calls=%async_computation.1 | async-start | bytes 1835008 | tf_op jit(solution)/shard_map/all_to_all | solution.py:265
  101.2 24.3 %all-to-all-done.1 = bf16[64,56,128]{2,1,0:T(8,128)(2,1)S(1)} async-done(((bf16[64,56,128]{2,1,0:T(8,128)(2,1)}), bf16[64,56,128]{2,1,0:T(8,128)(2,1)S(1)}, u32[]{:S(2)}, u32[]{:S(2)}) %all-to-all-start.1) | async-done | bytes 917536 | tf_op jit(solution)/shard_map/all_to_all | solution.py:265
  125.7 0.4 convolution_convert_fusion.6
  128.0 0.7 copy.54
  128.7 5.8 %all-to-all-start.2 = ((bf16[32,16,128]{2,1,0:T(8,128)(2,1)}), bf16[32,16,128]{2,1,0:T(8,128)(2,1)S(1)}, u32[]{:S(2)}, u32[]{:S(2)}) async-start(bf16[32,16,128]{2,1,0:T(8,128)(2,1)} %copy.54), calls=%async_computation.2 | async-start | bytes 262144 | tf_op jit(solution)/shard_map/all_to_all | solution.py:297
  134.6 9.3 %all-to-all-done.2 = bf16[32,16,128]{2,1,0:T(8,128)(2,1)S(1)} async-done(((bf16[32,16,128]{2,1,0:T(8,128)(2,1)}), bf16[32,16,128]{2,1,0:T(8,128)(2,1)S(1)}, u32[]{:S(2)}, u32[]{:S(2)}) %all-to-all-start.2) | async-done | bytes 131104 | tf_op jit(solution)/shard_map/all_to_all | solution.py:297
  144.6 1.2 fusion.5
  145.8 1.5 %fusion.9 = f32[1,4,3072]{2,1,0:T(4,128)} fusion(f32[4,3072]{1,0:T(4,128)S(1)} %get-tuple-element.32, f32[4]{0:T(128)S(1)} %broadcast_multiply_fusion, f32[4]{0:T(128)S(1)} %get-tuple-element.30, f32[4]{0:T(128)S(1)} %get-tuple-element.29, bf16[128,3072]{1,0:T(8,128)(2,1)} %param.9, s32[]{:T(128)S(6)} %select_n.105, bf16[128,3072]{1,0:T(8,128)(2,1)} %param.8), kind=kLoop, calls=%fused_computation.43 | loop fusion | flops 86016 | bytes 147508 | tf_op jit(solution)/shard_map/broadcast_in_dim | solution.py:320
  (73 shorter events, 4.6 us)
Async XLA Ops:
  0.0 2.4 %copy-start = (bf16[3072,16]{0,1:T(8,128)(2,1)S(1)}, bf16[3072,16]{0,1:T(8,128)(2,1)}, u32[]{:S(2)}) copy-start(bf16[3072,16]{0,1:T(8,128)(2,1)} %param.11) | copy-start | bytes 294916
  0.0 4.5 %copy-start.3 = (bf16[128,3072]{1,0:T(8,128)(2,1)S(1)}, bf16[128,3072]{1,0:T(8,128)(2,1)}, u32[]{:S(2)}) copy-start(bf16[128,3072]{1,0:T(8,128)(2,1)} %param.8) | copy-start | bytes 2359300
  0.0 3.9 %copy-start.5 = (s32[128,4]{0,1:T(4,128)S(1)}, s32[128,4]{0,1:T(4,128)}, u32[]{:S(2)}) copy-start(s32[128,4]{0,1:T(4,128)} %param.12) | copy-start | bytes 6148
  0.0 4.5 %copy-start.6 = (f32[3072]{0:T(1024)S(1)}, f32[3072]{0:T(1024)}, u32[]{:S(2)}) copy-start(f32[3072]{0:T(1024)} %param.10) | copy-start | bytes 36868
  1.6 3.4 %copy-start.4 = (bf16[128,3072]{1,0:T(8,128)(2,1)S(1)}, bf16[128,3072]{1,0:T(8,128)(2,1)}, u32[]{:S(2)}) copy-start(bf16[128,3072]{1,0:T(8,128)(2,1)} %param.9) | copy-start | bytes 2359300
  7.3 11.0 %copy-start.1 = (bf16[1,3072,168]{1,2,0:T(8,128)(2,1)S(1)}, bf16[1,3072,168]{1,2,0:T(8,128)(2,1)}, u32[]{:S(2)}) copy-start(bf16[1,3072,168]{1,2,0:T(8,128)(2,1)} %param.13) | copy-start | bytes 3096580
  7.3 53.5 %all-to-all-start = ((bf16[8,16,6528]{2,1,0:T(8,128)(2,1)}), bf16[8,16,6528]{2,1,0:T(8,128)(2,1)S(1)}, u32[]{:S(2)}, u32[]{:S(2)}) async-start(bf16[8,16,6528]{2,1,0:T(8,128)(2,1)} %maximum_maximum_fusion), calls=%async_computation | async-start | bytes 3342336 | tf_op jit(solution)/shard_map/all_to_all | solution.py:256
  21.9 41.4 %collective-permute-start.1 = (bf16[3,168,3072]{2,1,0:T(8,128)(2,1)}, bf16[3,168,3072]{2,1,0:T(8,128)(2,1)}, u32[]{:S(2)}, u32[]{:S(2)}) collective-permute-start(bf16[3,168,3072]{2,1,0:T(8,128)(2,1)} %pad_maximum_fusion), channel_id=1, source_target_pairs={{1,48},{16,1},{33,16},{48,33},{65,112},{80,65},{97,80},{112,97},{1... | collective-permute-start | bytes 9289736 | tf_op jit(solution)/shard_map/ppermute | solution.py:229
  27.1 39.6 %collective-permute-start.2 = (bf16[3,168,3072]{2,1,0:T(8,128)(2,1)}, bf16[3,168,3072]{2,1,0:T(8,128)(2,1)}, u32[]{:S(2)}, u32[]{:S(2)}) collective-permute-start(bf16[3,168,3072]{2,1,0:T(8,128)(2,1)} %pad_maximum_fusion), channel_id=1, source_target_pairs={{1,16},{0,64},{16,33},{17,81},{33,48},{32,96},{48,1},{49,113},{65,... | collective-permute-start | bytes 9289736 | tf_op jit(solution)/shard_map/ppermute | solution.py:230
  60.8 5.8 %copy-start.2 = (bf16[8,16,6528]{2,1,0:T(8,128)(2,1)}, bf16[8,16,6528]{2,1,0:T(8,128)(2,1)S(1)}, u32[]{:S(2)}) copy-start(bf16[8,16,6528]{2,1,0:T(8,128)(2,1)S(1)} %all-to-all-done.rows_hbm) | copy-start | bytes 5013508
  60.8 5.8 %collective-permute-start = (bf16[8,16,6528]{2,1,0:T(8,128)(2,1)S(1)}, bf16[8,16,6528]{2,1,0:T(8,128)(2,1)}, u32[]{:S(2)}, u32[]{:S(2)}) collective-permute-start(bf16[8,16,6528]{2,1,0:T(8,128)(2,1)S(1)} %all-to-all-done.rows_hbm), channel_id=1, source_target_pairs={{0,1},{1,0},{2,3},{3,2},{4,5},{5,4},{6,7},{7,6},{8,9},{9,8},{10,11... | collective-permute-start | bytes 5013512 | tf_op jit(solution)/shard_map/ppermute | solution.py:257
  80.4 4.4 %collective-permute-start.3 = (bf16[8,8,56,128]{3,2,1,0:T(8,128)(2,1)S(1)}, bf16[8,8,56,128]{3,2,1,0:T(8,128)(2,1)S(1)}, u32[]{:S(2)}, u32[]{:S(2)}) collective-permute-start(bf16[8,8,56,128]{3,2,1,0:T(8,128)(2,1)S(1)} %get-tuple-element.8), channel_id=1, source_target_pairs={{0,1},{1,0},{2,3},{3,2},{4,5},{5,4},{6,7},{7,6},{8,9},{9,8},{10,11... | collective-permute-start | bytes 2752520 | tf_op jit(solution)/shard_map/ppermute | solution.py:262
  87.4 38.1 %all-to-all-start.1 = ((bf16[64,56,128]{2,1,0:T(8,128)(2,1)}), bf16[64,56,128]{2,1,0:T(8,128)(2,1)S(1)}, u32[]{:S(2)}, u32[]{:S(2)}) async-start(bf16[64,56,128]{2,1,0:T(8,128)(2,1)} %bitcast.17), calls=%async_computation.1 | async-start | bytes 1835008 | tf_op jit(solution)/shard_map/all_to_all | solution.py:265
  128.7 15.3 %all-to-all-start.2 = ((bf16[32,16,128]{2,1,0:T(8,128)(2,1)}), bf16[32,16,128]{2,1,0:T(8,128)(2,1)S(1)}, u32[]{:S(2)}, u32[]{:S(2)}) async-start(bf16[32,16,128]{2,1,0:T(8,128)(2,1)} %copy.54), calls=%async_computation.2 | async-start | bytes 262144 | tf_op jit(solution)/shard_map/all_to_all | solution.py:297

commit v9 on v8

--- a/solution.py
+++ b/solution.py
@@ -15,29 +15,97 @@
 f32 = jnp.float32
 
 
-def token_weights(acts, gain, router, ids):
-    wide = acts.astype(f32)
-    recip = lax.rsqrt(jnp.mean(wide * wide, axis=-1, keepdims=True) + eps)
-    h = (wide * recip * gain).astype(bf16)
-    logits = jnp.dot(h, router, preferred_element_type=f32)
-    experts = router.shape[1]
-    select = (ids[:, :, None] == jnp.arange(experts, dtype=jnp.int32)[None, None, :]).astype(f32)
-    picked = jnp.sum(select * logits[:, None, :], axis=-1)
-    sig = jax.nn.sigmoid(picked)
-    total = jnp.sum(sig, axis=1, keepdims=True)
-    return h, sig, total, sig / total, select
-
-
-def places(ids, names):
-    tokens = ids.shape[0]
-    member = jnp.any(ids[:, :, None] == names[None, None, :], axis=1)
-    below = (jnp.arange(tokens)[:, None] > jnp.arange(tokens)[None, :]).astype(bf16)
-    place = jnp.dot(below, member.astype(bf16), preferred_element_type=f32).astype(jnp.int32)
-    return jnp.where(member, place, -4096).T
-
-
 def at_rows(place, count):
     return place[:, None, :] == jnp.arange(count, dtype=jnp.int32)[None, :, None]
+
+
+def front_kernel(cap, flags, *refs):
+    sources, (out, sig_ref, place_ref), copied, sem = refs[:5], refs[5:8], refs[8:13], refs[13]
+    copies = [
+        pltpu.make_async_copy(source, ref, sem.at[i])
+        for i, (source, ref) in enumerate(zip(sources, copied))
+    ]
+    for copy in copies:
+        copy.start()
+    for copy in copies:
+        copy.wait()
+    acts, cotangent, gain, router, ids = copied
+    tokens, width = acts.shape
+    nz, main, _ = out.shape
+    top = ids.shape[0]
+    fold = 2 * width // main
+    parity, odd = flags[0], flags[1]
+    wide = acts[...].astype(f32)
+    recip = lax.rsqrt(jnp.mean(wide * wide, axis=1, keepdims=True) + eps)
+    h = (wide * recip * gain[...]).astype(bf16)
+    logits = lax.dot_general(
+        router[...], h, (((1,), (1,)), ((), ())), preferred_element_type=f32
+    )
+    named = lax.broadcasted_iota(jnp.int32, logits.shape, 0)
+    sig = []
+    for k in range(top):
+        picked = jnp.where(named == ids[k : k + 1], logits, 0.0)
+        sig.append(jax.nn.sigmoid(jnp.sum(picked, axis=0, keepdims=True)))
+    sig_ref[...] = jnp.concatenate(sig, axis=0)
+    total = sum(sig[1:], sig[0])
+    names = 2 * lax.broadcasted_iota(jnp.int32, (nz, tokens), 0) + parity
+    member = jnp.zeros((nz, tokens), f32)
+    dense = jnp.zeros((nz, tokens), f32)
+    for k in range(top):
+        hit = names == ids[k : k + 1]
+        member = jnp.where(hit, 1.0, member)
+        dense = jnp.where(hit, sig[k] / total, dense)
+    dense = dense.astype(bf16).astype(f32)
+    before = lax.broadcasted_iota(jnp.int32, (tokens, tokens), 0)
+    before = before < lax.broadcasted_iota(jnp.int32, (tokens, tokens), 1)
+    place = jnp.dot(member.astype(bf16), before.astype(bf16), preferred_element_type=f32)
+    place = jnp.where(member > 0.0, place.astype(jnp.int32), -4096)
+    place_ref[...] = place
+    place = place - odd * cap
+    slot = lax.broadcasted_iota(jnp.int32, (main, tokens), 0)
+    pick, scaled = [], []
+    for z in range(nz):
+        one = jnp.where(place[z : z + 1] == slot, 1.0, 0.0)
+        pick.append(one)
+        scaled.append(one * dense[z : z + 1])
+    extra = jnp.where(place == main, 1.0, 0.0)
+    sides = (
+        (h, jnp.concatenate(pick, axis=0), extra),
+        (cotangent[...], jnp.concatenate(scaled, axis=0), extra * dense),
+    )
+    folded = []
+    for j, (values, mains, extras) in enumerate(sides):
+        rows = jnp.dot(mains.astype(bf16), values, preferred_element_type=f32).astype(bf16)
+        for z in range(nz):
+            out[z, :, j * width : (j + 1) * width] = rows[z * main : (z + 1) * main]
+        folded.append(jnp.dot(extras.astype(bf16), values, preferred_element_type=f32))
+    for z in range(nz):
+        lines = [v[z : z + 1, i * fold : (i + 1) * fold] for v in folded for i in range(main // 2)]
+        out[z, :, 2 * width :] = jnp.concatenate(lines, axis=0).astype(bf16)
+
+
+def front_rows(flags, acts, cotangent, gain, router, ids, nz, cap):
+    tokens, width = acts.shape
+    smem, vmem, hbm = (pl.BlockSpec(memory_space=m) for m in (pltpu.SMEM, pltpu.VMEM, pl.ANY))
+    values = (acts, cotangent, gain.reshape(1, width), router.T, ids.T)
+    return pl.pallas_call(
+        functools.partial(front_kernel, cap),
+        out_shape=(
+            jax.ShapeDtypeStruct((nz, MAIN, 2 * width + 2 * width // MAIN), bf16),
+            jax.ShapeDtypeStruct(ids.T.shape, f32),
+            jax.ShapeDtypeStruct((nz, tokens), jnp.int32),
+        ),
+        in_specs=[smem] + [hbm] * 5,
+        out_specs=(vmem, vmem, vmem),
+        scratch_shapes=[pltpu.VMEM(v.shape, v.dtype) for v in values]
+        + [pltpu.SemaphoreType.DMA((5,))],
+        compiler_params=pltpu.CompilerParams(vmem_limit_bytes=60 * 1024 * 1024),
+        cost_estimate=pl.CostEstimate(
+            flops=4 * tokens * tokens * width,
+            bytes_accessed=4 * tokens * width + 4 * nz * MAIN * width,
+            transcendentals=tokens * 5,
+        ),
+    )(flags, *values)
 
 
 def expert_kernel(nz, info, rows_hbm, others_hbm, *refs):
@@ -178,7 +246,7 @@
     return pl.pallas_call(
         functools.partial(expert_kernel, nz),
         out_shape=(
-            jax.ShapeDtypeStruct((ny, nz, rank, LANE), f32),
+            jax.ShapeDtypeStruct((ny, nz, rank, LANE), bf16),
             jax.ShapeDtypeStruct((ny, nz, rank, LANE), bf16),
         ),
         in_specs=[pl.BlockSpec(memory_space=pltpu.SMEM)] + [hbm] * 7,
@@ -188,13 +256,13 @@
             pltpu.VMEM((2 * nz + 1, MAIN, width), bf16),
             pltpu.VMEM((2 * nz, MAIN, 2 * width // MAIN), bf16),
             pltpu.VMEM((2, kinds, hidden, width), bf16),
-            pltpu.VMEM((ny, nz, rank, LANE), f32),
+            pltpu.VMEM((ny, nz, rank, LANE), bf16),
             pltpu.VMEM((ny, nz, rank, LANE), bf16),
             pltpu.SemaphoreType.DMA((3, 2)),
             pltpu.SemaphoreType.DMA((2, 3)),
             pltpu.SemaphoreType.DMA((ny, 2)),
         ],
-        compiler_params=pltpu.CompilerParams(vmem_limit_bytes=52 * 1024 * 1024),
+        compiler_params=pltpu.CompilerParams(vmem_limit_bytes=56 * 1024 * 1024),
         cost_estimate=pl.CostEstimate(
             flops=20 * count * width * hidden,
             bytes_accessed=2 * (4 * count * width + 6 * width * hidden),
@@ -230,29 +298,18 @@
     other = lax.ppermute(mine, ("y", "x", "core"), ahead)
     info = (core == parity).astype(jnp.int32).reshape(1)
 
-    h, sig, total, weight, select = token_weights(acts, gain, router, ids)
     names = 2 * jnp.arange(nz, dtype=jnp.int32) + parity
-    place = places(ids, names)
+    flags = jnp.stack([parity, (x // 2 + y) % 2]).astype(jnp.int32)
+    rows, sig, place = front_rows(flags, acts, cotangent, gain, router, ids, nz, cap)
+    sig = sig.T
+    total = jnp.sum(sig, axis=1, keepdims=True)
+    weight = sig / total
+    select = (ids[:, :, None] == jnp.arange(experts, dtype=jnp.int32)[None, None, :]).astype(f32)
     halves = [
         jnp.where((place >= n * cap) & (place < (n + 1) * cap), place - n * cap, -4096)
         for n in (0, 1)
     ]
-    odd = (x // 2 + y) % 2 == 1
-    here = jnp.where(odd, halves[1], halves[0])
     of_name = (ids[:, :, None] == names[None, None, :]).astype(f32)
-    dense = jnp.sum(of_name * weight[:, :, None], axis=1).astype(bf16).T
-
-    def picked(scale, values):
-        main = (at_rows(here, MAIN).astype(bf16) * scale[:, None, :]).reshape(nz * MAIN, tokens)
-        extra = (here == MAIN).astype(bf16) * scale
-        main = jnp.dot(main, values, preferred_element_type=f32).astype(bf16)
-        extra = jnp.dot(extra, values, preferred_element_type=f32).astype(bf16)
-        return main.reshape(nz, MAIN, width), extra.reshape(nz, MAIN // 2, 2 * width // MAIN)
-
-    h_main, h_extra = picked(jnp.ones_like(dense), h)
-    dy_main, dy_extra = picked(dense, cotangent)
-    extra = jnp.concatenate([h_extra, dy_extra], axis=1)
-    rows = jnp.concatenate([h_main, dy_main, extra], axis=2)
     rows = lax.all_to_all(rows, "z", 0, 0, tiled=True)
     others = lax.ppermute(rows, "core", swap)
 
@@ -260,7 +317,7 @@
     rank = -(-(pieces * cap + 4) // 8) * 8
     keep, give = expert_rows(info, rows, others, (*mine_parts, left, other), ny, rank)
     got = lax.ppermute(give, "core", swap)
-    back = (keep + got.astype(f32)).astype(bf16)
+    back = (keep.astype(f32) + got.astype(f32)).astype(bf16)
 
     back = lax.all_to_all(back.reshape(ny * nz, rank, LANE), ("y", "z"), 0, 0, tiled=True)
     flat = back.reshape(ny * nz * rank, LANE)

time: 149 us -> 145 us (0.973)
  other arithmetic: 12.9 us -> 9.21 us
  matrix products: 5.58 us -> 2.46 us
  Pallas kernels: 13.7 us -> 16.1 us
    pallas_call x0 -> x1, Pallas kernels: none -> 4.52 us  [front_rows(): pl.pallas_call(functools.partial(front_kernel, cap), out_shape=(jax.Shape...]
    dot_general x6 -> x0, matrix products: 3.04 us -> none  [the longest x1 1.51 us: token_weights(): logits = jnp.dot(h, router, preferred_element_type=f32)]
    pallas_call x1, Pallas kernels: 13.7 us -> 11.5 us  [expert_rows(): pl.pallas_call(functools.partial(expert_kernel, nz), out_shape=(jax.Shape...]
where the time goes in v9:
time: 145 us; the launch traced here: 143 us
  waiting for transfers between devices  71.1 us (49%)
  starting transfers between devices  41.7 us (29%)
  Pallas kernels  16.1 us (11%)
  other arithmetic  9.21 us (6%)
  matrix products  2.46 us (2%)
  local copies, waits for them, and re-layouts  1.91 us (1%)
    all_to_all x1, waiting for transfers between devices, shards(): rows = lax.all_to_all(rows, 'z', 0, 0, tiled=True)  31.8 us
    all_to_all x1, waiting for transfers between devices, shards(): lax.all_to_all(back.reshape(ny * nz, rank, LANE), ('y', 'z'), 0, 0, tiled...  24.5 us
    all_to_all x1, starting transfers between devices, shards(): lax.all_to_all(back.reshape(ny * nz, rank, LANE), ('y', 'z'), 0, 0, tiled...  13 us
    pallas_call x1, Pallas kernels, expert_rows(): pl.pallas_call(functools.partial(expert_kernel, nz), out_shape=(jax.Shape...  11.5 us
    all_to_all x1, starting transfers between devices, shards(): rows = lax.all_to_all(rows, 'z', 0, 0, tiled=True)  10.9 us
    all_to_all x1, waiting for transfers between devices, shards(): packet = lax.all_to_all(packet, ('y', 'x'), 0, 0, tiled=True)  9.31 us
    all_to_all x1, starting transfers between devices, shards(): packet = lax.all_to_all(packet, ('y', 'x'), 0, 0, tiled=True)  5.81 us
    ppermute x1, starting transfers between devices, shards(): left = lax.ppermute(mine, ('y', 'x', 'core'), behind)  5.22 us
  transfers between devices with their start and end apart: 7, of which 5 were waited for; matrix products, arithmetic and copies ran while one was open for 3% of the time, Pallas kernels for 0%

profile of v9, /device:TPU:1, one launch (start us, length us, event | category | flops | bytes accessed | tf_op | source)
XLA Modules:
  0.0 142.9 jit_solution(14627163420014687857)
XLA Ops:
  0.0 0.6 pad_add_fusion.flags
  0.6 4.5 %shard_map.82 = (bf16[8,16,6528]{2,1,0:T(8,128)(2,1)}, f32[4,128]{1,0:T(4,128)}, s32[8,128]{1,0:T(8,128)}) custom-call(s32[2]{0:T(128)} %pad_add_fusion.flags, bf16[128,3072]{1,0:T(8,128)(2,1)} %refs_0_.1, bf16[128,3072]{1,0:T(8,128)(2,1)} %refs_1_.1, f32[1,3072]{1,0:T(1,128)} %bitcast.83, bf16[16,3072]{1,0:T(8,128)(2,1)} %bitcast.76, s32[4,128]{1,0:T(4,128)} %bitcast.84), custom_call_target="tpu_custom_call" | custom-call | flops 201326592 | bytes 3145728 | tf_op jit(solution)/shard_map/pallas_call | solution.py:91
  5.1 10.9 %all-to-all-start = ((bf16[8,16,6528]{2,1,0:T(8,128)(2,1)}), bf16[8,16,6528]{2,1,0:T(8,128)(2,1)S(1)}, u32[]{:S(2)}, u32[]{:S(2)}) async-start(bf16[8,16,6528]{2,1,0:T(8,128)(2,1)} %get-tuple-element.11), calls=%async_computation | async-start | bytes 3342336 | tf_op jit(solution)/shard_map/all_to_all | solution.py:313
  16.0 3.6 %pad_maximum_fusion = bf16[3,168,3072]{2,1,0:T(8,128)(2,1)} fusion(bf16[1,168,3072]{2,1,0:T(8,128)(2,1)} %param.15, bf16[1,168,3072]{2,1,0:T(8,128)(2,1)} %bitcast.68, bf16[1,168,3072]{2,1,0:T(8,128)(2,1)S(1)} %bitcast.67), kind=kLoop, calls=%fused_computation.2 | loop fusion | flops 3096576 | bytes 6193152 | tf_op jit(solution)/shard_map/stack | solution.py:288
  19.5 5.2 %collective-permute-start.1 = (bf16[3,168,3072]{2,1,0:T(8,128)(2,1)}, bf16[3,168,3072]{2,1,0:T(8,128)(2,1)}, u32[]{:S(2)}, u32[]{:S(2)}) collective-permute-start(bf16[3,168,3072]{2,1,0:T(8,128)(2,1)} %pad_maximum_fusion), channel_id=1, source_target_pairs={{1,48},{16,1},{33,16},{48,33},{65,112},{80,65},{97,80},{112,97},{1... | collective-permute-start | bytes 9289736 | tf_op jit(solution)/shard_map/ppermute | solution.py:297
  24.7 1.9 %collective-permute-start.2 = (bf16[3,168,3072]{2,1,0:T(8,128)(2,1)}, bf16[3,168,3072]{2,1,0:T(8,128)(2,1)}, u32[]{:S(2)}, u32[]{:S(2)}) collective-permute-start(bf16[3,168,3072]{2,1,0:T(8,128)(2,1)} %pad_maximum_fusion), channel_id=1, source_target_pairs={{1,16},{0,64},{16,33},{17,81},{33,48},{32,96},{48,1},{49,113},{65,... | collective-permute-start | bytes 9289736 | tf_op jit(solution)/shard_map/ppermute | solution.py:298
  26.7 31.8 %all-to-all-done.rows_hbm = bf16[8,16,6528]{2,1,0:T(8,128)(2,1)S(1)} async-done(((bf16[8,16,6528]{2,1,0:T(8,128)(2,1)}), bf16[8,16,6528]{2,1,0:T(8,128)(2,1)S(1)}, u32[]{:S(2)}, u32[]{:S(2)}) %all-to-all-start) | async-done | bytes 1671200 | tf_op jit(solution)/shard_map/all_to_all | solution.py:313
  58.5 2.4 %collective-permute-start = (bf16[8,16,6528]{2,1,0:T(8,128)(2,1)S(1)}, bf16[8,16,6528]{2,1,0:T(8,128)(2,1)}, u32[]{:S(2)}, u32[]{:S(2)}) collective-permute-start(bf16[8,16,6528]{2,1,0:T(8,128)(2,1)S(1)} %all-to-all-done.rows_hbm), channel_id=1, source_target_pairs={{0,1},{1,0},{2,3},{3,2},{4,5},{5,4},{6,7},{7,6},{8,9},{9,8},{10,11... | collective-permute-start | bytes 5013512 | tf_op jit(solution)/shard_map/ppermute | solution.py:314
  60.9 3.4 %collective-permute-done.2.refs_4_ = bf16[3,168,3072]{2,1,0:T(8,128)(2,1)} collective-permute-done((bf16[3,168,3072]{2,1,0:T(8,128)(2,1)}, bf16[3,168,3072]{2,1,0:T(8,128)(2,1)}, u32[]{:S(2)}, u32[]{:S(2)}) %collective-permute-start.2) | collective-permute-done | bytes 3096608 | tf_op jit(solution)/shard_map/ppermute | solution.py:298
  64.4 11.5 %shard_map.83 = (bf16[8,8,56,128]{3,2,1,0:T(8,128)(2,1)}, bf16[8,8,56,128]{3,2,1,0:T(8,128)(2,1)}) custom-call(s32[1]{0:T(128)} %bitcast.6.info, bf16[8,16,6528]{2,1,0:T(8,128)(2,1)} %copy-done, bf16[8,16,6528]{2,1,0:T(8,128)(2,1)} %collective-permute-done.others_hbm, bf16[168,3072]{1,0:T(8,128)(2,1)} %bitcast.66, bf16[168,3072]{1,0:T(8,128)(2,1)} %bitcast.69, ...), custom_call_target="tpu_custom_call" | custom-call | flops 2807562240 | bytes 12877824 | tf_op jit(solution)/shard_map/pallas_call | solution.py:246
  75.9 2.4 %collective-permute-start.3 = (bf16[8,8,56,128]{3,2,1,0:T(8,128)(2,1)}, bf16[8,8,56,128]{3,2,1,0:T(8,128)(2,1)S(1)}, u32[]{:S(2)}, u32[]{:S(2)}) collective-permute-start(bf16[8,8,56,128]{3,2,1,0:T(8,128)(2,1)} %get-tuple-element.13), channel_id=1, source_target_pairs={{0,1},{1,0},{2,3},{3,2},{4,5},{5,4},{6,7},{7,6},{8,9},{9,8},{10,11... | collective-permute-start | bytes 2752520 | tf_op jit(solution)/shard_map/ppermute | solution.py:319
  78.6 2.0 %collective-permute-done.3 = bf16[8,8,56,128]{3,2,1,0:T(8,128)(2,1)S(1)} collective-permute-done((bf16[8,8,56,128]{3,2,1,0:T(8,128)(2,1)}, bf16[8,8,56,128]{3,2,1,0:T(8,128)(2,1)S(1)}, u32[]{:S(2)}, u32[]{:S(2)}) %collective-permute-start.3) | collective-permute-done | bytes 917536 | tf_op jit(solution)/shard_map/ppermute | solution.py:319
  80.6 2.4 %add_convert_fusion = bf16[8,8,56,128]{3,2,1,0:T(8,128)(2,1)} fusion(bf16[8,8,56,128]{3,2,1,0:T(8,128)(2,1)S(1)} %collective-permute-done.3, bf16[8,8,56,128]{3,2,1,0:T(8,128)(2,1)} %get-tuple-element.12), kind=kLoop, calls=%fused_computation.3 | loop fusion | flops 1835008 | bytes 2752512 | tf_op jit(solution)/shard_map/convert_element_type | solution.py:320
  83.0 13.0 %all-to-all-start.1 = ((bf16[64,56,128]{2,1,0:T(8,128)(2,1)}), bf16[64,56,128]{2,1,0:T(8,128)(2,1)S(1)}, u32[]{:S(2)}, u32[]{:S(2)}) async-start(bf16[64,56,128]{2,1,0:T(8,128)(2,1)} %bitcast.16), calls=%async_computation.1 | async-start | bytes 1835008 | tf_op jit(solution)/shard_map/all_to_all | solution.py:322
  96.4 24.5 %all-to-all-done.1 = bf16[64,56,128]{2,1,0:T(8,128)(2,1)S(1)} async-done(((bf16[64,56,128]{2,1,0:T(8,128)(2,1)}), bf16[64,56,128]{2,1,0:T(8,128)(2,1)S(1)}, u32[]{:S(2)}, u32[]{:S(2)}) %all-to-all-start.1) | async-done | bytes 917536 | tf_op jit(solution)/shard_map/all_to_all | solution.py:322
  121.1 0.4 convolution_convert_fusion.2
  121.5 0.1 broadcast_in_dim.44
  121.7 0.4 convolution_convert_fusion.1
  122.3 0.4 convolution_convert_fusion
  123.5 0.7 copy.46
  124.2 5.8 %all-to-all-start.2 = ((bf16[32,16,128]{2,1,0:T(8,128)(2,1)}), bf16[32,16,128]{2,1,0:T(8,128)(2,1)S(1)}, u32[]{:S(2)}, u32[]{:S(2)}) async-start(bf16[32,16,128]{2,1,0:T(8,128)(2,1)} %copy.46), calls=%async_computation.2 | async-start | bytes 262144 | tf_op jit(solution)/shard_map/all_to_all | solution.py:354
  130.1 9.3 %all-to-all-done.2 = bf16[32,16,128]{2,1,0:T(8,128)(2,1)S(1)} async-done(((bf16[32,16,128]{2,1,0:T(8,128)(2,1)}), bf16[32,16,128]{2,1,0:T(8,128)(2,1)S(1)}, u32[]{:S(2)}, u32[]{:S(2)}) %all-to-all-start.2) | async-done | bytes 131104 | tf_op jit(solution)/shard_map/all_to_all | solution.py:354
  140.2 1.1 fusion.1
  141.3 1.5 %fusion.5 = f32[1,4,3072]{2,1,0:T(4,128)} fusion(f32[4,3072]{1,0:T(4,128)S(1)} %get-tuple-element.33, f32[4]{0:T(128)S(1)} %broadcast_multiply_fusion, f32[4]{0:T(128)S(1)} %get-tuple-element.32, f32[4]{0:T(128)S(1)} %get-tuple-element.31, bf16[128,3072]{1,0:T(8,128)(2,1)} %refs_1_.1, s32[]{:T(128)S(6)} %select_n.94, bf16[128,3072]{1,0:T(8,128)(2,1)} %refs_0_.1), kind=kLoop, calls=%fused_computation.29 | loop fusion | flops 86016 | bytes 147508 | tf_op jit(solution)/shard_map/broadcast_in_dim | solution.py:377
  (60 shorter events, 2.3 us)
Async XLA Ops:
  0.0 16.0 %copy-start.1 = (bf16[1,3072,168]{1,2,0:T(8,128)(2,1)S(1)}, bf16[1,3072,168]{1,2,0:T(8,128)(2,1)}, u32[]{:S(2)}) copy-start(bf16[1,3072,168]{1,2,0:T(8,128)(2,1)} %param.13) | copy-start | bytes 3096580
  5.1 53.4 %all-to-all-start = ((bf16[8,16,6528]{2,1,0:T(8,128)(2,1)}), bf16[8,16,6528]{2,1,0:T(8,128)(2,1)S(1)}, u32[]{:S(2)}, u32[]{:S(2)}) async-start(bf16[8,16,6528]{2,1,0:T(8,128)(2,1)} %get-tuple-element.11), calls=%async_computation | async-start | bytes 3342336 | tf_op jit(solution)/shard_map/all_to_all | solution.py:313
  19.5 41.4 %collective-permute-start.1 = (bf16[3,168,3072]{2,1,0:T(8,128)(2,1)}, bf16[3,168,3072]{2,1,0:T(8,128)(2,1)}, u32[]{:S(2)}, u32[]{:S(2)}) collective-permute-start(bf16[3,168,3072]{2,1,0:T(8,128)(2,1)} %pad_maximum_fusion), channel_id=1, source_target_pairs={{1,48},{16,1},{33,16},{48,33},{65,112},{80,65},{97,80},{112,97},{1... | collective-permute-start | bytes 9289736 | tf_op jit(solution)/shard_map/ppermute | solution.py:297
  24.7 39.6 %collective-permute-start.2 = (bf16[3,168,3072]{2,1,0:T(8,128)(2,1)}, bf16[3,168,3072]{2,1,0:T(8,128)(2,1)}, u32[]{:S(2)}, u32[]{:S(2)}) collective-permute-start(bf16[3,168,3072]{2,1,0:T(8,128)(2,1)} %pad_maximum_fusion), channel_id=1, source_target_pairs={{1,16},{0,64},{16,33},{17,81},{33,48},{32,96},{48,1},{49,113},{65,... | collective-permute-start | bytes 9289736 | tf_op jit(solution)/shard_map/ppermute | solution.py:298
  58.5 5.8 %copy-start = (bf16[8,16,6528]{2,1,0:T(8,128)(2,1)}, bf16[8,16,6528]{2,1,0:T(8,128)(2,1)S(1)}, u32[]{:S(2)}) copy-start(bf16[8,16,6528]{2,1,0:T(8,128)(2,1)S(1)} %all-to-all-done.rows_hbm) | copy-start | bytes 5013508
  58.5 5.8 %collective-permute-start = (bf16[8,16,6528]{2,1,0:T(8,128)(2,1)S(1)}, bf16[8,16,6528]{2,1,0:T(8,128)(2,1)}, u32[]{:S(2)}, u32[]{:S(2)}) collective-permute-start(bf16[8,16,6528]{2,1,0:T(8,128)(2,1)S(1)} %all-to-all-done.rows_hbm), channel_id=1, source_target_pairs={{0,1},{1,0},{2,3},{3,2},{4,5},{5,4},{6,7},{7,6},{8,9},{9,8},{10,11... | collective-permute-start | bytes 5013512 | tf_op jit(solution)/shard_map/ppermute | solution.py:314
  64.3 14.0 %copy-start.4 = (s32[128,4]{0,1:T(4,128)S(1)}, s32[128,4]{0,1:T(4,128)}, u32[]{:S(2)}) copy-start(s32[128,4]{0,1:T(4,128)} %param.12) | copy-start | bytes 6148
  64.3 14.2 %copy-start.6 = (s32[8,128]{1,0:T(8,128)S(1)}, s32[8,128]{1,0:T(8,128)}, u32[]{:S(2)}) copy-start(s32[8,128]{1,0:T(8,128)} %get-tuple-element.10) | copy-start | bytes 12292
  75.9 4.7 %collective-permute-start.3 = (bf16[8,8,56,128]{3,2,1,0:T(8,128)(2,1)}, bf16[8,8,56,128]{3,2,1,0:T(8,128)(2,1)S(1)}, u32[]{:S(2)}, u32[]{:S(2)}) collective-permute-start(bf16[8,8,56,128]{3,2,1,0:T(8,128)(2,1)} %get-tuple-element.13), channel_id=1, source_target_pairs={{0,1},{1,0},{2,3},{3,2},{4,5},{5,4},{6,7},{7,6},{8,9},{9,8},{10,11... | collective-permute-start | bytes 2752520 | tf_op jit(solution)/shard_map/ppermute | solution.py:319
  83.0 38.0 %all-to-all-start.1 = ((bf16[64,56,128]{2,1,0:T(8,128)(2,1)}), bf16[64,56,128]{2,1,0:T(8,128)(2,1)S(1)}, u32[]{:S(2)}, u32[]{:S(2)}) async-start(bf16[64,56,128]{2,1,0:T(8,128)(2,1)} %bitcast.16), calls=%async_computation.1 | async-start | bytes 1835008 | tf_op jit(solution)/shard_map/all_to_all | solution.py:322
  121.7 8.3 %copy-start.5 = (f32[4,128]{1,0:T(4,128)S(1)}, f32[4,128]{1,0:T(4,128)}, u32[]{:S(2)}) copy-start(f32[4,128]{1,0:T(4,128)} %get-tuple-element.14) | copy-start | bytes 6148
  121.7 18.5 %copy-start.2 = (bf16[3072,16]{0,1:T(8,128)(2,1)S(1)}, bf16[3072,16]{0,1:T(8,128)(2,1)}, u32[]{:S(2)}) copy-start(bf16[3072,16]{0,1:T(8,128)(2,1)} %param.11) | copy-start | bytes 294916
  121.7 18.5 %copy-start.3 = (f32[3072]{0:T(1024)S(1)}, f32[3072]{0:T(1024)}, u32[]{:S(2)}) copy-start(f32[3072]{0:T(1024)} %param.10) | copy-start | bytes 36868
  124.2 15.3 %all-to-all-start.2 = ((bf16[32,16,128]{2,1,0:T(8,128)(2,1)}), bf16[32,16,128]{2,1,0:T(8,128)(2,1)S(1)}, u32[]{:S(2)}, u32[]{:S(2)}) async-start(bf16[32,16,128]{2,1,0:T(8,128)(2,1)} %copy.46), calls=%async_computation.2 | async-start | bytes 262144 | tf_op jit(solution)/shard_map/all_to_all | solution.py:354

commit v10 on v9

--- a/solution.py
+++ b/solution.py
@@ -19,13 +19,18 @@
     return place[:, None, :] == jnp.arange(count, dtype=jnp.int32)[None, :, None]
 
 
-def front_kernel(cap, flags, *refs):
-    sources, (out, sig_ref, place_ref), copied, sem = refs[:5], refs[5:8], refs[8:13], refs[13]
+def front_kernel(cap, *refs):
+    sources, weights, (out, sig_ref, place_ref, stacked) = refs[:5], refs[5:8], refs[8:12]
+    copied, sem, stack_sem = refs[12:17], refs[17], refs[18]
     copies = [
         pltpu.make_async_copy(source, ref, sem.at[i])
         for i, (source, ref) in enumerate(zip(sources, copied))
     ]
-    for copy in copies:
+    stacking = [
+        pltpu.make_async_copy(weight, stacked.at[j], stack_sem.at[j])
+        for j, weight in enumerate(weights)
+    ]
+    for copy in copies + stacking:
         copy.start()
     for copy in copies:
         copy.wait()
@@ -34,7 +39,8 @@
     nz, main, _ = out.shape
     top = ids.shape[0]
     fold = 2 * width // main
-    parity, odd = flags[0], flags[1]
+    x, y = lax.axis_index("x"), lax.axis_index("y")
+    parity, odd = x % 2, (x // 2 + y) % 2
     wide = acts[...].astype(f32)
     recip = lax.rsqrt(jnp.mean(wide * wide, axis=1, keepdims=True) + eps)
     h = (wide * recip * gain[...]).astype(bf16)
@@ -82,11 +88,13 @@
     for z in range(nz):
         lines = [v[z : z + 1, i * fold : (i + 1) * fold] for v in folded for i in range(main // 2)]
         out[z, :, 2 * width :] = jnp.concatenate(lines, axis=0).astype(bf16)
-
-
-def front_rows(flags, acts, cotangent, gain, router, ids, nz, cap):
+    for copy in stacking:
+        copy.wait()
+
+
+def front_rows(acts, cotangent, gain, router, ids, weights, nz, cap):
     tokens, width = acts.shape
-    smem, vmem, hbm = (pl.BlockSpec(memory_space=m) for m in (pltpu.SMEM, pltpu.VMEM, pl.ANY))
+    vmem, hbm = (pl.BlockSpec(memory_space=m) for m in (pltpu.VMEM, pl.ANY))
     values = (acts, cotangent, gain.reshape(1, width), router.T, ids.T)
     return pl.pallas_call(
         functools.partial(front_kernel, cap),
@@ -94,34 +102,34 @@
             jax.ShapeDtypeStruct((nz, MAIN, 2 * width + 2 * width // MAIN), bf16),
             jax.ShapeDtypeStruct(ids.T.shape, f32),
             jax.ShapeDtypeStruct((nz, tokens), jnp.int32),
+            jax.ShapeDtypeStruct((3, *weights[0].shape), bf16),
         ),
-        in_specs=[smem] + [hbm] * 5,
-        out_specs=(vmem, vmem, vmem),
+        in_specs=[hbm] * 8,
+        out_specs=(vmem, vmem, vmem, hbm),
         scratch_shapes=[pltpu.VMEM(v.shape, v.dtype) for v in values]
-        + [pltpu.SemaphoreType.DMA((5,))],
+        + [pltpu.SemaphoreType.DMA((5,)), pltpu.SemaphoreType.DMA((3,))],
         compiler_params=pltpu.CompilerParams(vmem_limit_bytes=60 * 1024 * 1024),
         cost_estimate=pl.CostEstimate(
             flops=4 * tokens * tokens * width,
             bytes_accessed=4 * tokens * width + 4 * nz * MAIN * width,
             transcendentals=tokens * 5,
         ),
-    )(flags, *values)
-
-
-def expert_kernel(nz, info, rows_hbm, others_hbm, *refs):
-    mine, (left, other, keep_hbm, give_hbm) = refs[:3], refs[3:7]
-    h_ref, g_ref, e_ref, w_ref, keep_ref, give_ref, row_sem, w_sem, out_sem = refs[7:]
+    )(*values, *weights)
+
+
+def expert_kernel(nz, rows_hbm, others_hbm, *refs):
+    mine, left, other, keep_hbm, give_hbm = refs[:5]
+    h_ref, g_ref, e_ref, w_ref, keep_ref, give_ref, row_sem, w_sem, out_sem = refs[5:]
     ny, rank, lane = keep_ref.shape[0], keep_ref.shape[2], keep_ref.shape[3]
     width = h_ref.shape[2]
     part, fold = width // ny, e_ref.shape[2]
     pieces = part // lane
     count = 2 * nz * MAIN
     contract = (((1,), (1,)), ((), ()))
-    own = info[0]
-    left, other = ([ref.at[j] for j in range(3)] for ref in (left, other))
+    own = (lax.axis_index("core") == lax.axis_index("x") % 2).astype(jnp.int32)
 
     def fetch(u, j, source):
-        return pltpu.make_async_copy(source[j], w_ref.at[u, j], w_sem.at[u, j])
+        return pltpu.make_async_copy(source.at[j], w_ref.at[u, j], w_sem.at[u, j])
 
     def start_first(j):
         @pl.when(own == 1)
@@ -238,9 +246,9 @@
     end(stores)
 
 
-def expert_rows(info, rows, others, slices, ny, rank):
+def expert_rows(rows, others, slices, ny, rank):
     nz = rows.shape[0]
-    kinds, hidden, width = slices[-1].shape
+    kinds, hidden, width = slices[0].shape
     hbm = pl.BlockSpec(memory_space=pl.ANY)
     count = (2 * nz + 1) * MAIN
     return pl.pallas_call(
@@ -249,7 +257,7 @@
             jax.ShapeDtypeStruct((ny, nz, rank, LANE), bf16),
             jax.ShapeDtypeStruct((ny, nz, rank, LANE), bf16),
         ),
-        in_specs=[pl.BlockSpec(memory_space=pltpu.SMEM)] + [hbm] * 7,
+        in_specs=[hbm] * 5,
         out_specs=(hbm, hbm),
         scratch_shapes=[
             pltpu.VMEM((2 * nz + 1, MAIN, width), bf16),
@@ -262,13 +270,13 @@
             pltpu.SemaphoreType.DMA((2, 3)),
             pltpu.SemaphoreType.DMA((ny, 2)),
         ],
-        compiler_params=pltpu.CompilerParams(vmem_limit_bytes=56 * 1024 * 1024),
+        compiler_params=pltpu.CompilerParams(vmem_limit_bytes=48 * 1024 * 1024),
         cost_estimate=pl.CostEstimate(
             flops=20 * count * width * hidden,
             bytes_accessed=2 * (4 * count * width + 6 * width * hidden),
             transcendentals=2 * count * hidden,
         ),
-    )(info, rows, others, *slices)
+    )(rows, others, *slices)
 
 
 def shards(acts, cotangent, gain, router, ids, w_gate, w_up, w_down):
@@ -284,8 +292,6 @@
     parity = x % 2
     swap = [(0, 1), (1, 0)]
 
-    mine_parts = (w_gate[0].T, w_up[0].T, w_down[0])
-    mine = jnp.stack(mine_parts)
     ahead, behind = [], []
     for j in range(ny):
         for i in range(nx):
@@ -294,13 +300,12 @@
             ahead.append((at(j, i, 1 - a), at(j, i + 1, a)))
             behind.append((at(j, i, 1 - a), at(j, i - 1, a)))
             ahead.append((at(j, i, a), at(j ^ 1, i, a)))
+
+    names = 2 * jnp.arange(nz, dtype=jnp.int32) + parity
+    weights = (w_gate[0].T, w_up[0].T, w_down[0])
+    rows, sig, place, mine = front_rows(acts, cotangent, gain, router, ids, weights, nz, cap)
     left = lax.ppermute(mine, ("y", "x", "core"), behind)
     other = lax.ppermute(mine, ("y", "x", "core"), ahead)
-    info = (core == parity).astype(jnp.int32).reshape(1)
-
-    names = 2 * jnp.arange(nz, dtype=jnp.int32) + parity
-    flags = jnp.stack([parity, (x // 2 + y) % 2]).astype(jnp.int32)
-    rows, sig, place = front_rows(flags, acts, cotangent, gain, router, ids, nz, cap)
     sig = sig.T
     total = jnp.sum(sig, axis=1, keepdims=True)
     weight = sig / total
@@ -315,7 +320,7 @@
 
     pieces = part // LANE
     rank = -(-(pieces * cap + 4) // 8) * 8
-    keep, give = expert_rows(info, rows, others, (*mine_parts, left, other), ny, rank)
+    keep, give = expert_rows(rows, others, (mine, left, other), ny, rank)
     got = lax.ppermute(give, "core", swap)
     back = (keep.astype(f32) + got.astype(f32)).astype(bf16)
 

time: 145 us -> 233 us (1.61)
  Pallas kernels: 16.1 us -> 110 us
  other arithmetic: 9.21 us -> 3.93 us
  waiting for transfers between devices: 71.1 us -> 74 us
  starting transfers between devices: 41.7 us -> 39 us
    pallas_call x1, Pallas kernels: 4.52 us -> 96.2 us  [front_rows(): pl.pallas_call(functools.partial(front_kernel, cap), out_shape=(jax.Shape...]
    another operation x2 -> x0, other arithmetic: 4.11 us -> none  [the longest x1 3.55 us: shards(): mine = jnp.stack(mine_parts)]
    all_to_all x1, waiting for transfers between devices: 31.8 us -> 35.2 us  [shards(): rows = lax.all_to_all(rows, 'z', 0, 0, tiled=True)]
    ppermute x1, waiting for transfers between devices: 3.42 us -> 0.03 us  [shards(): other = lax.ppermute(mine, ('y', 'x', 'core'), ahead)]
    ppermute x1, waiting for transfers between devices: 0.01 us -> 3.11 us  [shards(): others = lax.ppermute(rows, 'core', swap)]
    all_to_all x1, starting transfers between devices: 13 us -> 10.1 us  [shards(): lax.all_to_all(back.reshape(ny * nz, rank, LANE), ('y', 'z'), 0, 0, tiled...]
  transfers between devices with their start and end apart: 7 -> 7, of which waited for: 5 -> 5; matrix products, arithmetic and copies ran while one was open for 3% -> 0% of each run, Pallas kernels for 0% -> 0%
where the time goes in v10:
time: 233 us; the launch traced here: 232 us
  Pallas kernels  110 us (47%)
  waiting for transfers between devices  74 us (32%)
  starting transfers between devices  39 us (17%)
  other arithmetic  3.93 us (2%)
  matrix products  2.47 us (1%)
    pallas_call x1, Pallas kernels, front_rows(): pl.pallas_call(functools.partial(front_kernel, cap), out_shape=(jax.Shape...  96.2 us
    all_to_all x1, waiting for transfers between devices, shards(): rows = lax.all_to_all(rows, 'z', 0, 0, tiled=True)  35.2 us
    all_to_all x1, waiting for transfers between devices, shards(): lax.all_to_all(back.reshape(ny * nz, rank, LANE), ('y', 'z'), 0, 0, tiled...  24.5 us
    pallas_call x1, Pallas kernels, expert_rows(): pl.pallas_call(functools.partial(expert_kernel, nz), out_shape=(jax.Shape...  13.8 us
    all_to_all x1, starting transfers between devices, shards(): rows = lax.all_to_all(rows, 'z', 0, 0, tiled=True)  10.9 us
    all_to_all x1, starting transfers between devices, shards(): lax.all_to_all(back.reshape(ny * nz, rank, LANE), ('y', 'z'), 0, 0, tiled...  10.1 us
    all_to_all x1, waiting for transfers between devices, shards(): packet = lax.all_to_all(packet, ('y', 'x'), 0, 0, tiled=True)  9.31 us
    all_to_all x1, starting transfers between devices, shards(): packet = lax.all_to_all(packet, ('y', 'x'), 0, 0, tiled=True)  6.07 us
  transfers between devices with their start and end apart: 7, of which 5 were waited for; matrix products, arithmetic and copies ran while one was open for 0% of the time, Pallas kernels for 0%

profile of v10, /device:TPU:1, one launch (start us, length us, event | category | flops | bytes accessed | tf_op | source)
XLA Modules:
  0.0 231.7 jit_solution(15697612246578878476)
XLA Ops:
  0.0 96.2 %shard_map.82 = (bf16[8,16,6528]{2,1,0:T(8,128)(2,1)}, f32[4,128]{1,0:T(4,128)}, s32[8,128]{1,0:T(8,128)}, bf16[3,168,3072]{2,1,0:T(8,128)(2,1)}) custom-call(bf16[128,3072]{1,0:T(8,128)(2,1)} %refs_0_.1, bf16[128,3072]{1,0:T(8,128)(2,1)} %refs_1_.1, f32[1,3072]{1,0:T(1,128)} %bitcast.74, bf16[16,3072]{1,0:T(8,128)(2,1)} %bitcast.67, s32[4,128]{1,0:T(4,128)} %bitcast.75, ...), custom_call_target="tpu_custom_call" | custom-call | flops 201326592 | bytes 3145728 | tf_op jit(solution)/shard_map/pallas_call | solution.py:99
  96.2 10.9 %all-to-all-start = ((bf16[8,16,6528]{2,1,0:T(8,128)(2,1)}), bf16[8,16,6528]{2,1,0:T(8,128)(2,1)S(1)}, u32[]{:S(2)}, u32[]{:S(2)}) async-start(bf16[8,16,6528]{2,1,0:T(8,128)(2,1)} %get-tuple-element.12), calls=%async_computation | async-start | bytes 3342336 | tf_op jit(solution)/shard_map/all_to_all | solution.py:318
  107.1 5.4 %collective-permute-start.1 = (bf16[3,168,3072]{2,1,0:T(8,128)(2,1)}, bf16[3,168,3072]{2,1,0:T(8,128)(2,1)}, u32[]{:S(2)}, u32[]{:S(2)}) collective-permute-start(bf16[3,168,3072]{2,1,0:T(8,128)(2,1)} %get-tuple-element.13.refs_0_), channel_id=1, source_target_pairs={{1,48},{16,1},{33,16},{48,33},{65,112},{80,65},{97,80},{112,97},{1... | collective-permute-start | bytes 9289736 | tf_op jit(solution)/shard_map/ppermute | solution.py:307
  112.5 1.9 collective-permute-start.2
  114.4 35.2 %all-to-all-done.rows_hbm = bf16[8,16,6528]{2,1,0:T(8,128)(2,1)S(1)} async-done(((bf16[8,16,6528]{2,1,0:T(8,128)(2,1)}), bf16[8,16,6528]{2,1,0:T(8,128)(2,1)S(1)}, u32[]{:S(2)}, u32[]{:S(2)}) %all-to-all-start) | async-done | bytes 1671200 | tf_op jit(solution)/shard_map/all_to_all | solution.py:318
  149.6 2.4 %collective-permute-start = (bf16[8,16,6528]{2,1,0:T(8,128)(2,1)S(1)}, bf16[8,16,6528]{2,1,0:T(8,128)(2,1)S(1)}, u32[]{:S(2)}, u32[]{:S(2)}) collective-permute-start(bf16[8,16,6528]{2,1,0:T(8,128)(2,1)S(1)} %all-to-all-done.rows_hbm), channel_id=1, source_target_pairs={{0,1},{1,0},{2,3},{3,2},{4,5},{5,4},{6,7},{7,6},{8,9},{9,8},{10,11... | collective-permute-start | bytes 5013512 | tf_op jit(solution)/shard_map/ppermute | solution.py:319
  152.0 3.1 %collective-permute-done.others_hbm = bf16[8,16,6528]{2,1,0:T(8,128)(2,1)S(1)} collective-permute-done((bf16[8,16,6528]{2,1,0:T(8,128)(2,1)S(1)}, bf16[8,16,6528]{2,1,0:T(8,128)(2,1)S(1)}, u32[]{:S(2)}, u32[]{:S(2)}) %collective-permute-start) | collective-permute-done | bytes 1671200 | tf_op jit(solution)/shard_map/ppermute | solution.py:319
  155.2 13.8 %shard_map.83 = (bf16[8,8,56,128]{3,2,1,0:T(8,128)(2,1)S(1)}, bf16[8,8,56,128]{3,2,1,0:T(8,128)(2,1)S(1)}) custom-call(bf16[8,16,6528]{2,1,0:T(8,128)(2,1)S(1)} %all-to-all-done.rows_hbm, bf16[8,16,6528]{2,1,0:T(8,128)(2,1)S(1)} %collective-permute-done.others_hbm, bf16[3,168,3072]{2,1,0:T(8,128)(2,1)} %get-tuple-element.13.refs_0_, ...), custom_call_target="tpu_custom_call" | custom-call | flops 2807562240 | bytes 12877824 | tf_op jit(solution)/shard_map/pallas_call | solution.py:254
  169.0 2.3 collective-permute-start.3
  171.5 1.9 collective-permute-done.3
  173.4 1.2 add_convert_fusion
  174.5 10.1 %all-to-all-start.1 = ((bf16[64,56,128]{2,1,0:T(8,128)(2,1)}), bf16[64,56,128]{2,1,0:T(8,128)(2,1)S(1)}, u32[]{:S(2)}, u32[]{:S(2)}) async-start(bf16[64,56,128]{2,1,0:T(8,128)(2,1)} %bitcast.9), calls=%async_computation.1 | async-start | bytes 1835008 | tf_op jit(solution)/shard_map/all_to_all | solution.py:327
  185.1 24.5 %all-to-all-done.1 = bf16[64,56,128]{2,1,0:T(8,128)(2,1)S(1)} async-done(((bf16[64,56,128]{2,1,0:T(8,128)(2,1)}), bf16[64,56,128]{2,1,0:T(8,128)(2,1)S(1)}, u32[]{:S(2)}, u32[]{:S(2)}) %all-to-all-start.1) | async-done | bytes 917536 | tf_op jit(solution)/shard_map/all_to_all | solution.py:327
  210.1 0.1 broadcast_in_dim.46
  210.2 0.4 convolution_convert_fusion
  210.7 0.1 broadcast_in_dim.44
  210.8 0.4 convolution_convert_fusion.1
  211.3 0.1 broadcast_in_dim.42
  211.4 0.4 convolution_convert_fusion.2
  212.1 0.7 copy.46
  212.7 6.1 %all-to-all-start.2 = ((bf16[32,16,128]{2,1,0:T(8,128)(2,1)}), bf16[32,16,128]{2,1,0:T(8,128)(2,1)S(1)}, u32[]{:S(2)}, u32[]{:S(2)}) async-start(bf16[32,16,128]{2,1,0:T(8,128)(2,1)} %copy.46), calls=%async_computation.2 | async-start | bytes 262144 | tf_op jit(solution)/shard_map/all_to_all | solution.py:359
  219.0 9.3 %all-to-all-done.2 = bf16[32,16,128]{2,1,0:T(8,128)(2,1)S(1)} async-done(((bf16[32,16,128]{2,1,0:T(8,128)(2,1)}), bf16[32,16,128]{2,1,0:T(8,128)(2,1)S(1)}, u32[]{:S(2)}, u32[]{:S(2)}) %all-to-all-start.2) | async-done | bytes 131104 | tf_op jit(solution)/shard_map/all_to_all | solution.py:359
  229.0 1.1 fusion.1
  230.2 1.5 fusion.5
  (54 shorter events, 2.1 us)
Async XLA Ops:
  96.2 53.4 %all-to-all-start = ((bf16[8,16,6528]{2,1,0:T(8,128)(2,1)}), bf16[8,16,6528]{2,1,0:T(8,128)(2,1)S(1)}, u32[]{:S(2)}, u32[]{:S(2)}) async-start(bf16[8,16,6528]{2,1,0:T(8,128)(2,1)} %get-tuple-element.12), calls=%async_computation | async-start | bytes 3342336 | tf_op jit(solution)/shard_map/all_to_all | solution.py:318
  107.1 64.2 %copy-start.2 = (s32[128,4]{0,1:T(4,128)S(1)}, s32[128,4]{0,1:T(4,128)}, u32[]{:S(2)}) copy-start(s32[128,4]{0,1:T(4,128)} %param.12) | copy-start | bytes 6148
  107.1 64.4 %copy-start.4 = (s32[8,128]{1,0:T(8,128)S(1)}, s32[8,128]{1,0:T(8,128)}, u32[]{:S(2)}) copy-start(s32[8,128]{1,0:T(8,128)} %get-tuple-element.11) | copy-start | bytes 12292
  107.1 44.9 %collective-permute-start.1 = (bf16[3,168,3072]{2,1,0:T(8,128)(2,1)}, bf16[3,168,3072]{2,1,0:T(8,128)(2,1)}, u32[]{:S(2)}, u32[]{:S(2)}) collective-permute-start(bf16[3,168,3072]{2,1,0:T(8,128)(2,1)} %get-tuple-element.13.refs_0_), channel_id=1, source_target_pairs={{1,48},{16,1},{33,16},{48,33},{65,112},{80,65},{97,80},{112,97},{1... | collective-permute-start | bytes 9289736 | tf_op jit(solution)/shard_map/ppermute | solution.py:307
  112.5 39.6 %collective-permute-start.2 = (bf16[3,168,3072]{2,1,0:T(8,128)(2,1)}, bf16[3,168,3072]{2,1,0:T(8,128)(2,1)}, u32[]{:S(2)}, u32[]{:S(2)}) collective-permute-start(bf16[3,168,3072]{2,1,0:T(8,128)(2,1)} %get-tuple-element.13.refs_0_), channel_id=1, source_target_pairs={{1,16},{0,64},{16,33},{17,81},{33,48},{32,96},{48,1},{49,113},{65,... | collective-permute-start | bytes 9289736 | tf_op jit(solution)/shard_map/ppermute | solution.py:308
  149.6 5.6 %collective-permute-start = (bf16[8,16,6528]{2,1,0:T(8,128)(2,1)S(1)}, bf16[8,16,6528]{2,1,0:T(8,128)(2,1)S(1)}, u32[]{:S(2)}, u32[]{:S(2)}) collective-permute-start(bf16[8,16,6528]{2,1,0:T(8,128)(2,1)S(1)} %all-to-all-done.rows_hbm), channel_id=1, source_target_pairs={{0,1},{1,0},{2,3},{3,2},{4,5},{5,4},{6,7},{7,6},{8,9},{9,8},{10,11... | collective-permute-start | bytes 5013512 | tf_op jit(solution)/shard_map/ppermute | solution.py:319
  169.0 4.4 %collective-permute-start.3 = (bf16[8,8,56,128]{3,2,1,0:T(8,128)(2,1)S(1)}, bf16[8,8,56,128]{3,2,1,0:T(8,128)(2,1)S(1)}, u32[]{:S(2)}, u32[]{:S(2)}) collective-permute-start(bf16[8,8,56,128]{3,2,1,0:T(8,128)(2,1)S(1)} %get-tuple-element.15), channel_id=1, source_target_pairs={{0,1},{1,0},{2,3},{3,2},{4,5},{5,4},{6,7},{7,6},{8,9},{9,8},{10,11... | collective-permute-start | bytes 2752520 | tf_op jit(solution)/shard_map/ppermute | solution.py:324
  174.5 35.0 %all-to-all-start.1 = ((bf16[64,56,128]{2,1,0:T(8,128)(2,1)}), bf16[64,56,128]{2,1,0:T(8,128)(2,1)S(1)}, u32[]{:S(2)}, u32[]{:S(2)}) async-start(bf16[64,56,128]{2,1,0:T(8,128)(2,1)} %bitcast.9), calls=%async_computation.1 | async-start | bytes 1835008 | tf_op jit(solution)/shard_map/all_to_all | solution.py:327
  211.3 7.6 %copy-start.3 = (f32[4,128]{1,0:T(4,128)S(1)}, f32[4,128]{1,0:T(4,128)}, u32[]{:S(2)}) copy-start(f32[4,128]{1,0:T(4,128)} %get-tuple-element.16) | copy-start | bytes 6148
  211.4 17.6 %copy-start = (bf16[3072,16]{0,1:T(8,128)(2,1)S(1)}, bf16[3072,16]{0,1:T(8,128)(2,1)}, u32[]{:S(2)}) copy-start(bf16[3072,16]{0,1:T(8,128)(2,1)} %param.11) | copy-start | bytes 294916
  211.4 17.6 %copy-start.1 = (f32[3072]{0:T(1024)S(1)}, f32[3072]{0:T(1024)}, u32[]{:S(2)}) copy-start(f32[3072]{0:T(1024)} %param.10) | copy-start | bytes 36868
  212.7 15.5 %all-to-all-start.2 = ((bf16[32,16,128]{2,1,0:T(8,128)(2,1)}), bf16[32,16,128]{2,1,0:T(8,128)(2,1)S(1)}, u32[]{:S(2)}, u32[]{:S(2)}) async-start(bf16[32,16,128]{2,1,0:T(8,128)(2,1)} %copy.46), calls=%async_computation.2 | async-start | bytes 262144 | tf_op jit(solution)/shard_map/all_to_all | solution.py:359

commit v11 on v10

--- a/solution.py
+++ b/solution.py
@@ -20,17 +20,12 @@
 
 
 def front_kernel(cap, *refs):
-    sources, weights, (out, sig_ref, place_ref, stacked) = refs[:5], refs[5:8], refs[8:12]
-    copied, sem, stack_sem = refs[12:17], refs[17], refs[18]
+    sources, (out, sig_ref, place_ref), copied, sem = refs[:5], refs[5:8], refs[8:13], refs[13]
     copies = [
         pltpu.make_async_copy(source, ref, sem.at[i])
         for i, (source, ref) in enumerate(zip(sources, copied))
     ]
-    stacking = [
-        pltpu.make_async_copy(weight, stacked.at[j], stack_sem.at[j])
-        for j, weight in enumerate(weights)
-    ]
-    for copy in copies + stacking:
+    for copy in copies:
         copy.start()
     for copy in copies:
         copy.wait()
@@ -88,11 +83,9 @@
     for z in range(nz):
         lines = [v[z : z + 1, i * fold : (i + 1) * fold] for v in folded for i in range(main // 2)]
         out[z, :, 2 * width :] = jnp.concatenate(lines, axis=0).astype(bf16)
-    for copy in stacking:
-        copy.wait()
-
-
-def front_rows(acts, cotangent, gain, router, ids, weights, nz, cap):
+
+
+def front_rows(acts, cotangent, gain, router, ids, nz, cap):
     tokens, width = acts.shape
     vmem, hbm = (pl.BlockSpec(memory_space=m) for m in (pltpu.VMEM, pl.ANY))
     values = (acts, cotangent, gain.reshape(1, width), router.T, ids.T)
@@ -102,19 +95,18 @@
             jax.ShapeDtypeStruct((nz, MAIN, 2 * width + 2 * width // MAIN), bf16),
             jax.ShapeDtypeStruct(ids.T.shape, f32),
             jax.ShapeDtypeStruct((nz, tokens), jnp.int32),
-            jax.ShapeDtypeStruct((3, *weights[0].shape), bf16),
         ),
-        in_specs=[hbm] * 8,
-        out_specs=(vmem, vmem, vmem, hbm),
+        in_specs=[hbm] * 5,
+        out_specs=(vmem, vmem, vmem),
         scratch_shapes=[pltpu.VMEM(v.shape, v.dtype) for v in values]
-        + [pltpu.SemaphoreType.DMA((5,)), pltpu.SemaphoreType.DMA((3,))],
+        + [pltpu.SemaphoreType.DMA((5,))],
         compiler_params=pltpu.CompilerParams(vmem_limit_bytes=60 * 1024 * 1024),
         cost_estimate=pl.CostEstimate(
             flops=4 * tokens * tokens * width,
             bytes_accessed=4 * tokens * width + 4 * nz * MAIN * width,
             transcendentals=tokens * 5,
         ),
-    )(*values, *weights)
+    )(*values)
 
 
 def expert_kernel(nz, rows_hbm, others_hbm, *refs):
@@ -302,8 +294,8 @@
             ahead.append((at(j, i, a), at(j ^ 1, i, a)))
 
     names = 2 * jnp.arange(nz, dtype=jnp.int32) + parity
-    weights = (w_gate[0].T, w_up[0].T, w_down[0])
-    rows, sig, place, mine = front_rows(acts, cotangent, gain, router, ids, weights, nz, cap)
+    rows, sig, place = front_rows(acts, cotangent, gain, router, ids, nz, cap)
+    mine = jnp.stack([w_gate[0].T, w_up[0].T, w_down[0]])
     left = lax.ppermute(mine, ("y", "x", "core"), behind)
     other = lax.ppermute(mine, ("y", "x", "core"), ahead)
     sig = sig.T

time: 233 us -> 144 us (0.62)
  Pallas kernels: 110 us -> 17.8 us
  other arithmetic: 3.93 us -> 7.45 us
  waiting for transfers between devices: 74 us -> 71.1 us
  starting transfers between devices: 39 us -> 41.6 us
    pallas_call x1, Pallas kernels: 96.2 us -> 3.94 us  [front_rows(): pl.pallas_call(functools.partial(front_kernel, cap), out_shape=(jax.Shape...]
    another operation x0 -> x1, other arithmetic: none -> 3.51 us  [shards(): mine = jnp.stack([w_gate[0].T, w_up[0].T, w_down[0]])]
    ppermute x1, waiting for transfers between devices: 0.03 us -> 3.52 us  [shards(): other = lax.ppermute(mine, ('y', 'x', 'core'), ahead)]
    all_to_all x1, waiting for transfers between devices: 35.2 us -> 31.7 us  [shards(): rows = lax.all_to_all(rows, 'z', 0, 0, tiled=True)]
    all_to_all x1, starting transfers between devices: 10.1 us -> 13.4 us  [shards(): lax.all_to_all(back.reshape(ny * nz, rank, LANE), ('y', 'z'), 0, 0, tiled...]
    ppermute x1, waiting for transfers between devices: 3.11 us -> 0.01 us  [shards(): others = lax.ppermute(rows, 'core', swap)]
  transfers between devices with their start and end apart: 7 -> 7, of which waited for: 5 -> 5; matrix products, arithmetic and copies ran while one was open for 0% -> 3% of each run, Pallas kernels for 0% -> 0%
where the time goes in v11:
time: 144 us; the launch traced here: 143 us
  waiting for transfers between devices  71.1 us (49%)
  starting transfers between devices  41.6 us (29%)
  Pallas kernels  17.8 us (12%)
  other arithmetic  7.45 us (5%)
  matrix products  2.46 us (2%)
  local copies, waits for them, and re-layouts  1.9 us (1%)
    all_to_all x1, waiting for transfers between devices, shards(): rows = lax.all_to_all(rows, 'z', 0, 0, tiled=True)  31.7 us
    all_to_all x1, waiting for transfers between devices, shards(): lax.all_to_all(back.reshape(ny * nz, rank, LANE), ('y', 'z'), 0, 0, tiled...  24.3 us
    pallas_call x1, Pallas kernels, expert_rows(): pl.pallas_call(functools.partial(expert_kernel, nz), out_shape=(jax.Shape...  13.8 us
    all_to_all x1, starting transfers between devices, shards(): lax.all_to_all(back.reshape(ny * nz, rank, LANE), ('y', 'z'), 0, 0, tiled...  13.4 us
    all_to_all x1, starting transfers between devices, shards(): rows = lax.all_to_all(rows, 'z', 0, 0, tiled=True)  10.9 us
    all_to_all x1, waiting for transfers between devices, shards(): packet = lax.all_to_all(packet, ('y', 'x'), 0, 0, tiled=True)  9.31 us
    all_to_all x1, starting transfers between devices, shards(): packet = lax.all_to_all(packet, ('y', 'x'), 0, 0, tiled=True)  5.81 us
    ppermute x1, starting transfers between devices, shards(): left = lax.ppermute(mine, ('y', 'x', 'core'), behind)  5.34 us
  transfers between devices with their start and end apart: 7, of which 5 were waited for; matrix products, arithmetic and copies ran while one was open for 3% of the time, Pallas kernels for 0%

profile of v11, /device:TPU:1, one launch (start us, length us, event | category | flops | bytes accessed | tf_op | source)
XLA Modules:
  0.0 142.7 jit_solution(10550841555590162380)
XLA Ops:
  0.0 3.9 %shard_map.82 = (bf16[8,16,6528]{2,1,0:T(8,128)(2,1)}, f32[4,128]{1,0:T(4,128)}, s32[8,128]{1,0:T(8,128)}) custom-call(bf16[128,3072]{1,0:T(8,128)(2,1)} %refs_0_.1, bf16[128,3072]{1,0:T(8,128)(2,1)} %refs_1_.1, f32[1,3072]{1,0:T(1,128)} %bitcast.76, bf16[16,3072]{1,0:T(8,128)(2,1)} %bitcast.69, s32[4,128]{1,0:T(4,128)} %bitcast.77), custom_call_target="tpu_custom_call" | custom-call | flops 201326592 | bytes 3145728 | tf_op jit(solution)/shard_map/pallas_call | solution.py:92
  3.9 10.9 %all-to-all-start = ((bf16[8,16,6528]{2,1,0:T(8,128)(2,1)}), bf16[8,16,6528]{2,1,0:T(8,128)(2,1)S(1)}, u32[]{:S(2)}, u32[]{:S(2)}) async-start(bf16[8,16,6528]{2,1,0:T(8,128)(2,1)} %get-tuple-element.11), calls=%async_computation | async-start | bytes 3342336 | tf_op jit(solution)/shard_map/all_to_all | solution.py:310
  14.8 3.5 %pad_maximum_fusion.refs_0_ = bf16[3,168,3072]{2,1,0:T(8,128)(2,1)} fusion(bf16[1,168,3072]{2,1,0:T(8,128)(2,1)S(1)} %copy-done, bf16[1,168,3072]{2,1,0:T(8,128)(2,1)} %bitcast.65, bf16[1,168,3072]{2,1,0:T(8,128)(2,1)} %bitcast.66), kind=kLoop, calls=%fused_computation.2 | loop fusion | flops 3096576 | bytes 6193152 | tf_op jit(solution)/shard_map/stack | solution.py:298
  18.4 5.3 %collective-permute-start.1 = (bf16[3,168,3072]{2,1,0:T(8,128)(2,1)}, bf16[3,168,3072]{2,1,0:T(8,128)(2,1)}, u32[]{:S(2)}, u32[]{:S(2)}) collective-permute-start(bf16[3,168,3072]{2,1,0:T(8,128)(2,1)} %pad_maximum_fusion.refs_0_), channel_id=1, source_target_pairs={{1,48},{16,1},{33,16},{48,33},{65,112},{80,65},{97,80},{112,97},{1... | collective-permute-start | bytes 9289736 | tf_op jit(solution)/shard_map/ppermute | solution.py:299
  23.7 1.9 %collective-permute-start.2 = (bf16[3,168,3072]{2,1,0:T(8,128)(2,1)}, bf16[3,168,3072]{2,1,0:T(8,128)(2,1)}, u32[]{:S(2)}, u32[]{:S(2)}) collective-permute-start(bf16[3,168,3072]{2,1,0:T(8,128)(2,1)} %pad_maximum_fusion.refs_0_), channel_id=1, source_target_pairs={{1,16},{0,64},{16,33},{17,81},{33,48},{32,96},{48,1},{49,113},{65,... | collective-permute-start | bytes 9289736 | tf_op jit(solution)/shard_map/ppermute | solution.py:300
  25.6 31.7 %all-to-all-done.rows_hbm = bf16[8,16,6528]{2,1,0:T(8,128)(2,1)S(1)} async-done(((bf16[8,16,6528]{2,1,0:T(8,128)(2,1)}), bf16[8,16,6528]{2,1,0:T(8,128)(2,1)S(1)}, u32[]{:S(2)}, u32[]{:S(2)}) %all-to-all-start) | async-done | bytes 1671200 | tf_op jit(solution)/shard_map/all_to_all | solution.py:310
  57.4 2.4 %collective-permute-start = (bf16[8,16,6528]{2,1,0:T(8,128)(2,1)S(1)}, bf16[8,16,6528]{2,1,0:T(8,128)(2,1)S(1)}, u32[]{:S(2)}, u32[]{:S(2)}) collective-permute-start(bf16[8,16,6528]{2,1,0:T(8,128)(2,1)S(1)} %all-to-all-done.rows_hbm), channel_id=1, source_target_pairs={{0,1},{1,0},{2,3},{3,2},{4,5},{5,4},{6,7},{7,6},{8,9},{9,8},{10,11... | collective-permute-start | bytes 5013512 | tf_op jit(solution)/shard_map/ppermute | solution.py:311
  59.8 3.5 %collective-permute-done.2.refs_2_ = bf16[3,168,3072]{2,1,0:T(8,128)(2,1)} collective-permute-done((bf16[3,168,3072]{2,1,0:T(8,128)(2,1)}, bf16[3,168,3072]{2,1,0:T(8,128)(2,1)}, u32[]{:S(2)}, u32[]{:S(2)}) %collective-permute-start.2) | collective-permute-done | bytes 3096608 | tf_op jit(solution)/shard_map/ppermute | solution.py:300
  63.3 13.8 %shard_map.83 = (bf16[8,8,56,128]{3,2,1,0:T(8,128)(2,1)S(1)}, bf16[8,8,56,128]{3,2,1,0:T(8,128)(2,1)S(1)}) custom-call(bf16[8,16,6528]{2,1,0:T(8,128)(2,1)S(1)} %all-to-all-done.rows_hbm, bf16[8,16,6528]{2,1,0:T(8,128)(2,1)S(1)} %collective-permute-done.others_hbm, bf16[3,168,3072]{2,1,0:T(8,128)(2,1)} %pad_maximum_fusion.refs_0_, ...), custom_call_target="tpu_custom_call" | custom-call | flops 2807562240 | bytes 12877824 | tf_op jit(solution)/shard_map/pallas_call | solution.py:246
  77.1 1.9 %collective-permute-start.3 = (bf16[8,8,56,128]{3,2,1,0:T(8,128)(2,1)S(1)}, bf16[8,8,56,128]{3,2,1,0:T(8,128)(2,1)S(1)}, u32[]{:S(2)}, u32[]{:S(2)}) collective-permute-start(bf16[8,8,56,128]{3,2,1,0:T(8,128)(2,1)S(1)} %get-tuple-element.13), channel_id=1, source_target_pairs={{0,1},{1,0},{2,3},{3,2},{4,5},{5,4},{6,7},{7,6},{8,9},{9,8},{10,11... | collective-permute-start | bytes 2752520 | tf_op jit(solution)/shard_map/ppermute | solution.py:316
  79.3 2.2 %collective-permute-done.3 = bf16[8,8,56,128]{3,2,1,0:T(8,128)(2,1)S(1)} collective-permute-done((bf16[8,8,56,128]{3,2,1,0:T(8,128)(2,1)S(1)}, bf16[8,8,56,128]{3,2,1,0:T(8,128)(2,1)S(1)}, u32[]{:S(2)}, u32[]{:S(2)}) %collective-permute-start.3) | collective-permute-done | bytes 917536 | tf_op jit(solution)/shard_map/ppermute | solution.py:316
  81.5 1.2 add_convert_fusion
  82.7 13.4 %all-to-all-start.1 = ((bf16[64,56,128]{2,1,0:T(8,128)(2,1)}), bf16[64,56,128]{2,1,0:T(8,128)(2,1)S(1)}, u32[]{:S(2)}, u32[]{:S(2)}) async-start(bf16[64,56,128]{2,1,0:T(8,128)(2,1)} %bitcast.10), calls=%async_computation.1 | async-start | bytes 1835008 | tf_op jit(solution)/shard_map/all_to_all | solution.py:319
  96.5 24.3 %all-to-all-done.1 = bf16[64,56,128]{2,1,0:T(8,128)(2,1)S(1)} async-done(((bf16[64,56,128]{2,1,0:T(8,128)(2,1)}), bf16[64,56,128]{2,1,0:T(8,128)(2,1)S(1)}, u32[]{:S(2)}, u32[]{:S(2)}) %all-to-all-start.1) | async-done | bytes 917536 | tf_op jit(solution)/shard_map/all_to_all | solution.py:319
  121.4 0.1 broadcast_in_dim.46
  121.5 0.4 convolution_convert_fusion
  122.1 0.4 convolution_convert_fusion.1
  122.6 0.1 broadcast_in_dim.42
  122.7 0.4 convolution_convert_fusion.2
  123.3 0.7 copy.46
  124.0 5.8 %all-to-all-start.2 = ((bf16[32,16,128]{2,1,0:T(8,128)(2,1)}), bf16[32,16,128]{2,1,0:T(8,128)(2,1)S(1)}, u32[]{:S(2)}, u32[]{:S(2)}) async-start(bf16[32,16,128]{2,1,0:T(8,128)(2,1)} %copy.46), calls=%async_computation.2 | async-start | bytes 262144 | tf_op jit(solution)/shard_map/all_to_all | solution.py:351
  130.0 9.3 %all-to-all-done.2 = bf16[32,16,128]{2,1,0:T(8,128)(2,1)S(1)} async-done(((bf16[32,16,128]{2,1,0:T(8,128)(2,1)}), bf16[32,16,128]{2,1,0:T(8,128)(2,1)S(1)}, u32[]{:S(2)}, u32[]{:S(2)}) %all-to-all-start.2) | async-done | bytes 131104 | tf_op jit(solution)/shard_map/all_to_all | solution.py:351
  140.0 1.1 fusion.1
  141.2 1.5 %fusion.5 = f32[1,4,3072]{2,1,0:T(4,128)} fusion(f32[4,3072]{1,0:T(4,128)S(1)} %get-tuple-element.33, f32[4]{0:T(128)S(1)} %broadcast_multiply_fusion, f32[4]{0:T(128)S(1)} %get-tuple-element.32, f32[4]{0:T(128)S(1)} %get-tuple-element.31, bf16[128,3072]{1,0:T(8,128)(2,1)} %refs_1_.1, s32[]{:T(128)S(6)} %select_n.89, bf16[128,3072]{1,0:T(8,128)(2,1)} %refs_0_.1), kind=kLoop, calls=%fused_computation.29 | loop fusion | flops 86016 | bytes 147508 | tf_op jit(solution)/shard_map/broadcast_in_dim | solution.py:374
  (57 shorter events, 2.2 us)
Async XLA Ops:
  0.0 14.8 %copy-start = (bf16[1,168,3072]{2,1,0:T(8,128)(2,1)S(1)}, bf16[1,168,3072]{2,1,0:T(8,128)(2,1)}, u32[]{:S(2)}) copy-start(bf16[1,168,3072]{2,1,0:T(8,128)(2,1)} %param.15) | copy-start | bytes 3096580
  3.9 53.4 %all-to-all-start = ((bf16[8,16,6528]{2,1,0:T(8,128)(2,1)}), bf16[8,16,6528]{2,1,0:T(8,128)(2,1)S(1)}, u32[]{:S(2)}, u32[]{:S(2)}) async-start(bf16[8,16,6528]{2,1,0:T(8,128)(2,1)} %get-tuple-element.11), calls=%async_computation | async-start | bytes 3342336 | tf_op jit(solution)/shard_map/all_to_all | solution.py:310
  18.4 60.8 %copy-start.3 = (s32[128,4]{0,1:T(4,128)S(1)}, s32[128,4]{0,1:T(4,128)}, u32[]{:S(2)}) copy-start(s32[128,4]{0,1:T(4,128)} %param.12) | copy-start | bytes 6148
  18.4 60.9 %copy-start.5 = (s32[8,128]{1,0:T(8,128)S(1)}, s32[8,128]{1,0:T(8,128)}, u32[]{:S(2)}) copy-start(s32[8,128]{1,0:T(8,128)} %get-tuple-element.10) | copy-start | bytes 12292
  18.4 41.4 %collective-permute-start.1 = (bf16[3,168,3072]{2,1,0:T(8,128)(2,1)}, bf16[3,168,3072]{2,1,0:T(8,128)(2,1)}, u32[]{:S(2)}, u32[]{:S(2)}) collective-permute-start(bf16[3,168,3072]{2,1,0:T(8,128)(2,1)} %pad_maximum_fusion.refs_0_), channel_id=1, source_target_pairs={{1,48},{16,1},{33,16},{48,33},{65,112},{80,65},{97,80},{112,97},{1... | collective-permute-start | bytes 9289736 | tf_op jit(solution)/shard_map/ppermute | solution.py:299
  23.7 39.6 %collective-permute-start.2 = (bf16[3,168,3072]{2,1,0:T(8,128)(2,1)}, bf16[3,168,3072]{2,1,0:T(8,128)(2,1)}, u32[]{:S(2)}, u32[]{:S(2)}) collective-permute-start(bf16[3,168,3072]{2,1,0:T(8,128)(2,1)} %pad_maximum_fusion.refs_0_), channel_id=1, source_target_pairs={{1,16},{0,64},{16,33},{17,81},{33,48},{32,96},{48,1},{49,113},{65,... | collective-permute-start | bytes 9289736 | tf_op jit(solution)/shard_map/ppermute | solution.py:300
  57.4 5.9 %collective-permute-start = (bf16[8,16,6528]{2,1,0:T(8,128)(2,1)S(1)}, bf16[8,16,6528]{2,1,0:T(8,128)(2,1)S(1)}, u32[]{:S(2)}, u32[]{:S(2)}) collective-permute-start(bf16[8,16,6528]{2,1,0:T(8,128)(2,1)S(1)} %all-to-all-done.rows_hbm), channel_id=1, source_target_pairs={{0,1},{1,0},{2,3},{3,2},{4,5},{5,4},{6,7},{7,6},{8,9},{9,8},{10,11... | collective-permute-start | bytes 5013512 | tf_op jit(solution)/shard_map/ppermute | solution.py:311
  77.1 4.4 %collective-permute-start.3 = (bf16[8,8,56,128]{3,2,1,0:T(8,128)(2,1)S(1)}, bf16[8,8,56,128]{3,2,1,0:T(8,128)(2,1)S(1)}, u32[]{:S(2)}, u32[]{:S(2)}) collective-permute-start(bf16[8,8,56,128]{3,2,1,0:T(8,128)(2,1)S(1)} %get-tuple-element.13), channel_id=1, source_target_pairs={{0,1},{1,0},{2,3},{3,2},{4,5},{5,4},{6,7},{7,6},{8,9},{9,8},{10,11... | collective-permute-start | bytes 2752520 | tf_op jit(solution)/shard_map/ppermute | solution.py:316
  82.7 38.1 %all-to-all-start.1 = ((bf16[64,56,128]{2,1,0:T(8,128)(2,1)}), bf16[64,56,128]{2,1,0:T(8,128)(2,1)S(1)}, u32[]{:S(2)}, u32[]{:S(2)}) async-start(bf16[64,56,128]{2,1,0:T(8,128)(2,1)} %bitcast.10), calls=%async_computation.1 | async-start | bytes 1835008 | tf_op jit(solution)/shard_map/all_to_all | solution.py:319
  122.1 7.8 %copy-start.4 = (f32[4,128]{1,0:T(4,128)S(1)}, f32[4,128]{1,0:T(4,128)}, u32[]{:S(2)}) copy-start(f32[4,128]{1,0:T(4,128)} %get-tuple-element.14) | copy-start | bytes 6148
  122.1 17.9 %copy-start.1 = (bf16[3072,16]{0,1:T(8,128)(2,1)S(1)}, bf16[3072,16]{0,1:T(8,128)(2,1)}, u32[]{:S(2)}) copy-start(bf16[3072,16]{0,1:T(8,128)(2,1)} %param.11) | copy-start | bytes 294916
  122.1 17.9 %copy-start.2 = (f32[3072]{0:T(1024)S(1)}, f32[3072]{0:T(1024)}, u32[]{:S(2)}) copy-start(f32[3072]{0:T(1024)} %param.10) | copy-start | bytes 36868
  124.0 15.3 %all-to-all-start.2 = ((bf16[32,16,128]{2,1,0:T(8,128)(2,1)}), bf16[32,16,128]{2,1,0:T(8,128)(2,1)S(1)}, u32[]{:S(2)}, u32[]{:S(2)}) async-start(bf16[32,16,128]{2,1,0:T(8,128)(2,1)} %copy.46), calls=%async_computation.2 | async-start | bytes 262144 | tf_op jit(solution)/shard_map/all_to_all | solution.py:351

commit v12 on v10

--- a/solution.py
+++ b/solution.py
@@ -21,16 +21,20 @@
 
 def front_kernel(cap, *refs):
     sources, weights, (out, sig_ref, place_ref, stacked) = refs[:5], refs[5:8], refs[8:12]
-    copied, sem, stack_sem = refs[12:17], refs[17], refs[18]
+    copied, held, sem, stack_sem = refs[12:17], refs[17], refs[18], refs[19]
     copies = [
         pltpu.make_async_copy(source, ref, sem.at[i])
         for i, (source, ref) in enumerate(zip(sources, copied))
     ]
-    stacking = [
-        pltpu.make_async_copy(weight, stacked.at[j], stack_sem.at[j])
+    loads = [
+        pltpu.make_async_copy(weight, held.at[j], stack_sem.at[0, j])
         for j, weight in enumerate(weights)
     ]
-    for copy in copies + stacking:
+    stores = [
+        pltpu.make_async_copy(held.at[j], stacked.at[j], stack_sem.at[1, j])
+        for j in range(len(weights))
+    ]
+    for copy in copies + loads:
         copy.start()
     for copy in copies:
         copy.wait()
@@ -47,6 +51,9 @@
     logits = lax.dot_general(
         router[...], h, (((1,), (1,)), ((), ())), preferred_element_type=f32
     )
+    for load, store in zip(loads, stores):
+        load.wait()
+        store.start()
     named = lax.broadcasted_iota(jnp.int32, logits.shape, 0)
     sig = []
     for k in range(top):
@@ -88,8 +95,8 @@
     for z in range(nz):
         lines = [v[z : z + 1, i * fold : (i + 1) * fold] for v in folded for i in range(main // 2)]
         out[z, :, 2 * width :] = jnp.concatenate(lines, axis=0).astype(bf16)
-    for copy in stacking:
-        copy.wait()
+    for store in stores:
+        store.wait()
 
 
 def front_rows(acts, cotangent, gain, router, ids, weights, nz, cap):
@@ -107,7 +114,8 @@
         in_specs=[hbm] * 8,
         out_specs=(vmem, vmem, vmem, hbm),
         scratch_shapes=[pltpu.VMEM(v.shape, v.dtype) for v in values]
-        + [pltpu.SemaphoreType.DMA((5,)), pltpu.SemaphoreType.DMA((3,))],
+        + [pltpu.VMEM((3, *weights[0].shape), bf16)]
+        + [pltpu.SemaphoreType.DMA((5,)), pltpu.SemaphoreType.DMA((2, 3))],
         compiler_params=pltpu.CompilerParams(vmem_limit_bytes=60 * 1024 * 1024),
         cost_estimate=pl.CostEstimate(
             flops=4 * tokens * tokens * width,
@@ -270,7 +278,7 @@
             pltpu.SemaphoreType.DMA((2, 3)),
             pltpu.SemaphoreType.DMA((ny, 2)),
         ],
-        compiler_params=pltpu.CompilerParams(vmem_limit_bytes=48 * 1024 * 1024),
+        compiler_params=pltpu.CompilerParams(vmem_limit_bytes=51 * 1024 * 1024),
         cost_estimate=pl.CostEstimate(
             flops=20 * count * width * hidden,
             bytes_accessed=2 * (4 * count * width + 6 * width * hidden),

time: 233 us -> 144 us (0.62)
  Pallas kernels: 110 us -> 19.7 us
    pallas_call x1, Pallas kernels: 96.2 us -> 5.51 us  [front_rows(): pl.pallas_call(functools.partial(front_kernel, cap), out_shape=(jax.Shape...]
where the time goes in v12:
time: 144 us; the launch traced here: 143 us
  waiting for transfers between devices  74 us (51%)
  starting transfers between devices  39 us (27%)
  Pallas kernels  19.7 us (14%)
  other arithmetic  3.93 us (3%)
  local copies, waits for them, and re-layouts  3.07 us (2%)
  matrix products  2.47 us (2%)
    all_to_all x1, waiting for transfers between devices, shards(): rows = lax.all_to_all(rows, 'z', 0, 0, tiled=True)  35.2 us
    all_to_all x1, waiting for transfers between devices, shards(): lax.all_to_all(back.reshape(ny * nz, rank, LANE), ('y', 'z'), 0, 0, tiled...  24.5 us
    pallas_call x1, Pallas kernels, expert_rows(): pl.pallas_call(functools.partial(expert_kernel, nz), out_shape=(jax.Shape...  14.2 us
    all_to_all x1, starting transfers between devices, shards(): rows = lax.all_to_all(rows, 'z', 0, 0, tiled=True)  10.9 us
    all_to_all x1, starting transfers between devices, shards(): lax.all_to_all(back.reshape(ny * nz, rank, LANE), ('y', 'z'), 0, 0, tiled...  10.1 us
    all_to_all x1, waiting for transfers between devices, shards(): packet = lax.all_to_all(packet, ('y', 'x'), 0, 0, tiled=True)  9.31 us
    all_to_all x1, starting transfers between devices, shards(): packet = lax.all_to_all(packet, ('y', 'x'), 0, 0, tiled=True)  6.07 us
    pallas_call x1, Pallas kernels, front_rows(): pl.pallas_call(functools.partial(front_kernel, cap), out_shape=(jax.Shape...  5.51 us
  transfers between devices with their start and end apart: 7, of which 5 were waited for; matrix products, arithmetic and copies ran while one was open for 0% of the time, Pallas kernels for 0%

profile of v12, /device:TPU:1, one launch (start us, length us, event | category | flops | bytes accessed | tf_op | source)
XLA Modules:
  0.0 142.6 jit_solution(8037058087522700063)
XLA Ops:
  0.0 5.5 %shard_map.82 = (bf16[8,16,6528]{2,1,0:T(8,128)(2,1)}, f32[4,128]{1,0:T(4,128)}, s32[8,128]{1,0:T(8,128)}, bf16[3,168,3072]{2,1,0:T(8,128)(2,1)}) custom-call(bf16[128,3072]{1,0:T(8,128)(2,1)} %refs_0_.1, bf16[128,3072]{1,0:T(8,128)(2,1)} %refs_1_.1, f32[1,3072]{1,0:T(1,128)} %bitcast.74, bf16[16,3072]{1,0:T(8,128)(2,1)} %bitcast.67, s32[4,128]{1,0:T(4,128)} %bitcast.75, ...), custom_call_target="tpu_custom_call" | custom-call | flops 201326592 | bytes 3145728 | tf_op jit(solution)/shard_map/pallas_call | solution.py:106
  5.5 10.9 %all-to-all-start = ((bf16[8,16,6528]{2,1,0:T(8,128)(2,1)}), bf16[8,16,6528]{2,1,0:T(8,128)(2,1)S(1)}, u32[]{:S(2)}, u32[]{:S(2)}) async-start(bf16[8,16,6528]{2,1,0:T(8,128)(2,1)} %get-tuple-element.12), calls=%async_computation | async-start | bytes 3342336 | tf_op jit(solution)/shard_map/all_to_all | solution.py:326
  16.4 5.4 %collective-permute-start.1 = (bf16[3,168,3072]{2,1,0:T(8,128)(2,1)}, bf16[3,168,3072]{2,1,0:T(8,128)(2,1)}, u32[]{:S(2)}, u32[]{:S(2)}) collective-permute-start(bf16[3,168,3072]{2,1,0:T(8,128)(2,1)} %get-tuple-element.13.refs_0_), channel_id=1, source_target_pairs={{1,48},{16,1},{33,16},{48,33},{65,112},{80,65},{97,80},{112,97},{1... | collective-permute-start | bytes 9289736 | tf_op jit(solution)/shard_map/ppermute | solution.py:315
  21.8 1.9 %collective-permute-start.2 = (bf16[3,168,3072]{2,1,0:T(8,128)(2,1)}, bf16[3,168,3072]{2,1,0:T(8,128)(2,1)}, u32[]{:S(2)}, u32[]{:S(2)}) collective-permute-start(bf16[3,168,3072]{2,1,0:T(8,128)(2,1)} %get-tuple-element.13.refs_0_), channel_id=1, source_target_pairs={{1,16},{0,64},{16,33},{17,81},{33,48},{32,96},{48,1},{49,113},{65,... | collective-permute-start | bytes 9289736 | tf_op jit(solution)/shard_map/ppermute | solution.py:316
  23.7 35.2 %all-to-all-done.rows_hbm = bf16[8,16,6528]{2,1,0:T(8,128)(2,1)S(1)} async-done(((bf16[8,16,6528]{2,1,0:T(8,128)(2,1)}), bf16[8,16,6528]{2,1,0:T(8,128)(2,1)S(1)}, u32[]{:S(2)}, u32[]{:S(2)}) %all-to-all-start) | async-done | bytes 1671200 | tf_op jit(solution)/shard_map/all_to_all | solution.py:326
  58.9 2.4 %collective-permute-start = (bf16[8,16,6528]{2,1,0:T(8,128)(2,1)S(1)}, bf16[8,16,6528]{2,1,0:T(8,128)(2,1)S(1)}, u32[]{:S(2)}, u32[]{:S(2)}) collective-permute-start(bf16[8,16,6528]{2,1,0:T(8,128)(2,1)S(1)} %all-to-all-done.rows_hbm), channel_id=1, source_target_pairs={{0,1},{1,0},{2,3},{3,2},{4,5},{5,4},{6,7},{7,6},{8,9},{9,8},{10,11... | collective-permute-start | bytes 5013512 | tf_op jit(solution)/shard_map/ppermute | solution.py:327
  61.4 3.1 %collective-permute-done.others_hbm = bf16[8,16,6528]{2,1,0:T(8,128)(2,1)S(1)} collective-permute-done((bf16[8,16,6528]{2,1,0:T(8,128)(2,1)S(1)}, bf16[8,16,6528]{2,1,0:T(8,128)(2,1)S(1)}, u32[]{:S(2)}, u32[]{:S(2)}) %collective-permute-start) | collective-permute-done | bytes 1671200 | tf_op jit(solution)/shard_map/ppermute | solution.py:327
  64.5 1.2 copy-done.1
  65.7 14.2 %shard_map.83 = (bf16[8,8,56,128]{3,2,1,0:T(8,128)(2,1)S(1)}, bf16[8,8,56,128]{3,2,1,0:T(8,128)(2,1)S(1)}) custom-call(bf16[8,16,6528]{2,1,0:T(8,128)(2,1)} %copy-done, bf16[8,16,6528]{2,1,0:T(8,128)(2,1)} %copy-done.1, bf16[3,168,3072]{2,1,0:T(8,128)(2,1)} %get-tuple-element.13.refs_0_, bf16[3,168,3072]{2,1,0:T(8,128)(2,1)} %collective-permute-done.1.refs_1_, ...), custom_call_target="tpu_custom_call" | custom-call | flops 2807562240 | bytes 12877824 | tf_op jit(solution)/shard_map/pallas_call | solution.py:262
  79.9 2.3 %collective-permute-start.3 = (bf16[8,8,56,128]{3,2,1,0:T(8,128)(2,1)S(1)}, bf16[8,8,56,128]{3,2,1,0:T(8,128)(2,1)S(1)}, u32[]{:S(2)}, u32[]{:S(2)}) collective-permute-start(bf16[8,8,56,128]{3,2,1,0:T(8,128)(2,1)S(1)} %get-tuple-element.15), channel_id=1, source_target_pairs={{0,1},{1,0},{2,3},{3,2},{4,5},{5,4},{6,7},{7,6},{8,9},{9,8},{10,11... | collective-permute-start | bytes 2752520 | tf_op jit(solution)/shard_map/ppermute | solution.py:332
  82.4 1.9 %collective-permute-done.3 = bf16[8,8,56,128]{3,2,1,0:T(8,128)(2,1)S(1)} collective-permute-done((bf16[8,8,56,128]{3,2,1,0:T(8,128)(2,1)S(1)}, bf16[8,8,56,128]{3,2,1,0:T(8,128)(2,1)S(1)}, u32[]{:S(2)}, u32[]{:S(2)}) %collective-permute-start.3) | collective-permute-done | bytes 917536 | tf_op jit(solution)/shard_map/ppermute | solution.py:332
  84.3 1.2 add_convert_fusion
  85.4 10.1 %all-to-all-start.1 = ((bf16[64,56,128]{2,1,0:T(8,128)(2,1)}), bf16[64,56,128]{2,1,0:T(8,128)(2,1)S(1)}, u32[]{:S(2)}, u32[]{:S(2)}) async-start(bf16[64,56,128]{2,1,0:T(8,128)(2,1)} %bitcast.9), calls=%async_computation.1 | async-start | bytes 1835008 | tf_op jit(solution)/shard_map/all_to_all | solution.py:335
  96.0 24.5 %all-to-all-done.1 = bf16[64,56,128]{2,1,0:T(8,128)(2,1)S(1)} async-done(((bf16[64,56,128]{2,1,0:T(8,128)(2,1)}), bf16[64,56,128]{2,1,0:T(8,128)(2,1)S(1)}, u32[]{:S(2)}, u32[]{:S(2)}) %all-to-all-start.1) | async-done | bytes 917536 | tf_op jit(solution)/shard_map/all_to_all | solution.py:335
  121.0 0.1 broadcast_in_dim.46
  121.1 0.4 convolution_convert_fusion
  121.7 0.4 convolution_convert_fusion.1
  122.2 0.1 broadcast_in_dim.42
  122.3 0.4 convolution_convert_fusion.2
  123.0 0.7 copy.46
  123.6 6.1 %all-to-all-start.2 = ((bf16[32,16,128]{2,1,0:T(8,128)(2,1)}), bf16[32,16,128]{2,1,0:T(8,128)(2,1)S(1)}, u32[]{:S(2)}, u32[]{:S(2)}) async-start(bf16[32,16,128]{2,1,0:T(8,128)(2,1)} %copy.46), calls=%async_computation.2 | async-start | bytes 262144 | tf_op jit(solution)/shard_map/all_to_all | solution.py:367
  129.9 9.3 %all-to-all-done.2 = bf16[32,16,128]{2,1,0:T(8,128)(2,1)S(1)} async-done(((bf16[32,16,128]{2,1,0:T(8,128)(2,1)}), bf16[32,16,128]{2,1,0:T(8,128)(2,1)S(1)}, u32[]{:S(2)}, u32[]{:S(2)}) %all-to-all-start.2) | async-done | bytes 131104 | tf_op jit(solution)/shard_map/all_to_all | solution.py:367
  139.9 1.1 fusion.1
  141.1 1.5 %fusion.5 = f32[1,4,3072]{2,1,0:T(4,128)} fusion(f32[4,3072]{1,0:T(4,128)S(1)} %get-tuple-element.35, f32[4]{0:T(128)S(1)} %broadcast_multiply_fusion, f32[4]{0:T(128)S(1)} %get-tuple-element.34, f32[4]{0:T(128)S(1)} %get-tuple-element.33, bf16[128,3072]{1,0:T(8,128)(2,1)} %refs_1_.1, s32[]{:T(128)S(6)} %select_n.89, bf16[128,3072]{1,0:T(8,128)(2,1)} %refs_0_.1), kind=kLoop, calls=%fused_computation.28 | loop fusion | flops 86016 | bytes 147508 | tf_op jit(solution)/shard_map/broadcast_in_dim | solution.py:390
  (58 shorter events, 2.2 us)
Async XLA Ops:
  5.5 53.4 %all-to-all-start = ((bf16[8,16,6528]{2,1,0:T(8,128)(2,1)}), bf16[8,16,6528]{2,1,0:T(8,128)(2,1)S(1)}, u32[]{:S(2)}, u32[]{:S(2)}) async-start(bf16[8,16,6528]{2,1,0:T(8,128)(2,1)} %get-tuple-element.12), calls=%async_computation | async-start | bytes 3342336 | tf_op jit(solution)/shard_map/all_to_all | solution.py:326
  16.4 65.8 %copy-start.4 = (s32[128,4]{0,1:T(4,128)S(1)}, s32[128,4]{0,1:T(4,128)}, u32[]{:S(2)}) copy-start(s32[128,4]{0,1:T(4,128)} %param.12) | copy-start | bytes 6148
  16.4 66.0 %copy-start.6 = (s32[8,128]{1,0:T(8,128)S(1)}, s32[8,128]{1,0:T(8,128)}, u32[]{:S(2)}) copy-start(s32[8,128]{1,0:T(8,128)} %get-tuple-element.11) | copy-start | bytes 12292
  16.4 44.9 %collective-permute-start.1 = (bf16[3,168,3072]{2,1,0:T(8,128)(2,1)}, bf16[3,168,3072]{2,1,0:T(8,128)(2,1)}, u32[]{:S(2)}, u32[]{:S(2)}) collective-permute-start(bf16[3,168,3072]{2,1,0:T(8,128)(2,1)} %get-tuple-element.13.refs_0_), channel_id=1, source_target_pairs={{1,48},{16,1},{33,16},{48,33},{65,112},{80,65},{97,80},{112,97},{1... | collective-permute-start | bytes 9289736 | tf_op jit(solution)/shard_map/ppermute | solution.py:315
  21.8 39.6 %collective-permute-start.2 = (bf16[3,168,3072]{2,1,0:T(8,128)(2,1)}, bf16[3,168,3072]{2,1,0:T(8,128)(2,1)}, u32[]{:S(2)}, u32[]{:S(2)}) collective-permute-start(bf16[3,168,3072]{2,1,0:T(8,128)(2,1)} %get-tuple-element.13.refs_0_), channel_id=1, source_target_pairs={{1,16},{0,64},{16,33},{17,81},{33,48},{32,96},{48,1},{49,113},{65,... | collective-permute-start | bytes 9289736 | tf_op jit(solution)/shard_map/ppermute | solution.py:316
  58.9 5.6 %copy-start = (bf16[8,16,6528]{2,1,0:T(8,128)(2,1)}, bf16[8,16,6528]{2,1,0:T(8,128)(2,1)S(1)}, u32[]{:S(2)}) copy-start(bf16[8,16,6528]{2,1,0:T(8,128)(2,1)S(1)} %all-to-all-done.rows_hbm) | copy-start | bytes 5013508
  58.9 5.6 %collective-permute-start = (bf16[8,16,6528]{2,1,0:T(8,128)(2,1)S(1)}, bf16[8,16,6528]{2,1,0:T(8,128)(2,1)S(1)}, u32[]{:S(2)}, u32[]{:S(2)}) collective-permute-start(bf16[8,16,6528]{2,1,0:T(8,128)(2,1)S(1)} %all-to-all-done.rows_hbm), channel_id=1, source_target_pairs={{0,1},{1,0},{2,3},{3,2},{4,5},{5,4},{6,7},{7,6},{8,9},{9,8},{10,11... | collective-permute-start | bytes 5013512 | tf_op jit(solution)/shard_map/ppermute | solution.py:327
  64.5 1.2 copy-start.1
  79.9 4.4 %collective-permute-start.3 = (bf16[8,8,56,128]{3,2,1,0:T(8,128)(2,1)S(1)}, bf16[8,8,56,128]{3,2,1,0:T(8,128)(2,1)S(1)}, u32[]{:S(2)}, u32[]{:S(2)}) collective-permute-start(bf16[8,8,56,128]{3,2,1,0:T(8,128)(2,1)S(1)} %get-tuple-element.15), channel_id=1, source_target_pairs={{0,1},{1,0},{2,3},{3,2},{4,5},{5,4},{6,7},{7,6},{8,9},{9,8},{10,11... | collective-permute-start | bytes 2752520 | tf_op jit(solution)/shard_map/ppermute | solution.py:332
  85.4 35.0 %all-to-all-start.1 = ((bf16[64,56,128]{2,1,0:T(8,128)(2,1)}), bf16[64,56,128]{2,1,0:T(8,128)(2,1)S(1)}, u32[]{:S(2)}, u32[]{:S(2)}) async-start(bf16[64,56,128]{2,1,0:T(8,128)(2,1)} %bitcast.9), calls=%async_computation.1 | async-start | bytes 1835008 | tf_op jit(solution)/shard_map/all_to_all | solution.py:335
  122.2 7.6 %copy-start.5 = (f32[4,128]{1,0:T(4,128)S(1)}, f32[4,128]{1,0:T(4,128)}, u32[]{:S(2)}) copy-start(f32[4,128]{1,0:T(4,128)} %get-tuple-element.16) | copy-start | bytes 6148
  122.3 17.6 %copy-start.2 = (bf16[3072,16]{0,1:T(8,128)(2,1)S(1)}, bf16[3072,16]{0,1:T(8,128)(2,1)}, u32[]{:S(2)}) copy-start(bf16[3072,16]{0,1:T(8,128)(2,1)} %param.11) | copy-start | bytes 294916
  122.3 17.6 %copy-start.3 = (f32[3072]{0:T(1024)S(1)}, f32[3072]{0:T(1024)}, u32[]{:S(2)}) copy-start(f32[3072]{0:T(1024)} %param.10) | copy-start | bytes 36868
  123.6 15.5 %all-to-all-start.2 = ((bf16[32,16,128]{2,1,0:T(8,128)(2,1)}), bf16[32,16,128]{2,1,0:T(8,128)(2,1)S(1)}, u32[]{:S(2)}, u32[]{:S(2)}) async-start(bf16[32,16,128]{2,1,0:T(8,128)(2,1)} %copy.46), calls=%async_computation.2 | async-start | bytes 262144 | tf_op jit(solution)/shard_map/all_to_all | solution.py:367
